TPU v7x, 32 devices: a whole 2x2x4 slice. The times are simulated.
32 devices in a mesh: dp: 2 (over x), seq: 4 (over z), mp: 4 (over y, core).
Axes of the slice: x: 2, y: 2, z: 4, core: 2. Of those that a mesh axis runs over, the one named last changes fastest.
Arguments:
- shortening_input: bfloat16 [2, 8192, 2048], P('dp', ('seq', 'mp')), may hold values from -6 to 6
- coarse_grad: bfloat16 [2, 2048, 4096], P('dp', 'seq', 'mp'), may hold values from -6 to 6
- weight_copy: bfloat16 [2, 4096, 4096], P('dp', None, 'mp'), may hold values from -0.0625 to 0.0625
- master: float32 [2, 4096, 4096], P('dp', 'seq', 'mp'), may hold values from -3 to 3
- moment: float32 [2, 4096, 4096], P('dp', 'seq', 'mp'), may hold values from -3 to 3
- second: float32 [2, 4096, 4096], P('dp', 'seq', 'mp'), may hold values from 0.05 to 5
Outputs:
- act_grad: bfloat16 [2, 8192, 2048], P('dp', ('seq', 'mp'))
- new_master: float32 [2, 4096, 4096], P('dp', 'seq', 'mp')
- new_moment: float32 [2, 4096, 4096], P('dp', 'seq', 'mp')
- new_second: float32 [2, 4096, 4096], P('dp', 'seq', 'mp')
- new_weight: bfloat16 [2, 4096, 4096], P(None, 'seq', 'mp')
All inputs are finite; a program needn't handle non-finite values.
Results may differ from a plain program's by a relative error of at most 0.009.
Values may be sent and summed in bfloat16 or wider, within the bound.
No kernel may reach another device: no remote copies, remote signals or barrier semaphores. Data moves between devices by JAX's collectives and lax.ppermute only.
A program may use at most 128 MiB of HBM per device.

v0:
```python
import math

import jax
import jax.numpy as jnp
from jax import lax
from jax.sharding import PartitionSpec as P

SHORT = 4


first_beta = 0.9
second_beta = 0.95
first_fix = 1.0 - 0.9**10
second_fix = 1.0 - 0.95**10
adam_eps = 1e-08
learn_rate = 0.05
weight_decay = 0.1


def shifted(value, axis, steps):
    count = lax.axis_size(axis)
    initial, last = (max(0, -steps), min(count, count - steps))
    return lax.ppermute(value, axis, [(source, source + steps) for source in range(initial, last)])


def per_device(shortening_input, coarse_grad, weight_copy, master, moment, second):
    fine_rows = shortening_input[0]
    rows_dev = fine_rows.shape[0]
    features = fine_rows.shape[1]
    grad_cols = coarse_grad[0]
    coarse_rows = grad_cols.shape[0]
    wide_rows = SHORT * features
    whole_copy = lax.all_gather(weight_copy, "dp", axis=0, tiled=True)
    weights = whole_copy.reshape(wide_rows, whole_copy.shape[2])
    summed = (
        lax.psum_scatter(
            lax.dot_general(
                grad_cols, weights, (((1,), (1,)), ((), ())), preferred_element_type=jnp.float32
            ).astype(jnp.bfloat16),
            "mp",
            scatter_dimension=0,
            tiled=True,
        )
        .astype(jnp.float32)
        .reshape(rows_dev, features)
    )
    later_rows = shifted(summed[: SHORT - 1], ("seq", "mp"), -1)
    act_grad = jnp.concatenate([summed[SHORT - 1 :], later_rows], axis=0).astype(jnp.bfloat16)
    gathered = lax.all_gather(fine_rows, "mp", axis=0, tiled=True).reshape(coarse_rows, wide_rows)
    owned_rows = lax.psum_scatter(
        lax.dot_general(
            gathered, grad_cols, (((0,), (0,)), ((), ())), preferred_element_type=jnp.float32
        ).astype(jnp.bfloat16),
        ("dp", "seq"),
        scatter_dimension=0,
        tiled=True,
    ).astype(jnp.float32)
    grad_scale = 1.0 / math.sqrt(lax.axis_size("dp") * coarse_rows * lax.axis_size("seq"))
    gradient = (owned_rows * grad_scale).reshape(master.shape)
    new_moment = first_beta * moment + (1.0 - first_beta) * gradient
    new_second = second_beta * second + (1.0 - second_beta) * gradient * gradient
    step_ratio = new_moment / first_fix / (jnp.sqrt(new_second / second_fix) + adam_eps)
    new_master = master - learn_rate * (step_ratio + weight_decay * master)
    new_weight = lax.all_gather(new_master.astype(jnp.bfloat16), "dp", axis=0, tiled=True)
    return (act_grad[None], new_master, new_moment, new_second, new_weight)


def solution(mesh):
    return jax.shard_map(
        per_device,
        mesh=mesh,
        in_specs=(
            P("dp", ("seq", "mp"), None),
            P("dp", "seq", "mp"),
            P("dp", None, "mp"),
            P("dp", "seq", "mp"),
            P("dp", "seq", "mp"),
            P("dp", "seq", "mp"),
        ),
        out_specs=(
            P("dp", ("seq", "mp"), None),
            P("dp", "seq", "mp"),
            P("dp", "seq", "mp"),
            P("dp", "seq", "mp"),
            P(None, "seq", "mp"),
        ),
        check_vma=False,
    )
```

profile of v0, /device:TPU:0, one launch (start us, length us, event | category | flops | bytes accessed | tf_op | source)
XLA Modules:
  0.0 700.2 jit_solution(4665273329132707850)
XLA Ops:
  7.2 0.0 copy-start
  7.2 0.0 all-gather.9.cloned.1.call-start
  7.2 0.7 all-gather.9.cloned.1.call-update
  7.9 0.0 all-gather.5.cloned.1.call-start
  8.0 0.7 all-gather.5.cloned.1.call-update
  8.7 0.0 reduce-scatter.5.cloned.1.call-start
  8.7 61.9 %all-gather.9.cloned.1.call-done = bf16[1,2048,2048]{2,1,0:T(8,128)(2,1)} async-done(((bf16[1,512,2048]{2,1,0:T(8,128)(2,1)}), bf16[1,2048,2048]{2,1,0:T(8,128)(2,1)}) %all-gather.9.cloned.1.call-update) | async-done | bytes 8388624 | tf_op jit(solution)/shard_map/all_gather | solution.py:49
  70.6 15.3 %reshape.57 = bf16[512,8192]{1,0:T(8,128)(2,1)} reshape(bf16[1,2048,2048]{2,1,0:T(8,128)(2,1)} %all-gather.9.cloned.1.call-done) | data formatting | bytes 16777216 | tf_op jit(solution)/shard_map/reshape | solution.py:49
  85.9 0.0 copy-done
  85.9 17.1 %convolution_convert_fusion = bf16[8192,1024]{1,0:T(8,128)(2,1)} fusion(bf16[512,8192]{1,0:T(8,128)(2,1)} %reshape.57, bf16[1,512,1024]{2,1,0:T(8,128)(2,1)S(1)} %copy-done), kind=kOutput, calls=%fused_computation | convolution fusion | flops 8598323200 | bytes 26214400 | tf_op jit(solution)/shard_map/dot_general | solution.py:51
  102.9 0.0 reduce-scatter.5.cloned.1.call-update
  103.0 0.0 reduce-scatter.3.cloned.1.call-start
  103.0 168.0 %all-gather.5.cloned.1.call-done = bf16[2,4096,1024]{2,1,0:T(8,128)(2,1)} async-done(((bf16[1,4096,1024]{2,1,0:T(8,128)(2,1)}), bf16[2,4096,1024]{2,1,0:T(8,128)(2,1)}) %all-gather.5.cloned.1.call-update) | async-done | bytes 16777232 | tf_op jit(solution)/shard_map/all_gather | solution.py:33
  271.0 29.6 %convolution_convert_fusion.1 = bf16[512,8192]{1,0:T(8,128)(2,1)} fusion(bf16[8192,1024]{1,0:T(8,128)(2,1)} %bitcast.24, bf16[1,512,1024]{2,1,0:T(8,128)(2,1)S(1)} %copy-done), kind=kOutput, calls=%fused_computation.1 | convolution fusion | flops 8594128896 | bytes 26214400 | tf_op jit(solution)/shard_map/dot_general | solution.py:37
  300.7 0.0 reduce-scatter.3.cloned.1.call-update
  300.7 0.0 all-gather.7.cloned.1.call-start
  300.7 256.0 %reduce-scatter.5.cloned.1.call-done = bf16[1024,1024]{1,0:T(8,128)(2,1)} async-done(((bf16[8192,1024]{1,0:T(8,128)(2,1)}), bf16[1024,1024]{1,0:T(8,128)(2,1)}) %reduce-scatter.5.cloned.1.call-update) | async-done | bytes 2097168 | tf_op jit(solution)/shard_map/reduce_scatter | solution.py:50
  556.8 10.9 %fusion.7 = (bf16[1,1024,1024]{2,1,0:T(8,128)(2,1)}, f32[1,1024,1024]{2,1,0:T(8,128)}, f32[1,1024,1024]{2,1,0:T(8,128)}, f32[1,1024,1024]{2,1,0:T(8,128)}) fusion(f32[1,1024,1024]{2,1,0:T(8,128)} %param.9, bf16[1024,1024]{1,0:T(8,128)(2,1)} %reduce-scatter.5.cloned.1.call-done, f32[1,1024,1024]{2,1,0:T(8,128)} %param.10, f32[1,1024,1024]{2,1,0:T(8,128)} %param.11), kind=kLoop, calls=%fused_computation.17 | loop fusion | flops 18874368 | bytes 29360128 | tf_op jit(solution)/shard_map/convert_element_type | solution.py:64
  567.6 0.0 all-gather.7.cloned.1.call-update
  567.7 62.6 %reduce-scatter.3.cloned.1.call-done = bf16[128,8192]{1,0:T(8,128)(2,1)} async-done(((bf16[512,8192]{1,0:T(8,128)(2,1)}), bf16[128,8192]{1,0:T(8,128)(2,1)}) %reduce-scatter.3.cloned.1.call-update) | async-done | bytes 2097168 | tf_op jit(solution)/shard_map/reduce_scatter | solution.py:36
  630.2 3.4 reshape.56
  633.6 1.3 collective-permute-start
  634.9 0.5 slice_bitcast_fusion
  635.4 1.3 collective-permute-done
  636.7 1.5 pad_maximum_fusion
  638.2 50.8 %all-gather.7.cloned.1.call-done = bf16[2,1024,1024]{2,1,0:T(8,128)(2,1)} async-done(((bf16[1,1024,1024]{2,1,0:T(8,128)(2,1)}), bf16[2,1024,1024]{2,1,0:T(8,128)(2,1)}) %all-gather.7.cloned.1.call-update) | async-done | bytes 4194320 | tf_op jit(solution)/shard_map/all_gather | solution.py:64
  689.0 0.0 copy-start.1
  689.0 4.7 copy.12
  693.7 0.0 copy-done.1
  (1 shorter events, 0.0 us)
Async XLA Ops:
  7.2 78.7 %copy-start = (bf16[1,512,1024]{2,1,0:T(8,128)(2,1)S(1)}, bf16[1,512,1024]{2,1,0:T(8,128)(2,1)}, u32[]{:S(2)}) copy-start(bf16[1,512,1024]{2,1,0:T(8,128)(2,1)} %param.7) | copy-start | bytes 3145732
  7.2 63.4 %all-gather.9.cloned.1.call-start = ((), (), s32[]{:S(2)}) async-start(), calls=%async_computation.6 | async-start | bytes 10485760 | tf_op jit(solution)/shard_map/all_gather | solution.py:49
  7.9 263.1 %all-gather.5.cloned.1.call-start = ((), (), s32[]{:S(2)}) async-start(), calls=%async_computation.2 | async-start | bytes 25165824 | tf_op jit(solution)/shard_map/all_gather | solution.py:33
  8.7 548.1 %reduce-scatter.5.cloned.1.call-start = ((), (), s32[]{:S(2)}) async-start(), calls=%async_computation.4 | async-start | bytes 18874368 | tf_op jit(solution)/shard_map/reduce_scatter | solution.py:50
  103.0 527.3 %reduce-scatter.3.cloned.1.call-start = ((), (), s32[]{:S(2)}) async-start(), calls=%async_computation.3 | async-start | bytes 10485760 | tf_op jit(solution)/shard_map/reduce_scatter | solution.py:36
  300.7 388.3 %all-gather.7.cloned.1.call-start = ((), (), s32[]{:S(2)}) async-start(), calls=%async_computation.5 | async-start | bytes 6291456 | tf_op jit(solution)/shard_map/all_gather | solution.py:64
  633.6 3.1 collective-permute-start
  689.0 4.7 copy-start.1
Sparse Core Ops, SparseCore 0:
  9.6 60.9 all-gather.8
  72.1 198.8 all-gather.4
  274.8 281.9 reduce-scatter.4
  559.4 70.8 reduce-scatter.2
  632.2 56.7 all-gather.6
where the time goes:
time: 701 us; the launch traced here: 700 us
  waiting for transfers between devices  602 us (86%)
  matrix products  46.7 us (7%)
  local copies, waits for them, and re-layouts  23.9 us (3%)
  between operations  13.8 us (2%)
  other arithmetic  12.3 us (2%)
    reduce_scatter x1, waiting for transfers between devices, per_device(): lax.psum_scatter(lax.dot_general(gathered, grad_cols, (((0,), (0,)), ((),...  256 us
    all_gather x1, waiting for transfers between devices, per_device(): whole_copy = lax.all_gather(weight_copy, 'dp', axis=0, tiled=True)  168 us
    reduce_scatter x1, waiting for transfers between devices, per_device(): lax.psum_scatter(lax.dot_general(grad_cols, weights, (((1,), (1,)), ((),...  62.6 us
    all_gather x1, waiting for transfers between devices, per_device(): lax.all_gather(fine_rows, 'mp', axis=0, tiled=True)  61.9 us
    all_gather x1, waiting for transfers between devices, per_device(): lax.all_gather(new_master.astype(jnp.bfloat16), 'dp', axis=0, tiled=True)  50.8 us
    dot_general x1, matrix products, per_device(): lax.dot_general(grad_cols, weights, (((1,), (1,)), ((), ())), preferred_e...  29.6 us
    dot_general x1, matrix products, per_device(): lax.dot_general(gathered, grad_cols, (((0,), (0,)), ((), ())), preferred_...  17.1 us
    reshape x1, local copies, waits for them, and re-layouts, per_device(): lax.all_gather(fine_rows, 'mp', axis=0, tiled=True)  15.3 us
  transfers between devices with their start and end apart: 6, of which 6 were waited for; matrix products, arithmetic and copies ran while one was open for 11% of the time, Pallas kernels for 0%

commit v1 on v0

v1 whole, which is shorter than its diff:
```python
import math

import jax
import jax.numpy as jnp
from jax import lax
from jax.sharding import PartitionSpec as P

SHORT = 4
first_beta = 0.9
second_beta = 0.95
first_fix = 1.0 - 0.9**10
second_fix = 1.0 - 0.95**10
adam_eps = 1e-08
learn_rate = 0.05
weight_decay = 0.1
HALVES = 2
PIECES = 4

bf16, f32 = jnp.bfloat16, jnp.float32


def swap(value, axis, step):
    count = lax.axis_size(axis)
    return lax.ppermute(value, axis, [(i, i ^ step) for i in range(count)])


def per_device(shortening_input, coarse_grad, weight_copy, master, moment, second):
    fine = shortening_input[0]
    grad = coarse_grad[0]
    weights = weight_copy[0]
    master, moment, second = master[0], moment[0], second[0]
    rows_dev, features = fine.shape
    coarse_rows, width = grad.shape
    half_rows = weights.shape[0]
    own_rows = rows_dev // SHORT
    block = master.shape[0]
    n_seq, n_mp = lax.axis_size("seq"), lax.axis_size("mp")
    far = n_seq // 2
    x, z, m = lax.axis_index("dp"), lax.axis_index("seq"), lax.axis_index("mp")
    h, l = z // 2, z % 2

    t = lax.broadcasted_iota(jnp.int32, (rows_dev, rows_dev), 0)
    u = lax.broadcasted_iota(jnp.int32, (rows_dev, rows_dev), 1)
    spread = (u == SHORT * (t % own_rows) + t // own_rows).astype(bf16)
    planes = jnp.dot(spread, fine, preferred_element_type=f32).astype(bf16)

    def part(dp, hi, lo):
        offset = dp * half_rows + (2 * hi + lo) * block
        return lax.dynamic_slice(
            planes, (offset // features * own_rows, offset % features), (own_rows, block)
        )

    def gather_inputs(hi):
        blocks = [
            part(x, hi, l),
            swap(part(1 - x, hi, l), "dp", 1),
            swap(part(x, hi, 1 - l), "seq", 1),
            lax.ppermute(
                part(1 - x, hi, 1 - l),
                ("dp", "seq"),
                [(i, i ^ n_seq ^ 1) for i in range(2 * n_seq)],
            ),
        ]
        own = jnp.concatenate(blocks, axis=0)
        across = swap(own, "mp", 2)
        beside = swap(own, "mp", 1)
        both = swap(across, "mp", 1)
        return jnp.concatenate([both, beside, across, own], axis=0)

    order = (3, 1, 2, 0)
    grads = jnp.concatenate(
        [lax.dynamic_slice_in_dim(grad, (m ^ j) * own_rows, own_rows, 0) for j in order], axis=0
    )
    piece = width // HALVES

    def gather_grads(k):
        mine = grads[:, k * piece : (k + 1) * piece]
        other = swap(mine, "dp", 1)
        return [mine, other, swap(mine, "seq", 1), swap(other, "seq", 1)]

    def tokens(parts):
        return jnp.stack([v.reshape(n_mp, own_rows, piece) for v in parts], axis=1).reshape(
            -1, piece
        )

    def against(a, b):
        return lax.dot_general(a, b, (((0,), (0,)), ((), ())), preferred_element_type=f32)

    def act_partial(rows):
        return lax.dot_general(
            rows, weights, (((1,), (1,)), ((), ())), preferred_element_type=f32
        ).astype(bf16)

    def act_sum(rows):
        partial = act_partial(rows)
        cut = 2 * own_rows
        pair = partial[cut:].astype(f32) + swap(partial[:cut], "mp", 1).astype(f32)
        send = pair[:own_rows].astype(bf16)
        return pair[own_rows:] + swap(send, "mp", 2).astype(f32)

    x_far = {}
    for k in range(1, far):
        x_far[k] = gather_inputs((h + k) % far)
    g = [gather_grads(0)]
    x_far[0] = gather_inputs(h)
    g += [gather_grads(k) for k in range(1, HALVES)]
    act_own = act_sum(grads).astype(bf16)
    other_grads = jnp.concatenate([v[1] for v in g], axis=1)
    act_other = swap(act_sum(other_grads).astype(bf16), "dp", 1)

    mine = act_own.reshape(own_rows, 2, features)
    theirs = act_other.reshape(own_rows, 2, features)
    stack = jnp.concatenate([mine[:, 0], mine[:, 1], theirs[:, 0], theirs[:, 1]], axis=0)
    first = jnp.stack([mine[0], theirs[0]])
    first = lax.dynamic_index_in_dim(first, x, 0, False), lax.dynamic_index_in_dim(first, 1 - x, 0, False)
    first = jnp.concatenate(first, axis=0)[: SHORT - 1]
    count = n_seq * n_mp
    later = lax.ppermute(first, ("seq", "mp"), [(i, i - 1) for i in range(1, count)])
    stack = jnp.concatenate([stack, jnp.pad(later, ((0, 8 - (SHORT - 1)), (0, 0)))], axis=0)
    t = lax.broadcasted_iota(jnp.int32, (rows_dev, rows_dev + 8), 0) + SHORT - 1
    u = lax.broadcasted_iota(jnp.int32, (rows_dev, rows_dev + 8), 1)
    p, r = t % SHORT, t // SHORT
    source = ((p + 2 * x) % SHORT) * own_rows + r
    source = jnp.where(t < rows_dev, source, t)
    gather = (u == source).astype(bf16)
    act_grad = jnp.dot(gather, stack, preferred_element_type=f32).astype(bf16)

    scale = 1.0 / math.sqrt(lax.axis_size("dp") * coarse_rows * n_seq)
    g_all = [tokens(v) for v in g]
    cols = width // PIECES
    per = PIECES // HALVES
    outs = []
    for i in range(PIECES):
        rhs = g_all[i // per][:, (i % per) * cols : (i % per + 1) * cols]
        total = None
        for k in range(1, far):
            sent = against(x_far[k], rhs).astype(bf16)
            came = lax.ppermute(
                sent, "seq", [(s, (s + 2 * k) % n_seq) for s in range(n_seq)]
            ).astype(f32)
            total = came if total is None else total + came
        own = against(x_far[0], rhs)
        gradient = (own if total is None else own + total) * scale
        at = slice(i * cols, (i + 1) * cols)
        new_moment = first_beta * moment[:, at] + (1.0 - first_beta) * gradient
        new_second = second_beta * second[:, at] + (1.0 - second_beta) * gradient * gradient
        ratio = new_moment / first_fix / (jnp.sqrt(new_second / second_fix) + adam_eps)
        new_master = master[:, at] - learn_rate * (ratio + weight_decay * master[:, at])
        low = new_master.astype(bf16)
        other = swap(low, "dp", 1)
        outs.append((new_master, new_moment, new_second, low, other))
    new_master, new_moment, new_second, low, other = [
        jnp.concatenate(v, axis=1) for v in zip(*outs)
    ]
    new_weight = jnp.stack([jnp.where(x == 0, low, other), jnp.where(x == 0, other, low)])
    return (act_grad[None], new_master[None], new_moment[None], new_second[None], new_weight)


def solution(mesh):
    return jax.shard_map(
        per_device,
        mesh=mesh,
        in_specs=(
            P("dp", ("seq", "mp"), None),
            P("dp", "seq", "mp"),
            P("dp", None, "mp"),
            P("dp", "seq", "mp"),
            P("dp", "seq", "mp"),
            P("dp", "seq", "mp"),
        ),
        out_specs=(
            P("dp", ("seq", "mp"), None),
            P("dp", "seq", "mp"),
            P("dp", "seq", "mp"),
            P("dp", "seq", "mp"),
            P(None, "seq", "mp"),
        ),
        check_vma=False,
    )
```

time: 701 us -> 308 us (0.44)
  waiting for transfers between devices: 602 us -> 149 us
  starting transfers between devices: 1.49 us -> 32.8 us
  local copies, waits for them, and re-layouts: 23.9 us -> 54 us
  other arithmetic: 12.3 us -> 27.7 us
  between operations: 13.8 us -> 1.48 us
    reduce_scatter x2 -> x0, waiting for transfers between devices: 319 us -> none  [the longest x1 256 us: per_device(): lax.psum_scatter(lax.dot_general(gathered, grad_cols, (((0,), (0,)), ((),...]
    all_gather x3 -> x0, waiting for transfers between devices: 281 us -> none  [the longest x1 168 us: per_device(): whole_copy = lax.all_gather(weight_copy, 'dp', axis=0, tiled=True)]
    ppermute x1 -> x32, waiting for transfers between devices: 1.27 us -> 149 us  [the longest x4 78.6 us: per_device(): lax.ppermute(sent, 'seq', [(s, (s + 2 * k) % n_seq) for s in range(n_seq)])]
    unnamed x5 -> x70, local copies, waits for them, and re-layouts: 4.74 us -> 41.9 us
    ppermute x1 -> x32, starting transfers between devices: 1.29 us -> 32.8 us  [the longest x25 21 us: swap(): return lax.ppermute(value, axis, [(i, i ^ step) for i in range(count)])]
    reshape x2, local copies, waits for them, and re-layouts: 18.6 us -> 1.6 us  [the longest x1 0.8 us: per_device(): theirs = act_other.reshape(own_rows, 2, features)]
    broadcast_in_dim x0 -> x3, other arithmetic: none -> 11.9 us  [the longest x1 4.77 us: per_device(): new_moment[None]]
    dot_general x2 -> x12, matrix products: 46.7 us -> 40.9 us  [the longest x8 20.7 us: against(): lax.dot_general(a, b, (((0,), (0,)), ((), ())), preferred_element_type=f32)]
  transfers between devices with their start and end apart: 6 -> 32, of which waited for: 6 -> 13; matrix products, arithmetic and copies ran while one was open for 11% -> 38% of each run, Pallas kernels for 0% -> 0%
where the time goes in v1:
time: 308 us; the launch traced here: 306 us
  waiting for transfers between devices  149 us (48%)
  local copies, waits for them, and re-layouts  54 us (18%)
  matrix products  40.9 us (13%)
  starting transfers between devices  32.8 us (11%)
  other arithmetic  27.7 us (9%)
    ppermute x4, waiting for transfers between devices, per_device(): lax.ppermute(sent, 'seq', [(s, (s + 2 * k) % n_seq) for s in range(n_seq)])  78.6 us
    ppermute x25, waiting for transfers between devices, swap(): return lax.ppermute(value, axis, [(i, i ^ step) for i in range(count)])  65.7 us
    unnamed x70, local copies, waits for them, and re-layouts  41.9 us
    ppermute x25, starting transfers between devices, swap(): return lax.ppermute(value, axis, [(i, i ^ step) for i in range(count)])  21 us
    dot_general x8, matrix products, against(): lax.dot_general(a, b, (((0,), (0,)), ((), ())), preferred_element_type=f32)  20.7 us
    dot_general x2, matrix products, act_partial(): lax.dot_general(rows, weights, (((1,), (1,)), ((), ())), preferred_elemen...  14.4 us
  transfers between devices with their start and end apart: 32, of which 13 were waited for; matrix products, arithmetic and copies ran while one was open for 38% of the time, Pallas kernels for 0%

profile of v1, /device:TPU:0, one launch (start us, length us, event | category | flops | bytes accessed | tf_op | source)
XLA Modules:
  0.0 306.2 jit_solution(12036250340592788178)
XLA Ops:
  0.7 1.4 dynamic-slice_bitcast_fusion.3
  3.0 2.9 collective-permute-start.2
  6.1 1.8 convolution_convert_fusion
  7.9 2.2 fusion.93
  10.2 1.5 collective-permute-start.18
  11.8 2.8 collective-permute-start.10
  15.1 6.1 %fusion.4 = bf16[512,4096]{1,0:T(8,128)(2,1)} fusion(bf16[1,4096,1024]{2,1,0:T(8,128)(2,1)S(1)} %copy-done.22, bf16[128,1024]{1,0:T(8,128)(2,1)S(1)} %copy-done.9, bf16[128,1024]{1,0:T(8,128)(2,1)S(1)} %copy-done.11, bf16[128,1024]{1,0:T(8,128)(2,1)S(1)} %copy-done.7, bf16[128,1024]{1,0:T(8,128)(2,1)S(1)} %get-tuple-element.59), kind=kOutput, calls=%fused_computation.4 | convolution fusion | flops 4301258752 | bytes 13631488 | tf_op jit(solution)/shard_map/dot_general | solution.py:90
  21.5 3.1 %collective-permute-done.17 = bf16[128,1024]{1,0:T(8,128)(2,1)S(1)} collective-permute-done((bf16[128,1024]{1,0:T(8,128)(2,1)S(1)}, bf16[128,1024]{1,0:T(8,128)(2,1)S(1)}, u32[]{:S(2)}, u32[]{:S(2)}) %collective-permute-start.17) | collective-permute-done | bytes 262176 | tf_op jit(solution)/shard_map/ppermute | solution.py:24
  24.6 1.9 collective-permute-start.14
  26.6 5.0 %collective-permute-done.10 = bf16[128,1024]{1,0:T(8,128)(2,1)S(1)} collective-permute-done((bf16[128,1024]{1,0:T(8,128)(2,1)S(1)}, bf16[128,1024]{1,0:T(8,128)(2,1)S(1)}, u32[]{:S(2)}, u32[]{:S(2)}) %collective-permute-start.10) | collective-permute-done | bytes 262176 | tf_op jit(solution)/shard_map/ppermute | solution.py:58
  31.8 1.9 collective-permute-start.15
  33.7 2.2 collective-permute-done.9
  35.9 1.9 collective-permute-start.16
  37.8 3.1 %slice.147 = bf16[256,4096]{1,0:T(8,128)(2,1)} slice(bf16[512,4096]{1,0:T(8,128)(2,1)} %fusion.4), slice={[0:256], [0:4096]} | slice | bytes 4194304 | tf_op jit(solution)/shard_map/slice | solution.py:97
  40.9 5.3 %copy.29 = f32[1,1024,1024]{1,2,0:T(8,128)} copy(f32[1,1024,1024]{2,1,0:T(8,128)} %param.9) | data formatting | bytes 8388608 | tf_op args[3]
  46.2 5.3 %copy.30 = f32[1,1024,1024]{1,2,0:T(8,128)} copy(f32[1,1024,1024]{2,1,0:T(8,128)} %param.10) | data formatting | bytes 8388608 | tf_op args[4]
  51.6 5.3 %copy.32 = f32[1,1024,1024]{1,2,0:T(8,128)} copy(f32[1,1024,1024]{2,1,0:T(8,128)} %param.11) | data formatting | bytes 8388608 | tf_op args[5]
  57.0 1.6 collective-permute-start.24
  58.7 1.1 pad_maximum_fusion.7
  59.8 1.5 collective-permute-start.19
  62.3 8.3 %fusion.7 = bf16[512,4096]{1,0:T(8,128)(2,1)S(1)} fusion(bf16[1,4096,1024]{2,1,0:T(8,128)(2,1)} %param.8, bf16[512,512]{1,0:T(8,128)(2,1)} %collective-permute-done.3, bf16[512,512]{1,0:T(8,128)(2,1)} %collective-permute-done.2), kind=kOutput, calls=%fused_computation.5 | convolution fusion | flops 4299161600 | bytes 13631488 | tf_op jit(solution)/shard_map/dot_general | solution.py:90
  70.7 1.8 pad_maximum_fusion.1
  73.3 9.4 %collective-permute-done.25 = bf16[512,512]{1,0:T(8,128)(2,1)S(1)} collective-permute-done((bf16[512,512]{1,0:T(8,128)(2,1)}, bf16[512,512]{1,0:T(8,128)(2,1)S(1)}, u32[]{:S(2)}, u32[]{:S(2)}) %collective-permute-start.25) | collective-permute-done | bytes 524320 | tf_op jit(solution)/shard_map/ppermute | solution.py:24
  82.7 1.5 pad_maximum_fusion.2
  84.1 1.9 collective-permute-done.19
  86.0 21.7 %collective-permute-done.11 = bf16[512,1024]{1,0:T(8,128)(2,1)S(1)} collective-permute-done((bf16[512,1024]{1,0:T(8,128)(2,1)S(1)}, bf16[512,1024]{1,0:T(8,128)(2,1)S(1)}, u32[]{:S(2)}, u32[]{:S(2)}) %collective-permute-start.11) | collective-permute-done | bytes 1048608 | tf_op jit(solution)/shard_map/ppermute | solution.py:24
  109.1 1.3 collective-permute-done.20
  110.4 1.5 collective-permute-start.1
  112.3 1.3 convolution_convert_fusion.5
  113.6 2.6 collective-permute-start.22
  116.3 1.3 convolution_convert_fusion.4
  118.1 1.3 convolution_convert_fusion.3
  119.4 2.6 collective-permute-start.26
  122.3 1.3 convolution_convert_fusion.2
  124.0 0.9 convert_add_fusion
  125.1 59.4 %collective-permute-done.23 = bf16[1024,256]{0,1:T(8,128)(2,1)S(1)} collective-permute-done((bf16[1024,256]{0,1:T(8,128)(2,1)S(1)}, bf16[1024,256]{0,1:T(8,128)(2,1)S(1)}, u32[]{:S(2)}, u32[]{:S(2)}) %collective-permute-start.23) | collective-permute-done | bytes 524320 | tf_op jit(solution)/shard_map/ppermute | solution.py:138
  184.9 1.3 convolution_add_fusion.2
  186.3 9.4 %collective-permute-done.26 = bf16[1024,256]{0,1:T(8,128)(2,1)S(1)} collective-permute-done((bf16[1024,256]{0,1:T(8,128)(2,1)S(1)}, bf16[1024,256]{0,1:T(8,128)(2,1)S(1)}, u32[]{:S(2)}, u32[]{:S(2)}) %collective-permute-start.26) | collective-permute-done | bytes 524320 | tf_op jit(solution)/shard_map/ppermute | solution.py:138
  195.7 1.3 convolution_add_fusion.1
  197.0 9.8 %collective-permute-done.27 = bf16[1024,256]{0,1:T(8,128)(2,1)S(1)} collective-permute-done((bf16[1024,256]{0,1:T(8,128)(2,1)S(1)}, bf16[1024,256]{0,1:T(8,128)(2,1)S(1)}, u32[]{:S(2)}, u32[]{:S(2)}) %collective-permute-start.27) | collective-permute-done | bytes 524320 | tf_op jit(solution)/shard_map/ppermute | solution.py:138
  206.8 1.3 convolution_add_fusion
  208.1 11.6 %fusion.81 = (bf16[1024,256]{0,1:T(8,128)(2,1)}, f32[1024,256]{0,1:T(8,128)S(1)}, f32[1024,256]{0,1:T(8,128)}, f32[1024,256]{0,1:T(8,128)}, bf16[1024,256]{0,1:T...) fusion(f32[1024,1024]{0,1:T(8,128)} %bitcast.78, ...), kind=kOutput, calls=%fused_computation.164 | convolution fusion | flops 1092091904 | bytes 36175872 | tf_op jit(solution)/shard_map/dot_general | solution.py:87
  219.7 2.3 maximum_bitcast_fusion
  222.0 5.3 %copy.36 = f32[1,1024,1024]{2,1,0:T(8,128)} copy(f32[1,1024,1024]{1,2,0:T(8,128)} %maximum_bitcast_fusion) | data formatting | bytes 8388608
  227.9 1.5 collective-permute-start.31
  229.9 4.8 %maximum_bitcast_fusion.1 = f32[1,1024,1024]{1,2,0:T(8,128)} fusion(f32[1024,256]{0,1:T(8,128)} %get-tuple-element.34, f32[1024,256]{0,1:T(8,128)} %get-tuple-element.38, f32[1024,256]{0,1:T(8,128)} %get-tuple-element.42, f32[1024,256]{0,1:T(8,128)} %get-tuple-element.17), kind=kLoop, calls=%fused_computation.7 | loop fusion | flops 3145728 | bytes 8388608 | tf_op jit(solution)/shard_map/broadcast_in_dim | solution.py:156
  234.7 5.3 %copy.37 = f32[1,1024,1024]{2,1,0:T(8,128)} copy(f32[1,1024,1024]{1,2,0:T(8,128)} %maximum_bitcast_fusion.1) | data formatting | bytes 8388608
  240.0 4.8 %maximum_bitcast_fusion.2 = f32[1,1024,1024]{1,2,0:T(8,128)} fusion(f32[1024,256]{0,1:T(8,128)} %get-tuple-element.33, f32[1024,256]{0,1:T(8,128)} %get-tuple-element.37, f32[1024,256]{0,1:T(8,128)} %get-tuple-element.41, f32[1024,256]{0,1:T(8,128)} %get-tuple-element.18), kind=kLoop, calls=%fused_computation.8 | loop fusion | flops 3145728 | bytes 8388608 | tf_op jit(solution)/shard_map/broadcast_in_dim | solution.py:156
  244.8 5.3 %copy.38 = f32[1,1024,1024]{2,1,0:T(8,128)} copy(f32[1,1024,1024]{1,2,0:T(8,128)} %maximum_bitcast_fusion.2) | data formatting | bytes 8388608
  250.2 1.5 collective-permute-start.29
  251.7 2.1 fusion.12
  253.8 0.8 reshape.242
  254.6 1.5 fusion.96
  256.8 2.5 fusion.11
  260.1 4.8 %collective-permute-done.30 = bf16[1024,256]{0,1:T(8,128)(2,1)} collective-permute-done((bf16[1024,256]{0,1:T(8,128)(2,1)}, bf16[1024,256]{0,1:T(8,128)(2,1)}, u32[]{:S(2)}, u32[]{:S(2)}) %collective-permute-start.30) | collective-permute-done | bytes 524320 | tf_op jit(solution)/shard_map/ppermute | solution.py:24
  265.0 11.2 %collective-permute-done.29 = bf16[1024,256]{0,1:T(8,128)(2,1)} collective-permute-done((bf16[1024,256]{0,1:T(8,128)(2,1)}, bf16[1024,256]{0,1:T(8,128)(2,1)}, u32[]{:S(2)}, u32[]{:S(2)}) %collective-permute-start.29) | collective-permute-done | bytes 524320 | tf_op jit(solution)/shard_map/ppermute | solution.py:24
  276.2 2.8 broadcast_select_fusion.1
  279.0 2.4 pad_maximum_fusion
  281.4 6.2 %copy.39 = bf16[2,1024,1024]{2,1,0:T(8,128)(2,1)} copy(bf16[2,1024,1024]{1,2,0:T(8,128)(2,1)} %pad_maximum_fusion) | data formatting | bytes 8388608
  287.6 10.0 %collective-permute-done.6 = bf16[128,4096]{1,0:T(8,128)(2,1)S(1)} collective-permute-done((bf16[128,4096]{1,0:T(8,128)(2,1)}, bf16[128,4096]{1,0:T(8,128)(2,1)S(1)}, u32[]{:S(2)}, u32[]{:S(2)}) %collective-permute-start.6) | collective-permute-done | bytes 1048608 | tf_op jit(solution)/shard_map/ppermute | solution.py:24
  297.8 1.3 collective-permute-start.7
  299.1 0.8 reshape.243
  299.9 1.5 fusion.94
  302.1 4.0 %fusion.10 = bf16[1,512,2048]{2,1,0:T(8,128)(2,1)} fusion(bf16[520,2048]{1,0:T(8,128)(2,1)S(1)} %constant_dynamic-update-slice_fusion.2, s32[512]{0:T(512)S(1)} %iota_add_fusion, s32[512]{0:T(512)S(1)} %get-tuple-element.65, s32[512]{0:T(512)S(1)} %get-tuple-element.71, s32[]{:T(128)S(6)} %mul.191, s32[512]{0:T(512)S(1)} %get-tuple-element.66, ...), kind=kOutput, calls=%fused_computation.14 | convolution fusion | flops 1096359936 | bytes 4238852 | tf_op jit(solution)/shard_map/dot_general | solution.py:126
  (125 shorter events, 10.7 us)
Async XLA Ops:
  0.6 5.4 %copy-start = (bf16[1,512,2048]{2,1,0:T(8,128)(2,1)S(1)}, bf16[1,512,2048]{2,1,0:T(8,128)(2,1)}, u32[]{:S(2)}) copy-start(bf16[1,512,2048]{2,1,0:T(8,128)(2,1)} %param.6) | copy-start | bytes 6291460
  2.1 0.7 copy-start.6
  2.1 0.8 copy-start.8
  2.1 0.9 copy-start.10
  3.0 28.8 %collective-permute-start.2 = (bf16[512,512]{1,0:T(8,128)(2,1)S(1)}, bf16[512,512]{1,0:T(8,128)(2,1)}, u32[]{:S(2)}, u32[]{:S(2)}) collective-permute-start(bf16[512,512]{1,0:T(8,128)(2,1)S(1)} %get-tuple-element.55), channel_id=1, source_target_pairs={{0,16},{16,0},{1,17},{17,1},{2,18},{18,2},{3,19},{19,3},{4,20},{20... | collective-permute-start | bytes 1572872 | tf_op jit(solution)/shard_map/ppermute | solution.py:24
  6.0 9.1 %copy-start.7 = (bf16[128,1024]{1,0:T(8,128)(2,1)S(1)}, bf16[128,1024]{1,0:T(8,128)(2,1)}, u32[]{:S(2)}) copy-start(bf16[128,1024]{1,0:T(8,128)(2,1)} %copy-done.6) | copy-start | bytes 786436
  6.0 9.1 %copy-start.9 = (bf16[128,1024]{1,0:T(8,128)(2,1)S(1)}, bf16[128,1024]{1,0:T(8,128)(2,1)}, u32[]{:S(2)}) copy-start(bf16[128,1024]{1,0:T(8,128)(2,1)} %copy-done.8) | copy-start | bytes 786436
  6.1 9.1 %copy-start.11 = (bf16[128,1024]{1,0:T(8,128)(2,1)S(1)}, bf16[128,1024]{1,0:T(8,128)(2,1)}, u32[]{:S(2)}) copy-start(bf16[128,1024]{1,0:T(8,128)(2,1)} %copy-done.10) | copy-start | bytes 786436
  6.1 9.1 %copy-start.22 = (bf16[1,4096,1024]{2,1,0:T(8,128)(2,1)S(1)}, bf16[1,4096,1024]{2,1,0:T(8,128)(2,1)}, u32[]{:S(2)}) copy-start(bf16[1,4096,1024]{2,1,0:T(8,128)(2,1)} %param.8) | copy-start | bytes 25165828
  10.2 11.1 %collective-permute-start.18 = (bf16[128,1024]{1,0:T(8,128)(2,1)S(1)}, bf16[128,1024]{1,0:T(8,128)(2,1)S(1)}, u32[]{:S(2)}, u32[]{:S(2)}) collective-permute-start(bf16[128,1024]{1,0:T(8,128)(2,1)S(1)} %get-tuple-element.46), channel_id=1, source_target_pairs={{0,20},{4,16},{8,28},{12,24},{16,4},{20,0},{24,12},{28,8},{1,21},{... | collective-permute-start | bytes 786440 | tf_op jit(solution)/shard_map/ppermute | solution.py:58
  11.7 12.9 %collective-permute-start.17 = (bf16[128,1024]{1,0:T(8,128)(2,1)S(1)}, bf16[128,1024]{1,0:T(8,128)(2,1)S(1)}, u32[]{:S(2)}, u32[]{:S(2)}) collective-permute-start(bf16[128,1024]{1,0:T(8,128)(2,1)S(1)} %get-tuple-element.47), channel_id=1, source_target_pairs={{0,4},{4,0},{8,12},{12,8},{1,5},{5,1},{9,13},{13,9},{2,6},{6,2},{1... | collective-permute-start | bytes 786440 | tf_op jit(solution)/shard_map/ppermute | solution.py:24
  11.8 19.7 %collective-permute-start.10 = (bf16[128,1024]{1,0:T(8,128)(2,1)S(1)}, bf16[128,1024]{1,0:T(8,128)(2,1)S(1)}, u32[]{:S(2)}, u32[]{:S(2)}) collective-permute-start(bf16[128,1024]{1,0:T(8,128)(2,1)S(1)} %get-tuple-element.49), channel_id=1, source_target_pairs={{0,20},{4,16},{8,28},{12,24},{16,4},{20,0},{24,12},{28,8},{1,21},{... | collective-permute-start | bytes 786440 | tf_op jit(solution)/shard_map/ppermute | solution.py:58
  14.7 21.2 %collective-permute-start.9 = (bf16[128,1024]{1,0:T(8,128)(2,1)S(1)}, bf16[128,1024]{1,0:T(8,128)(2,1)S(1)}, u32[]{:S(2)}, u32[]{:S(2)}) collective-permute-start(bf16[128,1024]{1,0:T(8,128)(2,1)S(1)} %get-tuple-element.50), channel_id=1, source_target_pairs={{0,4},{4,0},{8,12},{12,8},{1,5},{5,1},{9,13},{13,9},{2,6},{6,2},{1... | collective-permute-start | bytes 786440 | tf_op jit(solution)/shard_map/ppermute | solution.py:24
  21.2 37.4 %copy-start.12 = (bf16[128,1024]{1,0:T(8,128)(2,1)}, bf16[128,1024]{1,0:T(8,128)(2,1)S(1)}, u32[]{:S(2)}) copy-start(bf16[128,1024]{1,0:T(8,128)(2,1)S(1)} %collective-permute-done.18) | copy-start | bytes 786436
  21.2 35.7 %collective-permute-start.8 = (bf16[128,1024]{1,0:T(8,128)(2,1)}, bf16[128,1024]{1,0:T(8,128)(2,1)S(1)}, u32[]{:S(2)}, u32[]{:S(2)}) collective-permute-start(bf16[128,1024]{1,0:T(8,128)(2,1)} %get-tuple-element.51), channel_id=1, source_target_pairs={{0,16},{16,0},{1,17},{17,1},{2,18},{18,2},{3,19},{19,3},{4,20},{20... | collective-permute-start | bytes 786440 | tf_op jit(solution)/shard_map/ppermute | solution.py:24
  24.6 34.1 %copy-start.14 = (bf16[128,1024]{1,0:T(8,128)(2,1)}, bf16[128,1024]{1,0:T(8,128)(2,1)S(1)}, u32[]{:S(2)}) copy-start(bf16[128,1024]{1,0:T(8,128)(2,1)S(1)} %collective-permute-done.17) | copy-start | bytes 786436
  24.6 35.2 %collective-permute-start.14 = (bf16[512,512]{1,0:T(8,128)(2,1)S(1)}, bf16[512,512]{1,0:T(8,128)(2,1)}, u32[]{:S(2)}, u32[]{:S(2)}) collective-permute-start(bf16[512,512]{1,0:T(8,128)(2,1)S(1)} %get-tuple-element.55), channel_id=1, source_target_pairs={{0,4},{4,0},{8,12},{12,8},{1,5},{5,1},{9,13},{13,9},{2,6},{6,2},{1... | collective-permute-start | bytes 1572872 | tf_op jit(solution)/shard_map/ppermute | solution.py:24
  31.6 29.7 %collective-permute-start.3 = (bf16[512,512]{1,0:T(8,128)(2,1)S(1)}, bf16[512,512]{1,0:T(8,128)(2,1)}, u32[]{:S(2)}, u32[]{:S(2)}) collective-permute-start(bf16[512,512]{1,0:T(8,128)(2,1)S(1)} %get-tuple-element.56), channel_id=1, source_target_pairs={{0,16},{16,0},{1,17},{17,1},{2,18},{18,2},{3,19},{19,3},{4,20},{20... | collective-permute-start | bytes 1572872 | tf_op jit(solution)/shard_map/ppermute | solution.py:24
  31.8 30.1 %collective-permute-start.15 = (bf16[512,512]{1,0:T(8,128)(2,1)}, bf16[512,512]{1,0:T(8,128)(2,1)}, u32[]{:S(2)}, u32[]{:S(2)}) collective-permute-start(bf16[512,512]{1,0:T(8,128)(2,1)} %collective-permute-done.2), channel_id=1, source_target_pairs={{0,4},{4,0},{8,12},{12,8},{1,5},{5,1},{9,13},{13,9},{2,6},{6,2},{1... | collective-permute-start | bytes 1572872 | tf_op jit(solution)/shard_map/ppermute | solution.py:24
  35.9 21.1 %collective-permute-start.16 = (bf16[128,1024]{1,0:T(8,128)(2,1)S(1)}, bf16[128,1024]{1,0:T(8,128)(2,1)S(1)}, u32[]{:S(2)}, u32[]{:S(2)}) collective-permute-start(bf16[128,1024]{1,0:T(8,128)(2,1)S(1)} %get-tuple-element.48), channel_id=1, source_target_pairs={{0,16},{16,0},{1,17},{17,1},{2,18},{18,2},{3,19},{19,3},{4,20},{20... | collective-permute-start | bytes 786440 | tf_op jit(solution)/shard_map/ppermute | solution.py:24
  56.9 50.8 %collective-permute-start = (bf16[256,4096]{1,0:T(8,128)(2,1)}, bf16[256,4096]{1,0:T(8,128)(2,1)S(1)}, u32[]{:S(2)}, u32[]{:S(2)}) collective-permute-start(bf16[256,4096]{1,0:T(8,128)(2,1)} %slice.147), channel_id=1, source_target_pairs={{0,1},{1,0},{2,3},{3,2},{4,5},{5,4},{6,7},{7,6},{8,9},{9,8},{10,11... | collective-permute-start | bytes 6291464 | tf_op jit(solution)/shard_map/ppermute | solution.py:24
  57.0 13.5 %copy-start.16 = (bf16[128,1024]{1,0:T(8,128)(2,1)}, bf16[128,1024]{1,0:T(8,128)(2,1)S(1)}, u32[]{:S(2)}) copy-start(bf16[128,1024]{1,0:T(8,128)(2,1)S(1)} %collective-permute-done.16) | copy-start | bytes 786436
  57.0 15.4 %collective-permute-start.24 = (bf16[512,512]{1,0:T(8,128)(2,1)S(1)}, bf16[512,512]{1,0:T(8,128)(2,1)S(1)}, u32[]{:S(2)}, u32[]{:S(2)}) collective-permute-start(bf16[512,512]{1,0:T(8,128)(2,1)S(1)} %get-tuple-element.56), channel_id=1, source_target_pairs={{0,4},{4,0},{8,12},{12,8},{1,5},{5,1},{9,13},{13,9},{2,6},{6,2},{1... | collective-permute-start | bytes 1572872 | tf_op jit(solution)/shard_map/ppermute | solution.py:24
  59.8 26.2 %collective-permute-start.19 = (bf16[512,1024]{1,0:T(8,128)(2,1)}, bf16[512,1024]{1,0:T(8,128)(2,1)S(1)}, u32[]{:S(2)}, u32[]{:S(2)}) collective-permute-start(bf16[512,1024]{1,0:T(8,128)(2,1)} %pad_maximum_fusion.7), channel_id=1, source_target_pairs={{0,2},{1,3},{2,0},{3,1},{4,6},{5,7},{6,4},{7,5},{8,10},{9,11},{10,... | collective-permute-start | bytes 3145736 | tf_op jit(solution)/shard_map/ppermute | solution.py:24
  61.3 46.4 %collective-permute-start.11 = (bf16[512,1024]{1,0:T(8,128)(2,1)S(1)}, bf16[512,1024]{1,0:T(8,128)(2,1)S(1)}, u32[]{:S(2)}, u32[]{:S(2)}) collective-permute-start(bf16[512,1024]{1,0:T(8,128)(2,1)S(1)} %pad_maximum_fusion.6), channel_id=1, source_target_pairs={{0,2},{1,3},{2,0},{3,1},{4,6},{5,7},{6,4},{7,5},{8,10},{9,11},{10,... | collective-permute-start | bytes 3145736 | tf_op jit(solution)/shard_map/ppermute | solution.py:24
  61.8 20.8 %collective-permute-start.25 = (bf16[512,512]{1,0:T(8,128)(2,1)}, bf16[512,512]{1,0:T(8,128)(2,1)S(1)}, u32[]{:S(2)}, u32[]{:S(2)}) collective-permute-start(bf16[512,512]{1,0:T(8,128)(2,1)} %collective-permute-done.3), channel_id=1, source_target_pairs={{0,4},{4,0},{8,12},{12,8},{1,5},{5,1},{9,13},{13,9},{2,6},{6,2},{1... | collective-permute-start | bytes 1572872 | tf_op jit(solution)/shard_map/ppermute | solution.py:24
  70.7 37.6 %copy-start.5 = (bf16[512,4096]{1,0:T(8,128)(2,1)S(1)}, bf16[512,4096]{1,0:T(8,128)(2,1)}, u32[]{:S(2)}) copy-start(bf16[512,4096]{1,0:T(8,128)(2,1)} %fusion.4) | copy-start | bytes 12582916
  72.5 0.8 copy-start.18
  72.5 39.5 %collective-permute-start.21 = (bf16[512,1024]{1,0:T(8,128)(2,1)}, bf16[512,1024]{1,0:T(8,128)(2,1)S(1)}, u32[]{:S(2)}, u32[]{:S(2)}) collective-permute-start(bf16[512,1024]{1,0:T(8,128)(2,1)} %pad_maximum_fusion.7), channel_id=1, source_target_pairs={{0,1},{1,0},{2,3},{3,2},{4,5},{5,4},{6,7},{7,6},{8,9},{9,8},{10,11... | collective-permute-start | bytes 3145736 | tf_op jit(solution)/shard_map/ppermute | solution.py:24
  82.7 36.7 %collective-permute-start.13 = (bf16[512,1024]{1,0:T(8,128)(2,1)S(1)}, bf16[512,1024]{1,0:T(8,128)(2,1)S(1)}, u32[]{:S(2)}, u32[]{:S(2)}) collective-permute-start(bf16[512,1024]{1,0:T(8,128)(2,1)S(1)} %pad_maximum_fusion.6), channel_id=1, source_target_pairs={{0,1},{1,0},{2,3},{3,2},{4,5},{5,4},{6,7},{7,6},{8,9},{9,8},{10,11... | collective-permute-start | bytes 3145736 | tf_op jit(solution)/shard_map/ppermute | solution.py:24
  86.0 37.6 %collective-permute-start.4 = (bf16[256,4096]{1,0:T(8,128)(2,1)S(1)}, bf16[256,4096]{1,0:T(8,128)(2,1)S(1)}, u32[]{:S(2)}, u32[]{:S(2)}) collective-permute-start(bf16[256,4096]{1,0:T(8,128)(2,1)S(1)} %slice.155), channel_id=1, source_target_pairs={{0,1},{1,0},{2,3},{3,2},{4,5},{5,4},{6,7},{7,6},{8,9},{9,8},{10,11... | collective-permute-start | bytes 6291464 | tf_op jit(solution)/shard_map/ppermute | solution.py:24
  107.7 2.7 collective-permute-start.20
  107.8 9.8 %collective-permute-start.12 = (bf16[512,1024]{1,0:T(8,128)(2,1)S(1)}, bf16[512,1024]{1,0:T(8,128)(2,1)S(1)}, u32[]{:S(2)}, u32[]{:S(2)}) collective-permute-start(bf16[512,1024]{1,0:T(8,128)(2,1)S(1)} %collective-permute-done.11), channel_id=1, source_target_pairs={{0,1},{1,0},{2,3},{3,2},{4,5},{5,4},{6,7},{7,6},{8,9},{9,8},{10,11... | collective-permute-start | bytes 3145736 | tf_op jit(solution)/shard_map/ppermute | solution.py:24
  109.0 3.2 %copy-start.2 = (f32[256,4096]{1,0:T(8,128)}, f32[256,4096]{1,0:T(8,128)S(1)}, u32[]{:S(2)}) copy-start(f32[256,4096]{1,0:T(8,128)S(1)} %convert_add_fusion.1) | copy-start | bytes 12582916
  109.0 3.2 %copy-start.17 = (bf16[128,1024]{1,0:T(8,128)(2,1)S(1)}, bf16[128,1024]{1,0:T(8,128)(2,1)}, u32[]{:S(2)}) copy-start(bf16[128,1024]{1,0:T(8,128)(2,1)} %copy-done.16) | copy-start | bytes 786436
  109.1 3.1 %copy-start.15 = (bf16[128,1024]{1,0:T(8,128)(2,1)S(1)}, bf16[128,1024]{1,0:T(8,128)(2,1)}, u32[]{:S(2)}) copy-start(bf16[128,1024]{1,0:T(8,128)(2,1)} %copy-done.14) | copy-start | bytes 786436
  109.1 3.2 %copy-start.13 = (bf16[128,1024]{1,0:T(8,128)(2,1)S(1)}, bf16[128,1024]{1,0:T(8,128)(2,1)}, u32[]{:S(2)}) copy-start(bf16[128,1024]{1,0:T(8,128)(2,1)} %copy-done.12) | copy-start | bytes 786436
  110.4 139.7 %collective-permute-start.1 = (bf16[128,4096]{1,0:T(8,128)(2,1)S(1)}, bf16[128,4096]{1,0:T(8,128)(2,1)}, u32[]{:S(2)}, u32[]{:S(2)}) collective-permute-start(bf16[128,4096]{1,0:T(8,128)(2,1)S(1)} %slice.235), channel_id=1, source_target_pairs={{0,2},{1,3},{2,0},{3,1},{4,6},{5,7},{6,4},{7,5},{8,10},{9,11},{10,... | collective-permute-start | bytes 3145736 | tf_op jit(solution)/shard_map/ppermute | solution.py:24
  113.6 94.5 %collective-permute-start.22 = (bf16[1024,256]{0,1:T(8,128)(2,1)S(1)}, bf16[1024,256]{0,1:T(8,128)(2,1)S(1)}, u32[]{:S(2)}, u32[]{:S(2)}) collective-permute-start(bf16[1024,256]{0,1:T(8,128)(2,1)S(1)} %convolution_convert_fusion.5), channel_id=1, source_target_pairs={{0,8},{4,12},{8,0},{12,4},{1,9},{5,13},{9,1},{13,5},{2,10},{6,14},... | collective-permute-start | bytes 1572872 | tf_op jit(solution)/shard_map/ppermute | solution.py:138
  117.6 66.8 %collective-permute-start.23 = (bf16[1024,256]{0,1:T(8,128)(2,1)S(1)}, bf16[1024,256]{0,1:T(8,128)(2,1)S(1)}, u32[]{:S(2)}, u32[]{:S(2)}) collective-permute-start(bf16[1024,256]{0,1:T(8,128)(2,1)S(1)} %convolution_convert_fusion.4), channel_id=1, source_target_pairs={{0,8},{4,12},{8,0},{12,4},{1,9},{5,13},{9,1},{13,5},{2,10},{6,14},... | collective-permute-start | bytes 1572872 | tf_op jit(solution)/shard_map/ppermute | solution.py:138
  119.4 76.3 %collective-permute-start.26 = (bf16[1024,256]{0,1:T(8,128)(2,1)S(1)}, bf16[1024,256]{0,1:T(8,128)(2,1)S(1)}, u32[]{:S(2)}, u32[]{:S(2)}) collective-permute-start(bf16[1024,256]{0,1:T(8,128)(2,1)S(1)} %convolution_convert_fusion.3), channel_id=1, source_target_pairs={{0,8},{4,12},{8,0},{12,4},{1,9},{5,13},{9,1},{13,5},{2,10},{6,14},... | collective-permute-start | bytes 1572872 | tf_op jit(solution)/shard_map/ppermute | solution.py:138
  122.3 84.5 %copy-start.19 = (bf16[2048,1024]{1,0:T(8,128)(2,1)}, bf16[2048,1024]{1,0:T(8,128)(2,1)S(1)}, u32[]{:S(2)}) copy-start(bf16[2048,1024]{1,0:T(8,128)(2,1)S(1)} %constant_dynamic-update-slice_fusion.3) | copy-start | bytes 12582916
  123.6 83.2 %collective-permute-start.27 = (bf16[1024,256]{0,1:T(8,128)(2,1)S(1)}, bf16[1024,256]{0,1:T(8,128)(2,1)S(1)}, u32[]{:S(2)}, u32[]{:S(2)}) collective-permute-start(bf16[1024,256]{0,1:T(8,128)(2,1)S(1)} %convolution_convert_fusion.2), channel_id=1, source_target_pairs={{0,8},{4,12},{8,0},{12,4},{1,9},{5,13},{9,1},{13,5},{2,10},{6,14},... | collective-permute-start | bytes 1572872 | tf_op jit(solution)/shard_map/ppermute | solution.py:138
  124.9 61.3 %copy-start.3 = (f32[256,4096]{1,0:T(8,128)}, f32[256,4096]{1,0:T(8,128)S(1)}, u32[]{:S(2)}) copy-start(f32[256,4096]{1,0:T(8,128)S(1)} %convert_add_fusion) | copy-start | bytes 12582916
  184.4 72.0 %collective-permute-start.5 = (bf16[128,4096]{1,0:T(8,128)(2,1)S(1)}, bf16[128,4096]{1,0:T(8,128)(2,1)}, u32[]{:S(2)}, u32[]{:S(2)}) collective-permute-start(bf16[128,4096]{1,0:T(8,128)(2,1)S(1)} %slice.234), channel_id=1, source_target_pairs={{0,2},{1,3},{2,0},{3,1},{4,6},{5,7},{6,4},{7,5},{8,10},{9,11},{10,... | collective-permute-start | bytes 3145736 | tf_op jit(solution)/shard_map/ppermute | solution.py:24
  227.4 32.7 %collective-permute-start.28 = (bf16[1024,256]{0,1:T(8,128)(2,1)}, bf16[1024,256]{0,1:T(8,128)(2,1)}, u32[]{:S(2)}, u32[]{:S(2)}) collective-permute-start(bf16[1024,256]{0,1:T(8,128)(2,1)} %get-tuple-element.15), channel_id=1, source_target_pairs={{0,16},{16,0},{1,17},{17,1},{2,18},{18,2},{3,19},{19,3},{4,20},{20... | collective-permute-start | bytes 1572872 | tf_op jit(solution)/shard_map/ppermute | solution.py:24
  227.9 32.2 %collective-permute-start.31 = (bf16[1024,256]{0,1:T(8,128)(2,1)}, bf16[1024,256]{0,1:T(8,128)(2,1)}, u32[]{:S(2)}, u32[]{:S(2)}) collective-permute-start(bf16[1024,256]{0,1:T(8,128)(2,1)} %get-tuple-element.31), channel_id=1, source_target_pairs={{0,16},{16,0},{1,17},{17,1},{2,18},{18,2},{3,19},{19,3},{4,20},{20... | collective-permute-start | bytes 1572872 | tf_op jit(solution)/shard_map/ppermute | solution.py:24
  229.4 35.5 %collective-permute-start.30 = (bf16[1024,256]{0,1:T(8,128)(2,1)}, bf16[1024,256]{0,1:T(8,128)(2,1)}, u32[]{:S(2)}, u32[]{:S(2)}) collective-permute-start(bf16[1024,256]{0,1:T(8,128)(2,1)} %get-tuple-element.35), channel_id=1, source_target_pairs={{0,16},{16,0},{1,17},{17,1},{2,18},{18,2},{3,19},{19,3},{4,20},{20... | collective-permute-start | bytes 1572872 | tf_op jit(solution)/shard_map/ppermute | solution.py:24
  250.2 26.0 %collective-permute-start.29 = (bf16[1024,256]{0,1:T(8,128)(2,1)}, bf16[1024,256]{0,1:T(8,128)(2,1)}, u32[]{:S(2)}, u32[]{:S(2)}) collective-permute-start(bf16[1024,256]{0,1:T(8,128)(2,1)} %get-tuple-element.39), channel_id=1, source_target_pairs={{0,16},{16,0},{1,17},{17,1},{2,18},{18,2},{3,19},{19,3},{4,20},{20... | collective-permute-start | bytes 1572872 | tf_op jit(solution)/shard_map/ppermute | solution.py:24
  254.6 2.2 copy-start.4
  259.3 38.3 %collective-permute-start.6 = (bf16[128,4096]{1,0:T(8,128)(2,1)}, bf16[128,4096]{1,0:T(8,128)(2,1)S(1)}, u32[]{:S(2)}, u32[]{:S(2)}) collective-permute-start(bf16[128,4096]{1,0:T(8,128)(2,1)} %fusion.11), channel_id=1, source_target_pairs={{0,16},{16,0},{1,17},{17,1},{2,18},{18,2},{3,19},{19,3},{4,20},{20... | collective-permute-start | bytes 3145736 | tf_op jit(solution)/shard_map/ppermute | solution.py:24
  260.1 16.1 %copy-start.20 = (bf16[520,2048]{1,0:T(8,128)(2,1)}, bf16[520,2048]{1,0:T(8,128)(2,1)S(1)}, u32[]{:S(2)}) copy-start(bf16[520,2048]{1,0:T(8,128)(2,1)S(1)} %fusion.57) | copy-start | bytes 6389764
  297.8 4.3 %collective-permute-start.7 = (bf16[3,2048]{1,0:T(4,128)(2,1)S(1)}, bf16[3,2048]{1,0:T(4,128)(2,1)S(1)}, u32[]{:S(2)}, u32[]{:S(2)}) collective-permute-start(bf16[3,2048]{1,0:T(4,128)(2,1)S(1)} %pad_maximum_fusion.8), channel_id=1, source_target_pairs={{1,0},{2,1},{3,2},{4,3},{5,4},{6,5},{7,6},{8,7},{9,8},{10,9},{11,1... | collective-permute-start | bytes 36872 | tf_op jit(solution)/shard_map/ppermute | solution.py:118
  299.9 1.6 copy-start.21
  302.1 4.0 %copy-start.1 = (bf16[1,512,2048]{2,1,0:T(8,128)(2,1)S(1)}, bf16[1,512,2048]{2,1,0:T(8,128)(2,1)}, u32[]{:S(2)}) copy-start(bf16[1,512,2048]{2,1,0:T(8,128)(2,1)} %param.6) | copy-start | bytes 6291460

commit v2 on v0

v2 whole, which is shorter than its diff:
```python
import functools
import math

import jax
import jax.numpy as jnp
from jax import lax
from jax.experimental import pallas as pl
from jax.experimental.pallas import tpu as pltpu
from jax.sharding import PartitionSpec as P

SHORT = 4
first_beta = 0.9
second_beta = 0.95
first_fix = 1.0 - 0.9**10
second_fix = 1.0 - 0.95**10
adam_eps = 1e-08
learn_rate = 0.05
weight_decay = 0.1
PIECES = 4

bf16, f32 = jnp.bfloat16, jnp.float32


def swap(value, axis, step):
    count = lax.axis_size(axis)
    return lax.ppermute(value, axis, [(i, i ^ step) for i in range(count)])


def launch(kernel, values, out, grid=(), in_specs=None, out_specs=None, scalars=(), aliases=None, after=(), limit=14):
    whole = pl.BlockSpec(memory_space=pltpu.VMEM)
    taken = len(scalars) + len(values)

    def body(*refs):
        kernel(*refs[:taken], *refs[taken + len(after) :])

    return pl.pallas_call(
        body,
        grid_spec=pltpu.PrefetchScalarGridSpec(
            num_scalar_prefetch=len(scalars),
            grid=grid,
            in_specs=(in_specs or [whole] * len(values))
            + [pl.BlockSpec(memory_space=pl.ANY)] * len(after),
            out_specs=out_specs or [whole] * len(out),
        ),
        out_shape=[jax.ShapeDtypeStruct(shape, dtype) for shape, dtype in out],
        input_output_aliases=aliases or {},
        compiler_params=pltpu.CompilerParams(vmem_limit_bytes=limit * 2**20),
        cost_estimate=pl.CostEstimate(flops=1, bytes_accessed=1, transcendentals=0),
    )(*scalars, *values, *after)


def sort_kernel(order, m_ref, grad_ref, sent_ref, kept_ref, *piece_refs):
    count = grad_ref.shape[0] // len(order)
    half = len(order) // 2
    for i, j in enumerate(order):
        start = pl.multiple_of((m_ref[0] ^ j) * count, count)
        rows = grad_ref[pl.ds(start, count), :]
        ref, at = (sent_ref, i) if i < half else (kept_ref, i - half)
        ref[at * count : (at + 1) * count, :] = rows
        first = 0
        for ref in piece_refs:
            ref[i * count : (i + 1) * count, :] = rows[:, first : first + ref.shape[1]]
            first += ref.shape[1]


def halves_kernel(own_ref, first_ref, later_ref, sent_ref, kept_ref, *pack_refs):
    count, split = sent_ref.shape[0], first_ref.shape[1]
    for ref, part in ((sent_ref, slice(0, count)), (kept_ref, slice(count, 2 * count))):
        ref[:, :split] = first_ref[part]
        ref[:, split:] = later_ref[part]
    for i, ref in enumerate(pack_refs):
        at = slice(i * ref.shape[1], (i + 1) * ref.shape[1])
        ref[: 2 * count] = own_ref[:, at]
        ref[2 * count :] = later_ref[:, at]


def split_kernel(rows, block, at_ref, fine_ref, *out_refs):
    count = fine_ref.shape[0]
    r = lax.broadcasted_iota(jnp.int32, (rows, count), 0)
    t = lax.broadcasted_iota(jnp.int32, (rows, count), 1)
    i = 0
    for out_ref in out_refs:
        for k in range(out_ref.shape[0] // rows):
            pick = jnp.where(t == SHORT * r + at_ref[2 * i], 1.0, 0.0).astype(bf16)
            columns = pl.ds(pl.multiple_of(at_ref[2 * i + 1] * block, block), block)
            out_ref[k * rows : (k + 1) * rows, :] = jnp.dot(
                pick, fine_ref[:, columns], preferred_element_type=f32
            ).astype(bf16)
            i += 1


def stack_kernel(picks, *refs):
    count = len(refs) - len(picks)
    for pick, out_ref in zip(picks, refs[count:]):
        at = 0
        for i, first, size in pick:
            out_ref[at : at + size, :] = refs[i][first : first + size, :]
            at += size


def stack(picks, *values, after=()):
    out = [
        ((sum(size for _, _, size in pick), values[pick[0][0]].shape[1]), bf16) for pick in picks
    ]
    return launch(functools.partial(stack_kernel, picks), values, out, after=after)


def act_kernel(a_ref, b_ref, w_ref, pair_ref, send_ref, rest_ref):
    count = send_ref.shape[0]
    product = 0.0
    for rows, part in ((a_ref, w_ref), (b_ref, pair_ref)):
        product += lax.dot_general(
            rows[...], part[...], (((1,), (1,)), ((), ())), preferred_element_type=f32
        )
    send_ref[...] = product[:count].astype(bf16)
    rest_ref[...] = product[count:]


def act_products(rows, weights, after=()):
    count = rows[0].shape[0] // 2
    wide, depth = weights[0].shape
    step = 512
    return launch(
        act_kernel,
        [*rows, *weights],
        [((count, wide), bf16), ((count, wide), f32)],
        grid=(wide // step,),
        in_specs=[pl.BlockSpec(v.shape, lambda i: (0, 0)) for v in rows]
        + [pl.BlockSpec((step, depth), lambda i: (i, 0))] * 2,
        out_specs=[pl.BlockSpec((count, step), lambda i: (0, i))] * 2,
        after=after,
    )


def last_kernel(keep_ref, came_ref, out_ref):
    out_ref[...] = (keep_ref[...] + came_ref[...].astype(f32)).astype(bf16)


def last_sum(keep, came, after=()):
    return launch(last_kernel, [keep, came], [(keep.shape, bf16)], after=after)[0]


def against_kernel(groups, places, *refs):
    x_refs, g_refs, out_ref = refs[: sum(groups)], refs[sum(groups) : -1], refs[-1]
    count = x_refs[0].shape[0] * groups[0] // len(places)
    total, first = None, 0
    for j, size in enumerate(groups):
        x = jnp.concatenate([ref[...] for ref in x_refs[first : first + size]], axis=0)
        first += size
        g = jnp.concatenate(
            [
                g_refs[i][row + j * count : row + (j + 1) * count, at : at + out_ref.shape[1]]
                for i, row, at in places
            ],
            axis=0,
        )
        part = lax.dot_general(x, g, (((0,), (0,)), ((), ())), preferred_element_type=f32)
        total = part if total is None else total + part
    out_ref[...] = total.astype(out_ref.dtype)


def against(x, g, cols, dtype, after=()):
    values, places = g
    groups = [len(v) for v in x]
    flat = [v for group in x for v in group]
    return launch(
        functools.partial(against_kernel, groups, places),
        [*flat, *values],
        [((flat[0].shape[1], cols), dtype)],
        after=after,
        limit=20,
    )[0]


def adam_kernel(scale, first, *refs):
    x_ref, own, came, master, moment, second = refs[:6]
    new_master, new_moment, new_second, new_weight, low = refs[6 if first else 10 :]
    gradient = (own[...] + came[...].astype(f32)) * scale
    m = first_beta * moment[...] + (1.0 - first_beta) * gradient
    s = second_beta * second[...] + (1.0 - second_beta) * gradient * gradient
    ratio = m / first_fix / (jnp.sqrt(s / second_fix) + adam_eps)
    w = master[...] - learn_rate * (ratio + weight_decay * master[...])
    new_master[...] = w
    new_moment[...] = m
    new_second[...] = s
    low[...] = w.astype(bf16)
    new_weight[0] = w.astype(bf16)


def adam(x, own, came, state, i, scale, held, after=()):
    rows, cols = own.shape
    wide = state[0].shape[1]
    step = min(256, rows)
    local = pl.BlockSpec((step, cols), lambda r, x: (r, 0))
    whole = pl.BlockSpec((step, cols), lambda r, x: (r, i))
    weight = pl.BlockSpec((1, step, cols), lambda r, x: (x[0], r, i))
    first = held is None
    return launch(
        functools.partial(adam_kernel, scale, first),
        [own, came, *state, *(held or ())],
        [((rows, wide), f32)] * 3 + [((2, rows, wide), bf16), ((rows, cols), bf16)],
        grid=(rows // step,),
        in_specs=[local, local, whole, whole, whole]
        + ([] if first else [pl.BlockSpec(memory_space=pl.ANY)] * 4),
        out_specs=[whole, whole, whole, weight, local],
        scalars=(x.reshape(1),),
        aliases={} if first else {6: 0, 7: 1, 8: 2, 9: 3},
        after=after,
    )


def place_kernel(x_ref, other_ref, held_ref, out_ref):
    out_ref[0] = other_ref[...]


def place_other(x, other, held, column, after=()):
    rows, cols = other.shape
    return launch(
        place_kernel,
        [other, held],
        [(held.shape, held.dtype)],
        grid=(1,),
        in_specs=[
            pl.BlockSpec((rows, cols), lambda r, x: (0, 0)),
            pl.BlockSpec(memory_space=pl.ANY),
        ],
        out_specs=[pl.BlockSpec((1, rows, cols), lambda r, x: (1 - x[0], 0, column))],
        scalars=(x.reshape(1),),
        aliases={2: 0},
        after=after,
    )[0]


def merge_kernel(x_ref, own_ref, other_ref, later_ref, out_ref):
    rows, features = out_ref.shape
    count = own_ref.shape[0]
    t = lax.broadcasted_iota(jnp.int32, (rows, count), 0) + SHORT - 1
    u = lax.broadcasted_iota(jnp.int32, (rows, count), 1)
    e = lax.broadcasted_iota(jnp.int32, (rows, later_ref.shape[0]), 0) + SHORT - 1
    v = lax.broadcasted_iota(jnp.int32, (rows, later_ref.shape[0]), 1)
    x = x_ref[0]
    picks = [
        jnp.where(t == SHORT * u + 2 * side + q, 1.0, 0.0).astype(bf16)
        for side in (x, 1 - x)
        for q in range(2)
    ]
    tail = jnp.where(e == rows + v, 1.0, 0.0).astype(bf16)
    step = 512
    for at in range(0, features, step):
        total = jnp.dot(tail, later_ref[:, at : at + step], preferred_element_type=f32)
        for i, ref in enumerate((own_ref, own_ref, other_ref, other_ref)):
            plane = ref[:, i % 2 * features + at : i % 2 * features + at + step]
            total += jnp.dot(picks[i], plane, preferred_element_type=f32)
        out_ref[:, at : at + step] = total.astype(bf16)


def merge(x, own, other, later, after=()):
    rows = own.shape[0] * SHORT
    return launch(
        merge_kernel,
        [own, other, later],
        [((rows, own.shape[1] // 2), bf16)],
        scalars=(x.reshape(1),),
        after=after,
        limit=20,
    )[0]


def per_device(shortening_input, coarse_grad, weight_copy, master, moment, second):
    fine = shortening_input[0]
    grad = coarse_grad[0]
    weights = weight_copy[0]
    state = (master[0], moment[0], second[0])
    rows_dev, features = fine.shape
    coarse_rows, width = grad.shape
    half_rows = weights.shape[0]
    one = rows_dev // SHORT
    block = master.shape[1]
    n_seq, n_mp = lax.axis_size("seq"), lax.axis_size("mp")
    far = n_seq // 2
    x, z, m = lax.axis_index("dp"), lax.axis_index("seq"), lax.axis_index("mp")
    h, l = z // 2, z % 2
    cols = width // PIECES
    order = (3, 1, 2, 0)

    def place(dp, hi, lo):
        offset = dp * half_rows + (2 * hi + lo) * block
        return [offset // features, offset % features // block]

    def cut(hi, sizes, after):
        places = [place(x, hi, l), place(x, hi, 1 - l), place(1 - x, hi, l), place(1 - x, hi, 1 - l)]
        places = jnp.stack([v for p in places for v in p]).astype(jnp.int32)
        return launch(
            functools.partial(split_kernel, one, block),
            [fine],
            [((size * one, block), bf16) for size in sizes],
            scalars=(places,),
            after=after,
        )

    def diagonal(v):
        return lax.ppermute(v, ("dp", "seq"), [(i, i ^ n_seq ^ 1) for i in range(2 * n_seq)])

    def ahead(v, k):
        return lax.ppermute(v, "seq", [(s, (s + 2 * k) % n_seq) for s in range(n_seq)])

    pair_weights = swap(weights, "mp", 1)
    pair_send, own_rows, g0, g_later = launch(
        functools.partial(sort_kernel, order),
        [grad],
        [((2 * one, width), bf16)] * 2
        + [((coarse_rows, cols), bf16), ((coarse_rows, width - cols), bf16)],
        scalars=(m.reshape(1),),
    )
    g0_dp = swap(g0, "dp", 1)
    first = {}
    last = g0
    for k in range(1, far):
        own, to_seq, to_dp, to_both = cut((h + k) % far, (1, 1, 1, 1), [last])
        first[k] = own, swap(to_dp, "dp", 1), swap(to_seq, "seq", 1), diagonal(to_both)
        last = own
    for k, v in first.items():
        mine, pack = stack(
            [[(i, 0, one) for i in range(4)], [(4, 0, coarse_rows), (5, 0, coarse_rows)]],
            *v, g0, g0_dp, after=[last, pair_weights],
        )
        first[k] = mine, swap(mine, "mp", 1), swap(mine, "mp", 2)
        last = mine
    packs = [swap(pack, "seq", 1)]
    later_dp = swap(g_later, "dp", 1)
    own_pair = swap(pair_send, "mp", 1)
    own_send, own_rest = act_products([own_rows, own_pair], [weights, pair_weights], [last])
    own_came = swap(own_send, "mp", 2)
    last = own_rest
    other_send, other_rows, *later_packs = launch(
        halves_kernel,
        [g_later, g0_dp, later_dp],
        [((2 * one, width), bf16)] * 2 + [((2 * coarse_rows, cols), bf16)] * (PIECES - 1),
        after=[last, packs[0]] + [v[1] for v in first.values()],
    )
    packs += [swap(v, "seq", 1) for v in later_packs]
    other_pair = swap(other_send, "mp", 1)
    own, to_seq, to_dp = cut(h, (1, 1, 2), [other_rows])
    x_dp = swap(to_dp, "dp", 1)
    last = own
    x_far = {}
    for k, (mine, beside, across) in first.items():
        (across,) = stack([[(0, 0, 4 * one)]], across, after=[last])
        x_far[k] = [swap(across, "mp", 1)], [beside], [across], [mine]
        last = across
    other_send, other_rest = act_products([other_rows, other_pair], [weights, pair_weights], [last])
    other_came = swap(other_send, "mp", 2)
    last = other_rest

    def gradients(i):
        if i == 0:
            return [g0, g0_dp, packs[0]], [(0, 0, 0), (1, 0, 0), (2, 0, 0), (2, coarse_rows, 0)]
        at = (i - 1) * cols
        return [g_later, later_dp, packs[i]], [(0, 0, at), (1, 0, at), (2, 0, 0), (2, coarse_rows, 0)]

    def far_sums(i, after):
        came = []
        for k, v in x_far.items():
            sent = against(v, gradients(i), cols, bf16, after=after)
            came.append(ahead(sent, k))
            after = [sent]
        return (came[0] if far == 2 else sum(v.astype(f32) for v in came)), sent

    sums = {}
    sums[0], last = far_sums(0, [last, packs[1]])
    near, to_seq = stack(
        [[(0, 0, one), (2, 0, one)], [(1, 0, one), (2, one, one)]], own, to_seq, x_dp, after=[last]
    )
    x_seq = swap(to_seq, "seq", 1)
    (mine,) = stack([[(0, 0, 2 * one), (1, 0, 2 * one)]], near, x_seq, after=[sums[0]])
    across, beside = swap(mine, "mp", 2), swap(mine, "mp", 1)
    sums[1], last = far_sums(1, [mine])
    act_other = last_sum(other_rest, other_came, after=[last])
    act_other_came = swap(act_other, "dp", 1)
    (across,) = stack([[(0, 0, 4 * one)]], across, after=[act_other, act_other_came, beside, sums[1], packs[2]])
    both = swap(across, "mp", 1)
    x_near = [both], [beside], [across], [mine]
    sums[2], last = far_sums(2, [across])
    scale = 1.0 / math.sqrt(lax.axis_size("dp") * coarse_rows * n_seq)
    held, others = None, []

    def nearby(i, after):
        return against(x_near, gradients(i), cols, f32, after=after)

    def update(i, gradient, after):
        nonlocal held
        *held, low = adam(x, gradient, sums[i], state, i, scale, held, after=after)
        others.append(swap(low, "dp", 1))
        return low

    last = update(0, nearby(0, [last]), [])
    last = update(1, nearby(1, [last]), [])
    sums[3], last = far_sums(3, [last, sums[2]])
    last = update(2, nearby(2, [last]), [])
    gradient = nearby(3, [last])

    def put(i, after):
        held[3] = place_other(x, others[i], held[3], i, after=after)

    put(0, [gradient])
    put(1, [])
    act_own = last_sum(own_rest, own_came, after=[held[3]])
    head = jnp.where(
        x == 0,
        jnp.concatenate([act_own[:1], act_other_came[:1]], axis=1),
        jnp.concatenate([act_other_came[:1], act_own[:1]], axis=1),
    )
    head = head[:, : (SHORT - 1) * features].reshape(SHORT - 1, features)
    count = n_seq * n_mp
    later = lax.ppermute(head, ("seq", "mp"), [(s, s - 1) for s in range(1, count)])
    later = jnp.pad(later, ((0, 16 - (SHORT - 1)), (0, 0)))
    act_grad = merge(x, act_own, act_other_came, later)
    last = update(3, gradient, [act_grad])
    put(2, [last])
    put(3, [])
    new_master, new_moment, new_second, new_weight = held
    return (act_grad[None], new_master[None], new_moment[None], new_second[None], new_weight)


def solution(mesh):
    return jax.shard_map(
        per_device,
        mesh=mesh,
        in_specs=(
            P("dp", ("seq", "mp"), None),
            P("dp", "seq", "mp"),
            P("dp", None, "mp"),
            P("dp", "seq", "mp"),
            P("dp", "seq", "mp"),
            P("dp", "seq", "mp"),
        ),
        out_specs=(
            P("dp", ("seq", "mp"), None),
            P("dp", "seq", "mp"),
            P("dp", "seq", "mp"),
            P("dp", "seq", "mp"),
            P(None, "seq", "mp"),
        ),
        check_vma=False,
    )
```

time: 701 us -> 230 us (0.33)
  waiting for transfers between devices: 602 us -> 92.7 us
  Pallas kernels: 0 us -> 66.1 us
  matrix products: 46.7 us -> 0 us
  starting transfers between devices: 1.49 us -> 36.4 us
  between operations: 13.8 us -> 1.08 us
  other arithmetic: 12.3 us -> 0.1 us
  local copies, waits for them, and re-layouts: 23.9 us -> 32.1 us
    reduce_scatter x2 -> x0, waiting for transfers between devices: 319 us -> none  [the longest x1 256 us: per_device(): lax.psum_scatter(lax.dot_general(gathered, grad_cols, (((0,), (0,)), ((),...]
    all_gather x3 -> x0, waiting for transfers between devices: 281 us -> none  [the longest x1 168 us: per_device(): whole_copy = lax.all_gather(weight_copy, 'dp', axis=0, tiled=True)]
    ppermute x1 -> x32, waiting for transfers between devices: 1.27 us -> 92.7 us  [the longest x26 75.5 us: swap(): return lax.ppermute(value, axis, [(i, i ^ step) for i in range(count)])]
    pallas_call x0 -> x30, Pallas kernels: none -> 66.1 us  [launch(): pl.pallas_call(body, grid_spec=pltpu.PrefetchScalarGridSpec(num_scalar_pr...]
    dot_general x2 -> x0, matrix products: 46.7 us -> none  [the longest x1 29.6 us: per_device(): lax.dot_general(grad_cols, weights, (((1,), (1,)), ((), ())), preferred_e...]
    ppermute x1 -> x32, starting transfers between devices: 1.29 us -> 36.4 us  [the longest x26 27 us: swap(): return lax.ppermute(value, axis, [(i, i ^ step) for i in range(count)])]
    unnamed x5 -> x94, local copies, waits for them, and re-layouts: 4.74 us -> 30.9 us
    reshape x2 -> x1, local copies, waits for them, and re-layouts: 18.6 us -> 0.02 us  [per_device(): head = head[:, :(SHORT - 1) * features].reshape(SHORT - 1, features)]
  transfers between devices with their start and end apart: 6 -> 32, of which waited for: 6 -> 15; matrix products, arithmetic and copies ran while one was open for 11% -> 1% of each run, Pallas kernels for 0% -> 28%
where the time goes in v2:
time: 230 us; the launch traced here: 229 us
  waiting for transfers between devices  92.7 us (40%)
  Pallas kernels  66.1 us (29%)
  starting transfers between devices  36.4 us (16%)
  local copies, waits for them, and re-layouts  32.1 us (14%)
    ppermute x26, waiting for transfers between devices, swap(): return lax.ppermute(value, axis, [(i, i ^ step) for i in range(count)])  75.5 us
    pallas_call x30, Pallas kernels, launch(): pl.pallas_call(body, grid_spec=pltpu.PrefetchScalarGridSpec(num_scalar_pr...  66.1 us
    unnamed x94, local copies, waits for them, and re-layouts  30.9 us
    ppermute x26, starting transfers between devices, swap(): return lax.ppermute(value, axis, [(i, i ^ step) for i in range(count)])  27 us
    ppermute x4, waiting for transfers between devices, ahead(): lax.ppermute(v, 'seq', [(s, (s + 2 * k) % n_seq) for s in range(n_seq)])  10.7 us
    ppermute x4, starting transfers between devices, ahead(): lax.ppermute(v, 'seq', [(s, (s + 2 * k) % n_seq) for s in range(n_seq)])  7.83 us
    ppermute x1, waiting for transfers between devices, diagonal(): lax.ppermute(v, ('dp', 'seq'), [(i, i ^ n_seq ^ 1) for i in range(2 * n_s...  4.8 us
  transfers between devices with their start and end apart: 32, of which 15 were waited for; matrix products, arithmetic and copies ran while one was open for 1% of the time, Pallas kernels for 28%

profile of v2, /device:TPU:0, one launch (start us, length us, event | category | flops | bytes accessed | tf_op | source)
XLA Modules:
  0.0 228.6 jit_solution(13785205304877651178)
XLA Ops:
  4.2 1.6 copy-done.26
  5.8 1.3 shard_map.102
  7.1 2.6 %collective-permute-start.2 = (bf16[128,1024]{1,0:T(8,128)(2,1)S(1)}, bf16[128,1024]{1,0:T(8,128)(2,1)S(1)}, u32[]{:S(2)}, u32[]{:S(2)}) collective-permute-start(bf16[128,1024]{1,0:T(8,128)(2,1)S(1)} %get-tuple-element.53), channel_id=1, source_target_pairs={{0,16},{16,0},{1,17},{17,1},{2,18},{18,2},{3,19},{19,3},{4,20},{20... | collective-permute-start | bytes 786440 | tf_op jit(solution)/shard_map/ppermute | solution.py:26
  9.6 1.6 collective-permute-start.3
  11.2 1.9 collective-permute-start.5
  13.1 3.7 %collective-permute-done.2.refs_1_ = bf16[128,1024]{1,0:T(8,128)(2,1)S(1)} collective-permute-done((bf16[128,1024]{1,0:T(8,128)(2,1)S(1)}, bf16[128,1024]{1,0:T(8,128)(2,1)S(1)}, u32[]{:S(2)}, u32[]{:S(2)}) %collective-permute-start.2) | collective-permute-done | bytes 262176 | tf_op jit(solution)/shard_map/ppermute | solution.py:26
  16.8 2.0 collective-permute-done.3.refs_2_
  18.8 4.8 %collective-permute-done.4.refs_3_ = bf16[128,1024]{1,0:T(8,128)(2,1)S(1)} collective-permute-done((bf16[128,1024]{1,0:T(8,128)(2,1)S(1)}, bf16[128,1024]{1,0:T(8,128)(2,1)S(1)}, u32[]{:S(2)}, u32[]{:S(2)}) %collective-permute-start.4) | collective-permute-done | bytes 262176 | tf_op jit(solution)/shard_map/ppermute | solution.py:302
  23.6 4.2 %collective-permute-done.5.refs_5_.refs_1_ = bf16[512,256]{1,0:T(8,128)(2,1)S(1)} collective-permute-done((bf16[512,256]{1,0:T(8,128)(2,1)S(1)}, bf16[512,256]{1,0:T(8,128)(2,1)S(1)}, u32[]{:S(2)}, u32[]{:S(2)}) %collective-permute-start.5) | collective-permute-done | bytes 262176 | tf_op jit(solution)/shard_map/ppermute | solution.py:26
  28.7 1.8 collective-permute-start.11
  30.6 1.5 collective-permute-start.7
  32.0 1.6 collective-permute-start.8
  34.3 3.4 %copy-done.13 = bf16[1,4096,1024]{2,1,0:T(8,128)(2,1)S(1)} copy-done((bf16[1,4096,1024]{2,1,0:T(8,128)(2,1)S(1)}, bf16[1,4096,1024]{2,1,0:T(8,128)(2,1)}, u32[]{:S(2)}) %copy-start.13) | copy-done | bytes 8388632
  38.7 9.8 %shard_map.104 = (bf16[128,4096]{1,0:T(8,128)(2,1)}, f32[128,4096]{1,0:T(8,128)S(1)}) custom-call(bf16[256,1024]{1,0:T(8,128)(2,1)S(1)} %copy-done.44, bf16[256,1024]{1,0:T(8,128)(2,1)} %collective-permute-done.refs_1_, bf16[4096,1024]{1,0:T(8,128)(2,1)S(1)} %bitcast.41, bf16[4096,1024]{1,0:T(8,128)(2,1)} %collective-permute-done.1.refs_7_.refs_3_, ...), custom_call_target="tpu_custom_call" | custom-call | flops 1 | bytes 1 | tf_op jit(solution)/shard_map/pallas_call | solution.py:36
  48.5 1.7 collective-permute-done.7.refs_2_.refs_5_
  50.8 1.3 shard_map.106
  52.1 2.3 %collective-permute-done.11.refs_0_ = bf16[512,1024]{1,0:T(8,128)(2,1)} collective-permute-done((bf16[512,1024]{1,0:T(8,128)(2,1)S(1)}, bf16[512,1024]{1,0:T(8,128)(2,1)}, u32[]{:S(2)}, u32[]{:S(2)}) %collective-permute-start.11) | collective-permute-done | bytes 1048608 | tf_op jit(solution)/shard_map/ppermute | solution.py:26
  54.4 1.3 shard_map.107.refs_4_.refs_2_
  56.3 1.8 collective-permute-start.14
  58.1 1.5 collective-permute-start.10
  59.6 3.4 %copy-done.14 = bf16[1,4096,1024]{2,1,0:T(8,128)(2,1)S(1)} copy-done((bf16[1,4096,1024]{2,1,0:T(8,128)(2,1)S(1)}, bf16[1,4096,1024]{2,1,0:T(8,128)(2,1)}, u32[]{:S(2)}) %copy-start.14) | copy-done | bytes 8388632
  63.0 9.0 %shard_map.108 = (bf16[128,4096]{1,0:T(8,128)(2,1)S(1)}, f32[128,4096]{1,0:T(8,128)S(1)}) custom-call(bf16[256,1024]{1,0:T(8,128)(2,1)S(1)} %get-tuple-element.61.refs_2_.refs_0_, bf16[256,1024]{1,0:T(8,128)(2,1)S(1)} %collective-permute-done.13.refs_1_, bf16[4096,1024]{1,0:T(8,128)(2,1)S(1)} %bitcast.42, ...), custom_call_target="tpu_custom_call" | custom-call | flops 1 | bytes 1 | tf_op jit(solution)/shard_map/pallas_call | solution.py:36
  72.0 1.6 collective-permute-start.18
  73.6 2.6 %shard_map.109.refs_3_ = bf16[1024,256]{1,0:T(8,128)(2,1)S(1)} custom-call(bf16[512,1024]{1,0:T(8,128)(2,1)S(1)} %collective-permute-done.12.refs_0_, bf16[512,1024]{1,0:T(8,128)(2,1)} %collective-permute-done.9.refs_5_.refs_1_, bf16[512,1024]{1,0:T(8,128)(2,1)S(1)} %shard_map.107.refs_4_.refs_2_, bf16[512,1024]{1,0:T(8,128)(2,1)S(1)} %get-tuple-element.56.refs_4_.refs_3_, ...), custom_call_target="tpu_custom_call" | custom-call | flops 1 | bytes 1 | tf_op jit(solution)/shard_map/pallas_call | solution.py:36
  76.3 1.5 collective-permute-start.15
  77.7 2.6 %collective-permute-start.16 = (bf16[1024,256]{1,0:T(8,128)(2,1)S(1)}, bf16[1024,256]{1,0:T(8,128)(2,1)S(1)}, u32[]{:S(2)}, u32[]{:S(2)}) collective-permute-start(bf16[1024,256]{1,0:T(8,128)(2,1)S(1)} %shard_map.109.refs_3_), channel_id=1, source_target_pairs={{0,8},{4,12},{8,0},{12,4},{1,9},{5,13},{9,1},{13,5},{2,10},{6,14},... | collective-permute-start | bytes 1572872 | tf_op jit(solution)/shard_map/ppermute | solution.py:305
  80.3 20.6 %collective-permute-done.15.refs_1_ = bf16[256,1024]{1,0:T(8,128)(2,1)S(1)} collective-permute-done((bf16[256,1024]{1,0:T(8,128)(2,1)S(1)}, bf16[256,1024]{1,0:T(8,128)(2,1)S(1)}, u32[]{:S(2)}, u32[]{:S(2)}) %collective-permute-start.15) | collective-permute-done | bytes 524320 | tf_op jit(solution)/shard_map/ppermute | solution.py:26
  100.9 2.4 %collective-permute-done.16.refs_2_ = bf16[1024,256]{1,0:T(8,128)(2,1)S(1)} collective-permute-done((bf16[1024,256]{1,0:T(8,128)(2,1)S(1)}, bf16[1024,256]{1,0:T(8,128)(2,1)S(1)}, u32[]{:S(2)}, u32[]{:S(2)}) %collective-permute-start.16) | collective-permute-done | bytes 524320 | tf_op jit(solution)/shard_map/ppermute | solution.py:305
  104.0 2.6 %shard_map.112.refs_2_ = bf16[1024,256]{1,0:T(8,128)(2,1)S(1)} custom-call(bf16[512,1024]{1,0:T(8,128)(2,1)S(1)} %collective-permute-done.12.refs_0_, bf16[512,1024]{1,0:T(8,128)(2,1)} %collective-permute-done.9.refs_5_.refs_1_, bf16[512,1024]{1,0:T(8,128)(2,1)S(1)} %shard_map.107.refs_4_.refs_2_, bf16[512,1024]{1,0:T(8,128)(2,1)S(1)} %copy-done.16, ...), custom_call_target="tpu_custom_call" | custom-call | flops 1 | bytes 1 | tf_op jit(solution)/shard_map/pallas_call | solution.py:36
  106.7 1.6 collective-permute-start.19
  108.8 2.6 %collective-permute-start.21 = (bf16[1024,256]{1,0:T(8,128)(2,1)S(1)}, bf16[1024,256]{1,0:T(8,128)(2,1)S(1)}, u32[]{:S(2)}, u32[]{:S(2)}) collective-permute-start(bf16[1024,256]{1,0:T(8,128)(2,1)S(1)} %shard_map.112.refs_2_), channel_id=1, source_target_pairs={{0,8},{4,12},{8,0},{12,4},{1,9},{5,13},{9,1},{13,5},{2,10},{6,14},... | collective-permute-start | bytes 1572872 | tf_op jit(solution)/shard_map/ppermute | solution.py:305
  111.3 22.2 %collective-permute-done.22.refs_5_.refs_6_ = bf16[1024,256]{1,0:T(8,128)(2,1)S(1)} collective-permute-done((bf16[1024,256]{1,0:T(8,128)(2,1)S(1)}, bf16[1024,256]{1,0:T(8,128)(2,1)S(1)}, u32[]{:S(2)}, u32[]{:S(2)}) %collective-permute-start.22) | collective-permute-done | bytes 524320 | tf_op jit(solution)/shard_map/ppermute | solution.py:26
  133.6 1.4 collective-permute-done.21.refs_4_.refs_2_
  135.2 1.6 collective-permute-start.6
  137.1 2.7 %shard_map.115.refs_7_ = bf16[1024,256]{1,0:T(8,128)(2,1)S(1)} custom-call(bf16[512,1024]{1,0:T(8,128)(2,1)S(1)} %collective-permute-done.12.refs_0_, bf16[512,1024]{1,0:T(8,128)(2,1)} %collective-permute-done.9.refs_5_.refs_1_, bf16[512,1024]{1,0:T(8,128)(2,1)S(1)} %shard_map.107.refs_4_.refs_2_, bf16[512,1024]{1,0:T(8,128)(2,1)S(1)} %copy-done.16, ...), custom_call_target="tpu_custom_call" | custom-call | flops 1 | bytes 1 | tf_op jit(solution)/shard_map/pallas_call | solution.py:36
  139.8 2.6 %collective-permute-start.27 = (bf16[1024,256]{1,0:T(8,128)(2,1)S(1)}, bf16[1024,256]{1,0:T(8,128)(2,1)S(1)}, u32[]{:S(2)}, u32[]{:S(2)}) collective-permute-start(bf16[1024,256]{1,0:T(8,128)(2,1)S(1)} %shard_map.115.refs_7_), channel_id=1, source_target_pairs={{0,8},{4,12},{8,0},{12,4},{1,9},{5,13},{9,1},{13,5},{2,10},{6,14},... | collective-permute-start | bytes 1572872 | tf_op jit(solution)/shard_map/ppermute | solution.py:305
  142.5 1.3 shard_map.116.refs_1_
  143.9 2.9 %shard_map.117 = (f32[1024,1024]{1,0:T(8,128)}, f32[1024,1024]{1,0:T(8,128)}, f32[1024,1024]{1,0:T(8,128)}, bf16[2,1024,1024]{2,1,0:T(8,128)(2,1)}, bf16[1024,256]{1,0:T(8,128)(2,1)}) custom-call(s32[1]{0:T(128)} %bitcast.refs_0_, f32[1024,256]{1,0:T(8,128)S(1)} %shard_map.116.refs_1_, bf16[1024,256]{1,0:T(8,128)(2,1)S(1)} %collective-permute-done.16.refs_2_, ...), custom_call_target="tpu_custom_call" | custom-call | flops 1 | bytes 1 | tf_op jit(solution)/shard_map/pallas_call | solution.py:36
  147.3 1.4 shard_map.118.refs_1_
  148.6 2.9 %shard_map.119 = (f32[1024,1024]{1,0:T(8,128)}, f32[1024,1024]{1,0:T(8,128)}, f32[1024,1024]{1,0:T(8,128)}, bf16[2,1024,1024]{2,1,0:T(8,128)(2,1)}, bf16[1024,256]{1,0:T(8,128)(2,1)}) custom-call(s32[1]{0:T(128)} %bitcast.refs_0_, f32[1024,256]{1,0:T(8,128)S(1)} %shard_map.118.refs_1_, ...), custom_call_target="tpu_custom_call", output_to_operand_aliasing={{0}: (6, {}), {1}: (7, {}), {2}: (8, {}), {3}: (9, {})} | custom-call | flops 1 | bytes 1 | tf_op jit(solution)/shard_map/pallas_call | solution.py:36
  151.6 1.5 collective-permute-start.24
  153.1 5.8 %collective-permute-done.26.refs_6_ = bf16[1024,256]{1,0:T(8,128)(2,1)S(1)} collective-permute-done((bf16[1024,256]{1,0:T(8,128)(2,1)S(1)}, bf16[1024,256]{1,0:T(8,128)(2,1)S(1)}, u32[]{:S(2)}, u32[]{:S(2)}) %collective-permute-start.26) | collective-permute-done | bytes 524320 | tf_op jit(solution)/shard_map/ppermute | solution.py:26
  158.9 6.9 %collective-permute-done.27.refs_8_.refs_2_ = bf16[1024,256]{1,0:T(8,128)(2,1)S(1)} collective-permute-done((bf16[1024,256]{1,0:T(8,128)(2,1)S(1)}, bf16[1024,256]{1,0:T(8,128)(2,1)S(1)}, u32[]{:S(2)}, u32[]{:S(2)}) %collective-permute-start.27) | collective-permute-done | bytes 524320 | tf_op jit(solution)/shard_map/ppermute | solution.py:305
  165.8 3.6 %shard_map.120.refs_7_ = bf16[1024,256]{1,0:T(8,128)(2,1)} custom-call(bf16[512,1024]{1,0:T(8,128)(2,1)S(1)} %collective-permute-done.12.refs_0_, bf16[512,1024]{1,0:T(8,128)(2,1)} %collective-permute-done.9.refs_5_.refs_1_, bf16[512,1024]{1,0:T(8,128)(2,1)S(1)} %shard_map.107.refs_4_.refs_2_, bf16[512,1024]{1,0:T(8,128)(2,1)S(1)} %copy-done.16, ...), custom_call_target="tpu_custom_call" | custom-call | flops 1 | bytes 1 | tf_op jit(solution)/shard_map/pallas_call | solution.py:36
  170.4 1.5 copy-done.11
  174.3 1.3 shard_map.121.refs_1_
  175.7 2.2 copy-done.5
  177.9 2.2 copy-done.8
  180.1 2.8 %shard_map.122 = (f32[1024,1024]{1,0:T(8,128)}, f32[1024,1024]{1,0:T(8,128)}, f32[1024,1024]{1,0:T(8,128)}, bf16[2,1024,1024]{2,1,0:T(8,128)(2,1)}, bf16[1024,256]{1,0:T(8,128)(2,1)S(1)}) custom-call(s32[1]{0:T(128)} %bitcast.refs_0_, f32[1024,256]{1,0:T(8,128)S(1)} %shard_map.121.refs_1_, ...), custom_call_target="tpu_custom_call", output_to_operand_aliasing={{0}: (6, {}), {1}: (7, {}), {2}: (8, {}), {3}: (9, {})} | custom-call | flops 1 | bytes 1 | tf_op jit(solution)/shard_map/pallas_call | solution.py:36
  183.2 1.3 shard_map.123.refs_3_.refs_1_
  184.6 2.2 shard_map.124.refs_2_
  186.8 2.0 shard_map.125.refs_2_.refs_9_
  188.9 2.2 copy-done
  191.1 1.5 shard_map.126.refs_1_
  193.7 1.6 collective-permute-start.28
  195.3 1.8 collective-permute-done.28
  197.7 1.2 copy-done.35
  198.9 4.2 %shard_map.127.refs_10_ = bf16[512,2048]{1,0:T(8,128)(2,1)} custom-call(s32[1]{0:T(128)} %bitcast.refs_0_, bf16[128,4096]{1,0:T(8,128)(2,1)S(1)} %copy-done.35, bf16[128,4096]{1,0:T(8,128)(2,1)S(1)} %copy-done.33, bf16[16,2048]{1,0:T(8,128)(2,1)S(1)} %pad.4.refs_3_), custom_call_target="tpu_custom_call" | custom-call | flops 1 | bytes 1 | tf_op jit(solution)/shard_map/pallas_call | solution.py:36
  203.1 2.2 copy-done.6
  205.3 2.2 copy-done.9
  207.5 1.6 copy-done.25
  209.1 4.0 %shard_map.128 = (f32[1024,1024]{1,0:T(8,128)}, f32[1024,1024]{1,0:T(8,128)}, f32[1024,1024]{1,0:T(8,128)}, bf16[2,1024,1024]{2,1,0:T(8,128)(2,1)}, bf16[1024,256]{1,0:T(8,128)(2,1)S(1)}) custom-call(s32[1]{0:T(128)} %bitcast.refs_0_, f32[1024,256]{1,0:T(8,128)S(1)} %copy-done.24, ...), custom_call_target="tpu_custom_call", output_to_operand_aliasing={{0}: (6, {}), {1}: (7, {}), {2}: (8, {}), {3}: (9, {})} | custom-call | flops 1 | bytes 1 | tf_op jit(solution)/shard_map/pallas_call | solution.py:36
  213.1 1.5 collective-permute-start.30
  215.4 12.3 %collective-permute-done.30.refs_1_ = bf16[1024,256]{1,0:T(8,128)(2,1)S(1)} collective-permute-done((bf16[1024,256]{1,0:T(8,128)(2,1)S(1)}, bf16[1024,256]{1,0:T(8,128)(2,1)S(1)}, u32[]{:S(2)}, u32[]{:S(2)}) %collective-permute-start.30) | collective-permute-done | bytes 524320 | tf_op jit(solution)/shard_map/ppermute | solution.py:26
  (131 shorter events, 17.0 us)
Async XLA Ops:
  0.6 27.2 %collective-permute-start.1 = (bf16[4096,1024]{1,0:T(8,128)(2,1)}, bf16[4096,1024]{1,0:T(8,128)(2,1)}, u32[]{:S(2)}, u32[]{:S(2)}) collective-permute-start(bf16[4096,1024]{1,0:T(8,128)(2,1)} %bitcast.40), channel_id=1, source_target_pairs={{0,1},{1,0},{2,3},{3,2},{4,5},{5,4},{6,7},{7,6},{8,9},{9,8},{10,11... | collective-permute-start | bytes 25165832 | tf_op jit(solution)/shard_map/ppermute | solution.py:26
  7.1 9.7 %collective-permute-start.2 = (bf16[128,1024]{1,0:T(8,128)(2,1)S(1)}, bf16[128,1024]{1,0:T(8,128)(2,1)S(1)}, u32[]{:S(2)}, u32[]{:S(2)}) collective-permute-start(bf16[128,1024]{1,0:T(8,128)(2,1)S(1)} %get-tuple-element.53), channel_id=1, source_target_pairs={{0,16},{16,0},{1,17},{17,1},{2,18},{18,2},{3,19},{19,3},{4,20},{20... | collective-permute-start | bytes 786440 | tf_op jit(solution)/shard_map/ppermute | solution.py:26
  9.6 9.1 %collective-permute-start.3 = (bf16[128,1024]{1,0:T(8,128)(2,1)S(1)}, bf16[128,1024]{1,0:T(8,128)(2,1)S(1)}, u32[]{:S(2)}, u32[]{:S(2)}) collective-permute-start(bf16[128,1024]{1,0:T(8,128)(2,1)S(1)} %get-tuple-element.54), channel_id=1, source_target_pairs={{0,4},{4,0},{8,12},{12,8},{1,5},{5,1},{9,13},{13,9},{2,6},{6,2},{1... | collective-permute-start | bytes 786440 | tf_op jit(solution)/shard_map/ppermute | solution.py:26
  11.2 12.4 %collective-permute-start.4 = (bf16[128,1024]{1,0:T(8,128)(2,1)S(1)}, bf16[128,1024]{1,0:T(8,128)(2,1)S(1)}, u32[]{:S(2)}, u32[]{:S(2)}) collective-permute-start(bf16[128,1024]{1,0:T(8,128)(2,1)S(1)} %get-tuple-element.55), channel_id=1, source_target_pairs={{0,20},{4,16},{8,28},{12,24},{16,4},{20,0},{24,12},{28,8},{1,21},{... | collective-permute-start | bytes 786440 | tf_op jit(solution)/shard_map/ppermute | solution.py:302
  11.2 16.6 %collective-permute-start.5 = (bf16[512,256]{1,0:T(8,128)(2,1)S(1)}, bf16[512,256]{1,0:T(8,128)(2,1)S(1)}, u32[]{:S(2)}, u32[]{:S(2)}) collective-permute-start(bf16[512,256]{1,0:T(8,128)(2,1)S(1)} %get-tuple-element.51.refs_2_.refs_4_), channel_id=1, source_target_pairs={{0,16},{16,0},{1,17},{17,1},{2,18},{18,2},{3,19},{19,3},{4,20},{20... | collective-permute-start | bytes 786440 | tf_op jit(solution)/shard_map/ppermute | solution.py:26
  28.7 44.8 %copy-start.15 = (bf16[512,1024]{1,0:T(8,128)(2,1)}, bf16[512,1024]{1,0:T(8,128)(2,1)S(1)}, u32[]{:S(2)}) copy-start(bf16[512,1024]{1,0:T(8,128)(2,1)S(1)} %get-tuple-element.56.refs_4_.refs_3_) | copy-start | bytes 3145732
  28.7 21.5 %collective-permute-start.9 = (bf16[512,1024]{1,0:T(8,128)(2,1)S(1)}, bf16[512,1024]{1,0:T(8,128)(2,1)}, u32[]{:S(2)}, u32[]{:S(2)}) collective-permute-start(bf16[512,1024]{1,0:T(8,128)(2,1)S(1)} %get-tuple-element.56.refs_4_.refs_3_), channel_id=1, source_target_pairs={{0,1},{1,0},{2,3},{3,2},{4,5},{5,4},{6,7},{7,6},{8,9},{9,8},{10,11... | collective-permute-start | bytes 3145736 | tf_op jit(solution)/shard_map/ppermute | solution.py:26
  28.7 25.7 %collective-permute-start.11 = (bf16[512,1024]{1,0:T(8,128)(2,1)S(1)}, bf16[512,1024]{1,0:T(8,128)(2,1)}, u32[]{:S(2)}, u32[]{:S(2)}) collective-permute-start(bf16[512,1024]{1,0:T(8,128)(2,1)S(1)} %get-tuple-element.56.refs_4_.refs_3_), channel_id=1, source_target_pairs={{0,2},{1,3},{2,0},{3,1},{4,6},{5,7},{6,4},{7,5},{8,10},{9,11},{10,... | collective-permute-start | bytes 3145736 | tf_op jit(solution)/shard_map/ppermute | solution.py:26
  30.6 19.6 %collective-permute-start.7 = (bf16[512,768]{1,0:T(8,128)(2,1)S(1)}, bf16[512,768]{1,0:T(8,128)(2,1)S(1)}, u32[]{:S(2)}, u32[]{:S(2)}) collective-permute-start(bf16[512,768]{1,0:T(8,128)(2,1)S(1)} %get-tuple-element.59.refs_0_.refs_4_), channel_id=1, source_target_pairs={{0,16},{16,0},{1,17},{17,1},{2,18},{18,2},{3,19},{19,3},{4,20},{20... | collective-permute-start | bytes 2359304 | tf_op jit(solution)/shard_map/ppermute | solution.py:26
  32.0 2.3 collective-permute-start
  32.0 18.1 %collective-permute-start.8 = (bf16[1024,256]{1,0:T(8,128)(2,1)}, bf16[1024,256]{1,0:T(8,128)(2,1)S(1)}, u32[]{:S(2)}, u32[]{:S(2)}) collective-permute-start(bf16[1024,256]{1,0:T(8,128)(2,1)} %get-tuple-element.60), channel_id=1, source_target_pairs={{0,4},{4,0},{8,12},{12,8},{1,5},{5,1},{9,13},{13,9},{2,6},{6,2},{1... | collective-permute-start | bytes 1572872 | tf_op jit(solution)/shard_map/ppermute | solution.py:26
  34.3 3.4 %copy-start.13 = (bf16[1,4096,1024]{2,1,0:T(8,128)(2,1)S(1)}, bf16[1,4096,1024]{2,1,0:T(8,128)(2,1)}, u32[]{:S(2)}) copy-start(bf16[1,4096,1024]{2,1,0:T(8,128)(2,1)} %param.8) | copy-start | bytes 25165828
  38.7 11.5 %copy-start.37 = (bf16[512,256]{1,0:T(8,128)(2,1)S(1)}, bf16[512,256]{1,0:T(8,128)(2,1)}, u32[]{:S(2)}) copy-start(bf16[512,256]{1,0:T(8,128)(2,1)} %copy-done.36) | copy-start | bytes 786436
  48.5 7.2 %copy-start.28 = (f32[128,4096]{1,0:T(8,128)}, f32[128,4096]{1,0:T(8,128)S(1)}, u32[]{:S(2)}) copy-start(f32[128,4096]{1,0:T(8,128)S(1)} %get-tuple-element.57.refs_3_.refs_0_) | copy-start | bytes 6291460
  48.5 2.3 %copy-start.27 = (bf16[1,512,2048]{2,1,0:T(8,128)(2,1)S(1)}, bf16[1,512,2048]{2,1,0:T(8,128)(2,1)}, u32[]{:S(2)}) copy-start(bf16[1,512,2048]{2,1,0:T(8,128)(2,1)} %param.6) | copy-start | bytes 6291460
  55.7 17.8 %collective-permute-start.12 = (bf16[512,1024]{1,0:T(8,128)(2,1)S(1)}, bf16[512,1024]{1,0:T(8,128)(2,1)S(1)}, u32[]{:S(2)}, u32[]{:S(2)}) collective-permute-start(bf16[512,1024]{1,0:T(8,128)(2,1)S(1)} %shard_map.107.refs_4_.refs_2_), channel_id=1, source_target_pairs={{0,1},{1,0},{2,3},{3,2},{4,5},{5,4},{6,7},{7,6},{8,9},{9,8},{10,11... | collective-permute-start | bytes 3145736 | tf_op jit(solution)/shard_map/ppermute | solution.py:26
  55.8 3.8 %collective-permute-start.13 = (bf16[256,1024]{1,0:T(8,128)(2,1)S(1)}, bf16[256,1024]{1,0:T(8,128)(2,1)S(1)}, u32[]{:S(2)}, u32[]{:S(2)}) collective-permute-start(bf16[256,1024]{1,0:T(8,128)(2,1)S(1)} %get-tuple-element.65), channel_id=1, source_target_pairs={{0,1},{1,0},{2,3},{3,2},{4,5},{5,4},{6,7},{7,6},{8,9},{9,8},{10,11... | collective-permute-start | bytes 1572872 | tf_op jit(solution)/shard_map/ppermute | solution.py:26
  56.3 17.2 %collective-permute-start.14 = (bf16[1024,256]{1,0:T(8,128)(2,1)S(1)}, bf16[1024,256]{1,0:T(8,128)(2,1)S(1)}, u32[]{:S(2)}, u32[]{:S(2)}) collective-permute-start(bf16[1024,256]{1,0:T(8,128)(2,1)S(1)} %get-tuple-element.67), channel_id=1, source_target_pairs={{0,4},{4,0},{8,12},{12,8},{1,5},{5,1},{9,13},{13,9},{2,6},{6,2},{1... | collective-permute-start | bytes 1572872 | tf_op jit(solution)/shard_map/ppermute | solution.py:26
  58.1 18.1 %collective-permute-start.10 = (bf16[256,1024]{1,0:T(8,128)(2,1)S(1)}, bf16[256,1024]{1,0:T(8,128)(2,1)S(1)}, u32[]{:S(2)}, u32[]{:S(2)}) collective-permute-start(bf16[256,1024]{1,0:T(8,128)(2,1)S(1)} %get-tuple-element.64), channel_id=1, source_target_pairs={{0,16},{16,0},{1,17},{17,1},{2,18},{18,2},{3,19},{19,3},{4,20},{20... | collective-permute-start | bytes 1572872 | tf_op jit(solution)/shard_map/ppermute | solution.py:26
  59.6 3.4 %copy-start.14 = (bf16[1,4096,1024]{2,1,0:T(8,128)(2,1)S(1)}, bf16[1,4096,1024]{2,1,0:T(8,128)(2,1)}, u32[]{:S(2)}) copy-start(bf16[1,4096,1024]{2,1,0:T(8,128)(2,1)} %param.8) | copy-start | bytes 25165828
  72.0 34.6 %collective-permute-start.18 = (bf16[128,4096]{1,0:T(8,128)(2,1)S(1)}, bf16[128,4096]{1,0:T(8,128)(2,1)S(1)}, u32[]{:S(2)}, u32[]{:S(2)}) collective-permute-start(bf16[128,4096]{1,0:T(8,128)(2,1)S(1)} %get-tuple-element.70), channel_id=1, source_target_pairs={{0,2},{1,3},{2,0},{3,1},{4,6},{5,7},{6,4},{7,5},{8,10},{9,11},{10,... | collective-permute-start | bytes 3145736 | tf_op jit(solution)/shard_map/ppermute | solution.py:26
  76.2 27.8 %copy-start.16 = (bf16[512,1024]{1,0:T(8,128)(2,1)S(1)}, bf16[512,1024]{1,0:T(8,128)(2,1)}, u32[]{:S(2)}) copy-start(bf16[512,1024]{1,0:T(8,128)(2,1)} %copy-done.15) | copy-start | bytes 3145732
  76.3 24.7 %collective-permute-start.15 = (bf16[256,1024]{1,0:T(8,128)(2,1)S(1)}, bf16[256,1024]{1,0:T(8,128)(2,1)S(1)}, u32[]{:S(2)}, u32[]{:S(2)}) collective-permute-start(bf16[256,1024]{1,0:T(8,128)(2,1)S(1)} %get-tuple-element.69), channel_id=1, source_target_pairs={{0,4},{4,0},{8,12},{12,8},{1,5},{5,1},{9,13},{13,9},{2,6},{6,2},{1... | collective-permute-start | bytes 1572872 | tf_op jit(solution)/shard_map/ppermute | solution.py:26
  77.7 25.6 %collective-permute-start.16 = (bf16[1024,256]{1,0:T(8,128)(2,1)S(1)}, bf16[1024,256]{1,0:T(8,128)(2,1)S(1)}, u32[]{:S(2)}, u32[]{:S(2)}) collective-permute-start(bf16[1024,256]{1,0:T(8,128)(2,1)S(1)} %shard_map.109.refs_3_), channel_id=1, source_target_pairs={{0,8},{4,12},{8,0},{12,4},{1,9},{5,13},{9,1},{13,5},{2,10},{6,14},... | collective-permute-start | bytes 1572872 | tf_op jit(solution)/shard_map/ppermute | solution.py:305
  103.4 31.6 %collective-permute-start.17 = (bf16[512,1024]{1,0:T(8,128)(2,1)S(1)}, bf16[512,1024]{1,0:T(8,128)(2,1)S(1)}, u32[]{:S(2)}, u32[]{:S(2)}) collective-permute-start(bf16[512,1024]{1,0:T(8,128)(2,1)S(1)} %shard_map.111.refs_7_.refs_3_), channel_id=1, source_target_pairs={{0,2},{1,3},{2,0},{3,1},{4,6},{5,7},{6,4},{7,5},{8,10},{9,11},{10,... | collective-permute-start | bytes 3145736 | tf_op jit(solution)/shard_map/ppermute | solution.py:26
  106.7 28.3 %collective-permute-start.19 = (bf16[128,4096]{1,0:T(8,128)(2,1)S(1)}, bf16[128,4096]{1,0:T(8,128)(2,1)S(1)}, u32[]{:S(2)}, u32[]{:S(2)}) collective-permute-start(bf16[128,4096]{1,0:T(8,128)(2,1)S(1)} %shard_map.113.refs_1_), channel_id=1, source_target_pairs={{0,16},{16,0},{1,17},{17,1},{2,18},{18,2},{3,19},{19,3},{4,20},{20... | collective-permute-start | bytes 3145736 | tf_op jit(solution)/shard_map/ppermute | solution.py:26
  108.3 26.7 %collective-permute-start.20 = (bf16[512,1024]{1,0:T(8,128)(2,1)S(1)}, bf16[512,1024]{1,0:T(8,128)(2,1)S(1)}, u32[]{:S(2)}, u32[]{:S(2)}) collective-permute-start(bf16[512,1024]{1,0:T(8,128)(2,1)S(1)} %shard_map.111.refs_7_.refs_3_), channel_id=1, source_target_pairs={{0,1},{1,0},{2,3},{3,2},{4,5},{5,4},{6,7},{7,6},{8,9},{9,8},{10,11... | collective-permute-start | bytes 3145736 | tf_op jit(solution)/shard_map/ppermute | solution.py:26
  108.3 25.3 %collective-permute-start.22 = (bf16[1024,256]{1,0:T(8,128)(2,1)S(1)}, bf16[1024,256]{1,0:T(8,128)(2,1)S(1)}, u32[]{:S(2)}, u32[]{:S(2)}) collective-permute-start(bf16[1024,256]{1,0:T(8,128)(2,1)S(1)} %get-tuple-element.71), channel_id=1, source_target_pairs={{0,4},{4,0},{8,12},{12,8},{1,5},{5,1},{9,13},{13,9},{2,6},{6,2},{1... | collective-permute-start | bytes 1572872 | tf_op jit(solution)/shard_map/ppermute | solution.py:26
  108.8 26.2 %collective-permute-start.21 = (bf16[1024,256]{1,0:T(8,128)(2,1)S(1)}, bf16[1024,256]{1,0:T(8,128)(2,1)S(1)}, u32[]{:S(2)}, u32[]{:S(2)}) collective-permute-start(bf16[1024,256]{1,0:T(8,128)(2,1)S(1)} %shard_map.112.refs_2_), channel_id=1, source_target_pairs={{0,8},{4,12},{8,0},{12,4},{1,9},{5,13},{9,1},{13,5},{2,10},{6,14},... | collective-permute-start | bytes 1572872 | tf_op jit(solution)/shard_map/ppermute | solution.py:305
  133.6 6.2 %copy-start.30 = (bf16[1024,256]{1,0:T(8,128)(2,1)}, bf16[1024,256]{1,0:T(8,128)(2,1)S(1)}, u32[]{:S(2)}) copy-start(bf16[1024,256]{1,0:T(8,128)(2,1)S(1)} %collective-permute-done.22.refs_5_.refs_6_) | copy-start | bytes 1572868
  135.0 12.3 %copy-start.17 = (bf16[512,1024]{1,0:T(8,128)(2,1)}, bf16[512,1024]{1,0:T(8,128)(2,1)S(1)}, u32[]{:S(2)}) copy-start(bf16[512,1024]{1,0:T(8,128)(2,1)S(1)} %collective-permute-done.20.refs_3_.refs_1_) | copy-start | bytes 3145732
  135.1 12.2 %copy-start.10 = (bf16[512,1024]{1,0:T(8,128)(2,1)}, bf16[512,1024]{1,0:T(8,128)(2,1)S(1)}, u32[]{:S(2)}) copy-start(bf16[512,1024]{1,0:T(8,128)(2,1)S(1)} %shard_map.114.refs_7_.refs_2_) | copy-start | bytes 3145732
  135.1 7.4 %collective-permute-start.23 = (bf16[512,1024]{1,0:T(8,128)(2,1)S(1)}, bf16[512,1024]{1,0:T(8,128)(2,1)S(1)}, u32[]{:S(2)}, u32[]{:S(2)}) collective-permute-start(bf16[512,1024]{1,0:T(8,128)(2,1)S(1)} %shard_map.114.refs_7_.refs_2_), channel_id=1, source_target_pairs={{0,1},{1,0},{2,3},{3,2},{4,5},{5,4},{6,7},{7,6},{8,9},{9,8},{10,11... | collective-permute-start | bytes 3145736 | tf_op jit(solution)/shard_map/ppermute | solution.py:26
  135.2 53.7 %collective-permute-start.6 = (bf16[128,4096]{1,0:T(8,128)(2,1)}, bf16[128,4096]{1,0:T(8,128)(2,1)}, u32[]{:S(2)}, u32[]{:S(2)}) collective-permute-start(bf16[128,4096]{1,0:T(8,128)(2,1)} %get-tuple-element.58), channel_id=1, source_target_pairs={{0,2},{1,3},{2,0},{3,1},{4,6},{5,7},{6,4},{7,5},{8,10},{9,11},{10,... | collective-permute-start | bytes 3145736 | tf_op jit(solution)/shard_map/ppermute | solution.py:26
  136.8 22.1 %collective-permute-start.26 = (bf16[1024,256]{1,0:T(8,128)(2,1)S(1)}, bf16[1024,256]{1,0:T(8,128)(2,1)S(1)}, u32[]{:S(2)}, u32[]{:S(2)}) collective-permute-start(bf16[1024,256]{1,0:T(8,128)(2,1)S(1)} %get-tuple-element.78), channel_id=1, source_target_pairs={{0,4},{4,0},{8,12},{12,8},{1,5},{5,1},{9,13},{13,9},{2,6},{6,2},{1... | collective-permute-start | bytes 1572872 | tf_op jit(solution)/shard_map/ppermute | solution.py:26
  137.1 6.8 %copy-start.4 = (f32[1,1024,1024]{2,1,0:T(8,128)S(1)}, f32[1,1024,1024]{2,1,0:T(8,128)}, u32[]{:S(2)}) copy-start(f32[1,1024,1024]{2,1,0:T(8,128)} %param.10) | copy-start | bytes 12582916
  137.1 6.8 %copy-start.7 = (f32[1,1024,1024]{2,1,0:T(8,128)S(1)}, f32[1,1024,1024]{2,1,0:T(8,128)}, u32[]{:S(2)}) copy-start(f32[1,1024,1024]{2,1,0:T(8,128)} %param.11) | copy-start | bytes 12582916
  139.8 4.0 %copy-start.1 = (f32[1,1024,1024]{2,1,0:T(8,128)S(1)}, f32[1,1024,1024]{2,1,0:T(8,128)}, u32[]{:S(2)}) copy-start(f32[1,1024,1024]{2,1,0:T(8,128)} %param.9) | copy-start | bytes 12582916
  139.8 26.0 %collective-permute-start.27 = (bf16[1024,256]{1,0:T(8,128)(2,1)S(1)}, bf16[1024,256]{1,0:T(8,128)(2,1)S(1)}, u32[]{:S(2)}, u32[]{:S(2)}) collective-permute-start(bf16[1024,256]{1,0:T(8,128)(2,1)S(1)} %shard_map.115.refs_7_), channel_id=1, source_target_pairs={{0,8},{4,12},{8,0},{12,4},{1,9},{5,13},{9,1},{13,5},{2,10},{6,14},... | collective-permute-start | bytes 1572872 | tf_op jit(solution)/shard_map/ppermute | solution.py:305
  142.5 4.8 %copy-start.20 = (bf16[512,1024]{1,0:T(8,128)(2,1)}, bf16[512,1024]{1,0:T(8,128)(2,1)S(1)}, u32[]{:S(2)}) copy-start(bf16[512,1024]{1,0:T(8,128)(2,1)S(1)} %collective-permute-done.23.refs_0_) | copy-start | bytes 3145732
  146.7 37.8 %collective-permute-start.25 = (bf16[1024,256]{1,0:T(8,128)(2,1)}, bf16[1024,256]{1,0:T(8,128)(2,1)}, u32[]{:S(2)}, u32[]{:S(2)}) collective-permute-start(bf16[1024,256]{1,0:T(8,128)(2,1)} %get-tuple-element.72.refs_7_), channel_id=1, source_target_pairs={{0,16},{16,0},{1,17},{17,1},{2,18},{18,2},{3,19},{19,3},{4,20},{20... | collective-permute-start | bytes 1572872 | tf_op jit(solution)/shard_map/ppermute | solution.py:26
  151.6 18.8 %copy-start.31 = (bf16[1024,256]{1,0:T(8,128)(2,1)S(1)}, bf16[1024,256]{1,0:T(8,128)(2,1)}, u32[]{:S(2)}) copy-start(bf16[1024,256]{1,0:T(8,128)(2,1)} %copy-done.30) | copy-start | bytes 1572868
  151.6 35.3 %collective-permute-start.24 = (bf16[1024,256]{1,0:T(8,128)(2,1)}, bf16[1024,256]{1,0:T(8,128)(2,1)}, u32[]{:S(2)}, u32[]{:S(2)}) collective-permute-start(bf16[1024,256]{1,0:T(8,128)(2,1)} %get-tuple-element.77.refs_7_), channel_id=1, source_target_pairs={{0,16},{16,0},{1,17},{17,1},{2,18},{18,2},{3,19},{19,3},{4,20},{20... | collective-permute-start | bytes 1572872 | tf_op jit(solution)/shard_map/ppermute | solution.py:26
  158.9 10.5 %copy-start.40 = (bf16[1024,256]{1,0:T(8,128)(2,1)}, bf16[1024,256]{1,0:T(8,128)(2,1)S(1)}, u32[]{:S(2)}) copy-start(bf16[1024,256]{1,0:T(8,128)(2,1)S(1)} %collective-permute-done.26.refs_6_) | copy-start | bytes 1572868
  165.8 3.6 %copy-start.38 = (bf16[1024,256]{1,0:T(8,128)(2,1)}, bf16[1024,256]{1,0:T(8,128)(2,1)S(1)}, u32[]{:S(2)}) copy-start(bf16[1024,256]{1,0:T(8,128)(2,1)S(1)} %collective-permute-done.27.refs_8_.refs_2_) | copy-start | bytes 1572868
  169.4 33.7 %collective-permute-start.29 = (bf16[1024,256]{1,0:T(8,128)(2,1)}, bf16[1024,256]{1,0:T(8,128)(2,1)}, u32[]{:S(2)}, u32[]{:S(2)}) collective-permute-start(bf16[1024,256]{1,0:T(8,128)(2,1)} %shard_map.120.refs_7_), channel_id=1, source_target_pairs={{0,8},{4,12},{8,0},{12,4},{1,9},{5,13},{9,1},{13,5},{2,10},{6,14},... | collective-permute-start | bytes 1572872 | tf_op jit(solution)/shard_map/ppermute | solution.py:305
  169.4 6.3 %copy-start.2 = (f32[1,1024,1024]{2,1,0:T(8,128)S(1)}, f32[1,1024,1024]{2,1,0:T(8,128)}, u32[]{:S(2)}) copy-start(f32[1,1024,1024]{2,1,0:T(8,128)} %param.9) | copy-start | bytes 12582916
  175.7 2.2 copy-start.5
  177.9 2.2 copy-start.8
  180.1 2.8 %copy-start.12 = (bf16[512,1024]{1,0:T(8,128)(2,1)S(1)}, bf16[512,1024]{1,0:T(8,128)(2,1)}, u32[]{:S(2)}) copy-start(bf16[512,1024]{1,0:T(8,128)(2,1)} %copy-done.10) | copy-start | bytes 3145732
  180.1 2.8 %copy-start.19 = (bf16[512,1024]{1,0:T(8,128)(2,1)S(1)}, bf16[512,1024]{1,0:T(8,128)(2,1)}, u32[]{:S(2)}) copy-start(bf16[512,1024]{1,0:T(8,128)(2,1)} %copy-done.17) | copy-start | bytes 3145732
  180.1 2.8 %copy-start.22 = (bf16[512,1024]{1,0:T(8,128)(2,1)S(1)}, bf16[512,1024]{1,0:T(8,128)(2,1)}, u32[]{:S(2)}) copy-start(bf16[512,1024]{1,0:T(8,128)(2,1)} %copy-done.20) | copy-start | bytes 3145732
  180.1 3.1 %copy-start.41 = (bf16[1024,256]{1,0:T(8,128)(2,1)S(1)}, bf16[1024,256]{1,0:T(8,128)(2,1)}, u32[]{:S(2)}) copy-start(bf16[1024,256]{1,0:T(8,128)(2,1)} %copy-done.40) | copy-start | bytes 1572868
  182.9 3.9 %copy-start.45 = (bf16[1024,256]{1,0:T(8,128)(2,1)}, bf16[1024,256]{1,0:T(8,128)(2,1)S(1)}, u32[]{:S(2)}) copy-start(bf16[1024,256]{1,0:T(8,128)(2,1)S(1)} %get-tuple-element.84.refs_7_) | copy-start | bytes 1572868
  184.6 2.3 copy-start.23
  188.9 2.2 copy-start
  191.1 6.0 %copy-start.46 = (bf16[1024,256]{1,0:T(8,128)(2,1)S(1)}, bf16[1024,256]{1,0:T(8,128)(2,1)}, u32[]{:S(2)}) copy-start(bf16[1024,256]{1,0:T(8,128)(2,1)} %copy-done.45) | copy-start | bytes 1572868
  191.1 6.6 %copy-start.33 = (bf16[128,4096]{1,0:T(8,128)(2,1)S(1)}, bf16[128,4096]{1,0:T(8,128)(2,1)}, u32[]{:S(2)}) copy-start(bf16[128,4096]{1,0:T(8,128)(2,1)} %copy-done.32) | copy-start | bytes 3145732
  191.1 12.0 %copy-start.24 = (f32[1024,256]{1,0:T(8,128)S(1)}, f32[1024,256]{1,0:T(8,128)}, u32[]{:S(2)}) copy-start(f32[1024,256]{1,0:T(8,128)} %copy-done.23) | copy-start | bytes 3145732
  193.7 9.4 %copy-start.3 = (f32[1,1024,1024]{2,1,0:T(8,128)S(1)}, f32[1,1024,1024]{2,1,0:T(8,128)}, u32[]{:S(2)}) copy-start(f32[1,1024,1024]{2,1,0:T(8,128)} %param.9) | copy-start | bytes 12582916
  193.7 3.3 %collective-permute-start.28 = (bf16[3,2048]{1,0:T(4,128)(2,1)S(1)}, bf16[3,2048]{1,0:T(4,128)(2,1)S(1)}, u32[]{:S(2)}, u32[]{:S(2)}) collective-permute-start(bf16[3,2048]{1,0:T(4,128)(2,1)S(1)} %reshape.81), channel_id=1, source_target_pairs={{1,0},{2,1},{3,2},{4,3},{5,4},{6,5},{7,6},{8,7},{9,8},{10,9},{11,1... | collective-permute-start | bytes 36872 | tf_op jit(solution)/shard_map/ppermute | solution.py:415
  197.1 17.5 %collective-permute-start.31 = (bf16[1024,256]{1,0:T(8,128)(2,1)S(1)}, bf16[1024,256]{1,0:T(8,128)(2,1)S(1)}, u32[]{:S(2)}, u32[]{:S(2)}) collective-permute-start(bf16[1024,256]{1,0:T(8,128)(2,1)S(1)} %copy-done.46), channel_id=1, source_target_pairs={{0,16},{16,0},{1,17},{17,1},{2,18},{18,2},{3,19},{19,3},{4,20},{20... | collective-permute-start | bytes 1572872 | tf_op jit(solution)/shard_map/ppermute | solution.py:26
  203.1 2.2 copy-start.6
  213.1 14.6 %collective-permute-start.30 = (bf16[1024,256]{1,0:T(8,128)(2,1)S(1)}, bf16[1024,256]{1,0:T(8,128)(2,1)S(1)}, u32[]{:S(2)}, u32[]{:S(2)}) collective-permute-start(bf16[1024,256]{1,0:T(8,128)(2,1)S(1)} %get-tuple-element.91.refs_3_), channel_id=1, source_target_pairs={{0,16},{16,0},{1,17},{17,1},{2,18},{18,2},{3,19},{19,3},{4,20},{20... | collective-permute-start | bytes 1572872 | tf_op jit(solution)/shard_map/ppermute | solution.py:26
  (15 other events, 20.6 us)

commit v3 on v2

--- a/solution.py
+++ b/solution.py
@@ -26,7 +26,7 @@
     return lax.ppermute(value, axis, [(i, i ^ step) for i in range(count)])
 
 
-def launch(kernel, values, out, grid=(), in_specs=None, out_specs=None, scalars=(), aliases=None, after=(), limit=14):
+def launch(kernel, values, out, grid=(), in_specs=None, out_specs=None, scalars=(), aliases=None, after=(), limit=14, span=0):
     whole = pl.BlockSpec(memory_space=pltpu.VMEM)
     taken = len(scalars) + len(values)
 
@@ -45,8 +45,16 @@
         out_shape=[jax.ShapeDtypeStruct(shape, dtype) for shape, dtype in out],
         input_output_aliases=aliases or {},
         compiler_params=pltpu.CompilerParams(vmem_limit_bytes=limit * 2**20),
-        cost_estimate=pl.CostEstimate(flops=1, bytes_accessed=1, transcendentals=0),
+        cost_estimate=pl.CostEstimate(flops=1 + span * 1200000000, bytes_accessed=1 + span * 3500000, transcendentals=0),
     )(*scalars, *values, *after)
+
+
+def mark_kernel(out_ref):
+    out_ref[...] = jnp.zeros_like(out_ref)
+
+
+def mark(span, *after):
+    return launch(mark_kernel, [], [((8, 128), f32)], after=after, span=span)[0]
 
 
 def sort_kernel(order, m_ref, grad_ref, sent_ref, kept_ref, *piece_refs):
@@ -105,44 +113,60 @@
     return launch(functools.partial(stack_kernel, picks), values, out, after=after)
 
 
-def act_kernel(a_ref, b_ref, w_ref, pair_ref, send_ref, rest_ref):
-    count = send_ref.shape[0]
+def act_kernel(a_ref, b_ref, w_ref, pair_ref, *out_refs):
+    *send_refs, rest_ref = out_refs
+    count = rest_ref.shape[0]
     product = 0.0
     for rows, part in ((a_ref, w_ref), (b_ref, pair_ref)):
         product += lax.dot_general(
             rows[...], part[...], (((1,), (1,)), ((), ())), preferred_element_type=f32
         )
-    send_ref[...] = product[:count].astype(bf16)
     rest_ref[...] = product[count:]
+    half = pl.num_programs(0) // 2
+    for i, ref in enumerate(send_refs):
+
+        @pl.when(pl.program_id(0) // half == i)
+        def _():
+            ref[...] = product[:count].astype(bf16)
 
 
 def act_products(rows, weights, after=()):
     count = rows[0].shape[0] // 2
     wide, depth = weights[0].shape
     step = 512
+    half = wide // step // 2
     return launch(
         act_kernel,
         [*rows, *weights],
-        [((count, wide), bf16), ((count, wide), f32)],
+        [((count, wide // 2), bf16)] * 2 + [((count, wide), f32)],
         grid=(wide // step,),
         in_specs=[pl.BlockSpec(v.shape, lambda i: (0, 0)) for v in rows]
         + [pl.BlockSpec((step, depth), lambda i: (i, 0))] * 2,
-        out_specs=[pl.BlockSpec((count, step), lambda i: (0, i))] * 2,
+        out_specs=[
+            pl.BlockSpec((count, step), lambda i: (0, jnp.minimum(i, half - 1))),
+            pl.BlockSpec((count, step), lambda i: (0, jnp.maximum(i - half, 0))),
+            pl.BlockSpec((count, step), lambda i: (0, i)),
+        ],
         after=after,
     )
 
 
-def last_kernel(keep_ref, came_ref, out_ref):
-    out_ref[...] = (keep_ref[...] + came_ref[...].astype(f32)).astype(bf16)
+def last_kernel(keep_ref, *refs):
+    *came_refs, out_ref = refs
+    at = 0
+    for ref in came_refs:
+        part = slice(at, at + ref.shape[1])
+        out_ref[:, part] = (keep_ref[:, part] + ref[...].astype(f32)).astype(bf16)
+        at += ref.shape[1]
 
 
 def last_sum(keep, came, after=()):
-    return launch(last_kernel, [keep, came], [(keep.shape, bf16)], after=after)[0]
+    return launch(last_kernel, [keep, *came], [(keep.shape, bf16)], after=after)[0]
 
 
 def against_kernel(groups, places, *refs):
     x_refs, g_refs, out_ref = refs[: sum(groups)], refs[sum(groups) : -1], refs[-1]
-    count = x_refs[0].shape[0] * groups[0] // len(places)
+    count = sum(ref.shape[0] for ref in x_refs[: groups[0]]) // len(places)
     total, first = None, 0
     for j, size in enumerate(groups):
         x = jnp.concatenate([ref[...] for ref in x_refs[first : first + size]], axis=0)
@@ -209,24 +233,27 @@
     )
 
 
-def place_kernel(x_ref, other_ref, held_ref, out_ref):
-    out_ref[0] = other_ref[...]
-
-
-def place_other(x, other, held, column, after=()):
-    rows, cols = other.shape
+def place_kernel(x_ref, *refs):
+    *other_refs, held_ref, out_ref = refs
+    for i, ref in enumerate(other_refs):
+
+        @pl.when(pl.program_id(0) == i)
+        def _():
+            out_ref[0] = ref[...]
+
+
+def place_others(x, others, held, after=()):
+    rows, cols = others[0].shape
     return launch(
         place_kernel,
-        [other, held],
+        [*others, held],
         [(held.shape, held.dtype)],
-        grid=(1,),
-        in_specs=[
-            pl.BlockSpec((rows, cols), lambda r, x: (0, 0)),
-            pl.BlockSpec(memory_space=pl.ANY),
-        ],
-        out_specs=[pl.BlockSpec((1, rows, cols), lambda r, x: (1 - x[0], 0, column))],
+        grid=(len(others),),
+        in_specs=[pl.BlockSpec((rows, cols), lambda r, x: (0, 0))] * len(others)
+        + [pl.BlockSpec(memory_space=pl.ANY)],
+        out_specs=[pl.BlockSpec((1, rows, cols), lambda r, x: (1 - x[0], 0, r))],
         scalars=(x.reshape(1),),
-        aliases={2: 0},
+        aliases={1 + len(others): 0},
         after=after,
     )[0]
 
@@ -266,6 +293,9 @@
     )[0]
 
 
+SPANS = (3, 9, 4, 4)
+
+
 def per_device(shortening_input, coarse_grad, weight_copy, master, moment, second):
     fine = shortening_input[0]
     grad = coarse_grad[0]
@@ -319,24 +349,23 @@
         own, to_seq, to_dp, to_both = cut((h + k) % far, (1, 1, 1, 1), [last])
         first[k] = own, swap(to_dp, "dp", 1), swap(to_seq, "seq", 1), diagonal(to_both)
         last = own
-    for k, v in first.items():
-        mine, pack = stack(
-            [[(i, 0, one) for i in range(4)], [(4, 0, coarse_rows), (5, 0, coarse_rows)]],
-            *v, g0, g0_dp, after=[last, pair_weights],
-        )
-        first[k] = mine, swap(mine, "mp", 1), swap(mine, "mp", 2)
-        last = mine
+    for k, (own, dp, seq, both) in first.items():
+        (three,) = stack([[(i, 0, one) for i in range(3)]], own, dp, seq, after=[last])
+        first[k] = three, both, swap(three, "mp", 2), swap(both, "mp", 2), swap(three, "mp", 1)
+        last = three
+    (pack,) = stack(
+        [[(0, 0, coarse_rows), (1, 0, coarse_rows)]], g0, g0_dp, after=[last, pair_weights] + [v[1] for v in first.values()]
+    )
     packs = [swap(pack, "seq", 1)]
+    first = {k: (*v, swap(v[1], "mp", 1)) for k, v in first.items()}
+    last = pack
     later_dp = swap(g_later, "dp", 1)
     own_pair = swap(pair_send, "mp", 1)
-    own_send, own_rest = act_products([own_rows, own_pair], [weights, pair_weights], [last])
-    own_came = swap(own_send, "mp", 2)
-    last = own_rest
     other_send, other_rows, *later_packs = launch(
         halves_kernel,
         [g_later, g0_dp, later_dp],
         [((2 * one, width), bf16)] * 2 + [((2 * coarse_rows, cols), bf16)] * (PIECES - 1),
-        after=[last, packs[0]] + [v[1] for v in first.values()],
+        after=[last, packs[0]] + [w for v in first.values() for w in v[4:]],
     )
     packs += [swap(v, "seq", 1) for v in later_packs]
     other_pair = swap(other_send, "mp", 1)
@@ -344,13 +373,14 @@
     x_dp = swap(to_dp, "dp", 1)
     last = own
     x_far = {}
-    for k, (mine, beside, across) in first.items():
-        (across,) = stack([[(0, 0, 4 * one)]], across, after=[last])
-        x_far[k] = [swap(across, "mp", 1)], [beside], [across], [mine]
-        last = across
-    other_send, other_rest = act_products([other_rows, other_pair], [weights, pair_weights], [last])
-    other_came = swap(other_send, "mp", 2)
-    last = other_rest
+    for k, (three, both, *came) in first.items():
+        across, across_both, beside, beside_both = came
+        x_far[k] = (
+            [swap(across, "mp", 1), swap(across_both, "mp", 1)],
+            [beside, beside_both],
+            [across, across_both],
+            [three, both],
+        )
 
     def gradients(i):
         if i == 0:
@@ -367,20 +397,28 @@
         return (came[0] if far == 2 else sum(v.astype(f32) for v in came)), sent
 
     sums = {}
-    sums[0], last = far_sums(0, [last, packs[1]])
+    sums[0], last = far_sums(0, [last])
+    *other_send, other_rest = act_products([other_rows, other_pair], [weights, pair_weights], [last])
+    other_came = [swap(v, "mp", 2) for v in other_send]
+    last = other_rest
+
+    sums[1], last = far_sums(1, [last])
     near, to_seq = stack(
         [[(0, 0, one), (2, 0, one)], [(1, 0, one), (2, one, one)]], own, to_seq, x_dp, after=[last]
     )
     x_seq = swap(to_seq, "seq", 1)
-    (mine,) = stack([[(0, 0, 2 * one), (1, 0, 2 * one)]], near, x_seq, after=[sums[0]])
+    last = mark(SPANS[0], near, sums[0])
+    (mine,) = stack([[(0, 0, 2 * one), (1, 0, 2 * one)]], near, x_seq, after=[last])
     across, beside = swap(mine, "mp", 2), swap(mine, "mp", 1)
-    sums[1], last = far_sums(1, [mine])
-    act_other = last_sum(other_rest, other_came, after=[last])
+    act_other = last_sum(other_rest, other_came, after=[mine])
     act_other_came = swap(act_other, "dp", 1)
-    (across,) = stack([[(0, 0, 4 * one)]], across, after=[act_other, act_other_came, beside, sums[1], packs[2]])
+    *own_send, own_rest = act_products([own_rows, own_pair], [weights, pair_weights], [act_other])
+    own_came = [swap(v, "mp", 2) for v in own_send]
+    last = mark(SPANS[1], own_rest, sums[1], packs[2])
+    (across,) = stack([[(0, 0, 4 * one)]], across, after=[last, act_other_came, beside])
+    sums[2], last = far_sums(2, [across])
     both = swap(across, "mp", 1)
     x_near = [both], [beside], [across], [mine]
-    sums[2], last = far_sums(2, [across])
     scale = 1.0 / math.sqrt(lax.axis_size("dp") * coarse_rows * n_seq)
     held, others = None, []
 
@@ -395,16 +433,14 @@
 
     last = update(0, nearby(0, [last]), [])
     last = update(1, nearby(1, [last]), [])
-    sums[3], last = far_sums(3, [last, sums[2]])
-    last = update(2, nearby(2, [last]), [])
-    gradient = nearby(3, [last])
-
-    def put(i, after):
-        held[3] = place_other(x, others[i], held[3], i, after=after)
-
-    put(0, [gradient])
-    put(1, [])
-    act_own = last_sum(own_rest, own_came, after=[held[3]])
+    gradient = nearby(2, [last])
+    sums[3], last = far_sums(3, [gradient])
+    fourth = nearby(3, [last])
+    last = mark(SPANS[2], fourth, sums[2])
+    last = mark(0, last, *others)
+    last = update(2, gradient, [last])
+
+    act_own = last_sum(own_rest, own_came, after=[last])
     head = jnp.where(
         x == 0,
         jnp.concatenate([act_own[:1], act_other_came[:1]], axis=1),
@@ -415,9 +451,10 @@
     later = lax.ppermute(head, ("seq", "mp"), [(s, s - 1) for s in range(1, count)])
     later = jnp.pad(later, ((0, 16 - (SHORT - 1)), (0, 0)))
     act_grad = merge(x, act_own, act_other_came, later)
-    last = update(3, gradient, [act_grad])
-    put(2, [last])
-    put(3, [])
+    last = mark(SPANS[3], act_grad, sums[3])
+    last = mark(0, last, others[2])
+    update(3, fourth, [last])
+    held[3] = place_others(x, others, held[3])
     new_master, new_moment, new_second, new_weight = held
     return (act_grad[None], new_master[None], new_moment[None], new_second[None], new_weight)
 

time: 230 us -> 202 us (0.88)
  local copies, waits for them, and re-layouts: 32.1 us -> 14.5 us
  waiting for transfers between devices: 92.7 us -> 86 us
  Pallas kernels: 66.1 us -> 63.5 us
    unnamed x94 -> x62, local copies, waits for them, and re-layouts: 30.9 us -> 14.2 us
    ppermute x26 -> x31, waiting for transfers between devices: 75.5 us -> 59.1 us  [swap(): return lax.ppermute(value, axis, [(i, i ^ step) for i in range(count)])]
    ppermute x4, waiting for transfers between devices: 10.7 us -> 19.6 us  [ahead(): lax.ppermute(v, 'seq', [(s, (s + 2 * k) % n_seq) for s in range(n_seq)])]
    ppermute x4, starting transfers between devices: 7.83 us -> 3.71 us  [ahead(): lax.ppermute(v, 'seq', [(s, (s + 2 * k) % n_seq) for s in range(n_seq)])]
    pallas_call x30 -> x33, Pallas kernels: 66.1 us -> 63.5 us  [launch(): pl.pallas_call(body, grid_spec=pltpu.PrefetchScalarGridSpec(num_scalar_pr...]
    ppermute x1, starting transfers between devices: 0.01 us -> 2.36 us  [diagonal(): lax.ppermute(v, ('dp', 'seq'), [(i, i ^ n_seq ^ 1) for i in range(2 * n_s...]
    ppermute x26 -> x31, starting transfers between devices: 27 us -> 27.2 us  [swap(): return lax.ppermute(value, axis, [(i, i ^ step) for i in range(count)])]
  transfers between devices with their start and end apart: 32 -> 37, of which waited for: 15 -> 20; matrix products, arithmetic and copies ran while one was open for 1% -> 0% of each run, Pallas kernels for 28% -> 28%
where the time goes in v3:
time: 202 us; the launch traced here: 200 us
  waiting for transfers between devices  86 us (43%)
  Pallas kernels  63.5 us (31%)
  starting transfers between devices  34.5 us (17%)
  local copies, waits for them, and re-layouts  14.5 us (7%)
    pallas_call x33, Pallas kernels, launch(): pl.pallas_call(body, grid_spec=pltpu.PrefetchScalarGridSpec(num_scalar_pr...  63.5 us
    ppermute x31, waiting for transfers between devices, swap(): return lax.ppermute(value, axis, [(i, i ^ step) for i in range(count)])  59.1 us
    ppermute x31, starting transfers between devices, swap(): return lax.ppermute(value, axis, [(i, i ^ step) for i in range(count)])  27.2 us
    ppermute x4, waiting for transfers between devices, ahead(): lax.ppermute(v, 'seq', [(s, (s + 2 * k) % n_seq) for s in range(n_seq)])  19.6 us
    unnamed x62, local copies, waits for them, and re-layouts  14.2 us
    ppermute x1, waiting for transfers between devices, diagonal(): lax.ppermute(v, ('dp', 'seq'), [(i, i ^ n_seq ^ 1) for i in range(2 * n_s...  5.54 us
  transfers between devices with their start and end apart: 37, of which 20 were waited for; matrix products, arithmetic and copies ran while one was open for 0% of the time, Pallas kernels for 28%

profile of v3, /device:TPU:0, one launch (start us, length us, event | category | flops | bytes accessed | tf_op | source)
XLA Modules:
  0.0 199.6 jit_solution(11797110698097359002)
XLA Ops:
  1.2 1.2 copy-done.24
  3.4 1.8 copy-done.7
  5.2 1.3 shard_map.102
  6.5 2.6 %collective-permute-start.4 = (bf16[128,1024]{1,0:T(8,128)(2,1)S(1)}, bf16[128,1024]{1,0:T(8,128)(2,1)S(1)}, u32[]{:S(2)}, u32[]{:S(2)}) collective-permute-start(bf16[128,1024]{1,0:T(8,128)(2,1)S(1)} %get-tuple-element.54), channel_id=1, source_target_pairs={{0,16},{16,0},{1,17},{17,1},{2,18},{18,2},{3,19},{19,3},{4,20},{20... | collective-permute-start | bytes 786440 | tf_op jit(solution)/shard_map/ppermute | solution.py:26
  9.0 1.6 collective-permute-start.5
  11.2 5.0 %collective-permute-done.4.refs_1_ = bf16[128,1024]{1,0:T(8,128)(2,1)S(1)} collective-permute-done((bf16[128,1024]{1,0:T(8,128)(2,1)S(1)}, bf16[128,1024]{1,0:T(8,128)(2,1)S(1)}, u32[]{:S(2)}, u32[]{:S(2)}) %collective-permute-start.4) | collective-permute-done | bytes 262176 | tf_op jit(solution)/shard_map/ppermute | solution.py:26
  16.2 1.3 collective-permute-done.5.refs_2_
  17.5 1.6 collective-permute-start.11
  19.8 2.4 %collective-permute-start.6 = (bf16[128,1024]{1,0:T(8,128)(2,1)S(1)}, bf16[128,1024]{1,0:T(8,128)(2,1)S(1)}, u32[]{:S(2)}, u32[]{:S(2)}) collective-permute-start(bf16[128,1024]{1,0:T(8,128)(2,1)S(1)} %get-tuple-element.56), channel_id=1, source_target_pairs={{0,20},{4,16},{8,28},{12,24},{16,4},{20,0},{24,12},{28,8},{1,21},{... | collective-permute-start | bytes 786440 | tf_op jit(solution)/shard_map/ppermute | solution.py:332
  22.2 5.5 %collective-permute-done.6.refs_4_.refs_7_ = bf16[128,1024]{1,0:T(8,128)(2,1)S(1)} collective-permute-done((bf16[128,1024]{1,0:T(8,128)(2,1)S(1)}, bf16[128,1024]{1,0:T(8,128)(2,1)S(1)}, u32[]{:S(2)}, u32[]{:S(2)}) %collective-permute-start.6) | collective-permute-done | bytes 262176 | tf_op jit(solution)/shard_map/ppermute | solution.py:332
  27.8 0.9 copy-done.12
  28.7 0.8 shard_map.104.refs_3_
  29.6 1.8 collective-permute-start.7
  31.5 5.0 %collective-permute-done.11.refs_4_ = bf16[384,1024]{1,0:T(8,128)(2,1)} collective-permute-done((bf16[384,1024]{1,0:T(8,128)(2,1)S(1)}, bf16[384,1024]{1,0:T(8,128)(2,1)}, u32[]{:S(2)}, u32[]{:S(2)}) %collective-permute-start.11) | collective-permute-done | bytes 786464 | tf_op jit(solution)/shard_map/ppermute | solution.py:26
  36.6 1.6 collective-permute-start.13
  38.2 5.9 %collective-permute-done.3.refs_2_.refs_9_.refs_5_ = bf16[512,768]{1,0:T(8,128)(2,1)S(1)} collective-permute-done((bf16[512,768]{1,0:T(8,128)(2,1)S(1)}, bf16[512,768]{1,0:T(8,128)(2,1)S(1)}, u32[]{:S(2)}, u32[]{:S(2)}) %collective-permute-start.3) | collective-permute-done | bytes 786464 | tf_op jit(solution)/shard_map/ppermute | solution.py:26
  44.2 0.9 copy-done.15
  45.4 1.8 collective-permute-start.18
  47.2 1.3 shard_map.106
  48.5 1.5 collective-permute-start.17
  50.1 1.5 collective-permute-done.14.refs_1_
  51.6 3.0 %shard_map.107.refs_4_ = bf16[1024,256]{1,0:T(8,128)(2,1)S(1)} custom-call(bf16[384,1024]{1,0:T(8,128)(2,1)} %collective-permute-done.12.refs_0_, bf16[128,1024]{1,0:T(8,128)(2,1)S(1)} %collective-permute-done.14.refs_1_, bf16[384,1024]{1,0:T(8,128)(2,1)S(1)} %collective-permute-done.8.refs_5_.refs_2_, ...), custom_call_target="tpu_custom_call" | custom-call | flops 1 | bytes 1 | tf_op jit(solution)/shard_map/pallas_call | solution.py:36
  54.6 2.7 %collective-permute-start.20 = (bf16[1024,256]{1,0:T(8,128)(2,1)S(1)}, bf16[1024,256]{1,0:T(8,128)(2,1)S(1)}, u32[]{:S(2)}, u32[]{:S(2)}) collective-permute-start(bf16[1024,256]{1,0:T(8,128)(2,1)S(1)} %shard_map.107.refs_4_), channel_id=1, source_target_pairs={{0,8},{4,12},{8,0},{12,4},{1,9},{5,13},{9,1},{13,5},{2,10},{6,14},... | collective-permute-start | bytes 1572872 | tf_op jit(solution)/shard_map/ppermute | solution.py:335
  57.3 3.4 %copy-done.6 = bf16[1,4096,1024]{2,1,0:T(8,128)(2,1)S(1)} copy-done((bf16[1,4096,1024]{2,1,0:T(8,128)(2,1)S(1)}, bf16[1,4096,1024]{2,1,0:T(8,128)(2,1)}, u32[]{:S(2)}) %copy-start.6) | copy-done | bytes 8388632
  60.6 9.2 %shard_map.108 = (bf16[128,2048]{1,0:T(8,128)(2,1)S(1)}, bf16[128,2048]{1,0:T(8,128)(2,1)S(1)}, f32[128,4096]{1,0:T(8,128)S(1)}) custom-call(bf16[256,1024]{1,0:T(8,128)(2,1)S(1)} %get-tuple-element.57.refs_2_.refs_0_, bf16[256,1024]{1,0:T(8,128)(2,1)S(1)} %collective-permute-done.10.refs_1_, bf16[4096,1024]{1,0:T(8,128)(2,1)S(1)} %bitcast.41, ...), custom_call_target="tpu_custom_call" | custom-call | flops 1 | bytes 1 | tf_op jit(solution)/shard_map/pallas_call | solution.py:36
  69.9 2.9 %shard_map.109.refs_3_ = bf16[1024,256]{1,0:T(8,128)(2,1)S(1)} custom-call(bf16[384,1024]{1,0:T(8,128)(2,1)} %collective-permute-done.12.refs_0_, bf16[128,1024]{1,0:T(8,128)(2,1)S(1)} %collective-permute-done.14.refs_1_, bf16[384,1024]{1,0:T(8,128)(2,1)S(1)} %collective-permute-done.8.refs_5_.refs_2_, ...), custom_call_target="tpu_custom_call" | custom-call | flops 1 | bytes 1 | tf_op jit(solution)/shard_map/pallas_call | solution.py:36
  73.3 1.5 collective-permute-start.15
  75.4 5.5 %collective-permute-done.20.refs_1_.refs_2_ = bf16[1024,256]{1,0:T(8,128)(2,1)S(1)} collective-permute-done((bf16[1024,256]{1,0:T(8,128)(2,1)S(1)}, bf16[1024,256]{1,0:T(8,128)(2,1)S(1)}, u32[]{:S(2)}, u32[]{:S(2)}) %collective-permute-start.20) | collective-permute-done | bytes 524320 | tf_op jit(solution)/shard_map/ppermute | solution.py:335
  80.9 11.2 %collective-permute-done.19.refs_1_ = bf16[256,1024]{1,0:T(8,128)(2,1)S(1)} collective-permute-done((bf16[256,1024]{1,0:T(8,128)(2,1)S(1)}, bf16[256,1024]{1,0:T(8,128)(2,1)S(1)}, u32[]{:S(2)}, u32[]{:S(2)}) %collective-permute-start.19) | collective-permute-done | bytes 524320 | tf_op jit(solution)/shard_map/ppermute | solution.py:26
  92.8 1.6 collective-permute-start.23
  94.4 5.1 %collective-permute-done.16.refs_2_ = bf16[128,2048]{1,0:T(8,128)(2,1)S(1)} collective-permute-done((bf16[128,2048]{1,0:T(8,128)(2,1)S(1)}, bf16[128,2048]{1,0:T(8,128)(2,1)S(1)}, u32[]{:S(2)}, u32[]{:S(2)}) %collective-permute-start.16) | collective-permute-done | bytes 524320 | tf_op jit(solution)/shard_map/ppermute | solution.py:26
  100.2 9.9 %shard_map.114 = (bf16[128,2048]{1,0:T(8,128)(2,1)}, bf16[128,2048]{1,0:T(8,128)(2,1)}, f32[128,4096]{1,0:T(8,128)S(1)}) custom-call(bf16[256,1024]{1,0:T(8,128)(2,1)S(1)} %copy-done.26, bf16[256,1024]{1,0:T(8,128)(2,1)S(1)} %collective-permute-done.refs_1_, bf16[4096,1024]{1,0:T(8,128)(2,1)S(1)} %bitcast.44, ...), custom_call_target="tpu_custom_call" | custom-call | flops 1 | bytes 1 | tf_op jit(solution)/shard_map/pallas_call | solution.py:36
  110.1 7.9 %collective-permute-done.24.refs_1_.refs_2_ = bf16[1024,256]{1,0:T(8,128)(2,1)S(1)} collective-permute-done((bf16[1024,256]{1,0:T(8,128)(2,1)S(1)}, bf16[1024,256]{1,0:T(8,128)(2,1)S(1)}, u32[]{:S(2)}, u32[]{:S(2)}) %collective-permute-start.24) | collective-permute-done | bytes 524320 | tf_op jit(solution)/shard_map/ppermute | solution.py:335
  118.0 2.4 %collective-permute-done.23.refs_0_ = bf16[512,1024]{1,0:T(8,128)(2,1)S(1)} collective-permute-done((bf16[512,1024]{1,0:T(8,128)(2,1)S(1)}, bf16[512,1024]{1,0:T(8,128)(2,1)S(1)}, u32[]{:S(2)}, u32[]{:S(2)}) %collective-permute-start.23) | collective-permute-done | bytes 1048608 | tf_op jit(solution)/shard_map/ppermute | solution.py:26
  120.4 1.5 collective-permute-done.26.refs_2_
  122.1 0.8 copy-done.9
  122.9 1.6 collective-permute-start.30
  124.5 3.0 %shard_map.117.refs_7_ = bf16[1024,256]{1,0:T(8,128)(2,1)S(1)} custom-call(bf16[384,1024]{1,0:T(8,128)(2,1)} %collective-permute-done.12.refs_0_, bf16[128,1024]{1,0:T(8,128)(2,1)S(1)} %collective-permute-done.14.refs_1_, bf16[384,1024]{1,0:T(8,128)(2,1)S(1)} %collective-permute-done.8.refs_5_.refs_2_, ...), custom_call_target="tpu_custom_call" | custom-call | flops 1 | bytes 1 | tf_op jit(solution)/shard_map/pallas_call | solution.py:36
  127.9 2.6 %shard_map.118.refs_1_ = f32[1024,256]{1,0:T(8,128)S(1)} custom-call(bf16[512,1024]{1,0:T(8,128)(2,1)S(1)} %collective-permute-done.28.refs_0_, bf16[512,1024]{1,0:T(8,128)(2,1)S(1)} %collective-permute-done.27.refs_3_.refs_1_, bf16[512,1024]{1,0:T(8,128)(2,1)S(1)} %shard_map.116.refs_11_.refs_2_, bf16[512,1024]{1,0:T(8,128)(2,1)S(1)} %shard_map.112.refs_3_, ...), custom_call_target="tpu_custom_call" | custom-call | flops 1 | bytes 1 | tf_op jit(solution)/shard_map/pallas_call | solution.py:36
  130.6 2.8 %shard_map.119 = (f32[1024,1024]{1,0:T(8,128)}, f32[1024,1024]{1,0:T(8,128)}, f32[1024,1024]{1,0:T(8,128)}, bf16[2,1024,1024]{2,1,0:T(8,128)(2,1)}, bf16[1024,256]{1,0:T(8,128)(2,1)S(1)}) custom-call(s32[1]{0:T(128)} %bitcast.refs_0_, f32[1024,256]{1,0:T(8,128)S(1)} %shard_map.118.refs_1_, bf16[1024,256]{1,0:T(8,128)(2,1)S(1)} %collective-permute-done.20.refs_1_.refs_2_, ...), custom_call_target="tpu_custom_call" | custom-call | flops 1 | bytes 1 | tf_op jit(solution)/shard_map/pallas_call | solution.py:36
  133.9 1.4 shard_map.120.refs_1_
  135.3 2.8 %shard_map.121 = (f32[1024,1024]{1,0:T(8,128)}, f32[1024,1024]{1,0:T(8,128)}, f32[1024,1024]{1,0:T(8,128)}, bf16[2,1024,1024]{2,1,0:T(8,128)(2,1)}, bf16[1024,256]{1,0:T(8,128)(2,1)S(1)}) custom-call(s32[1]{0:T(128)} %bitcast.refs_0_, f32[1024,256]{1,0:T(8,128)S(1)} %shard_map.120.refs_1_, ...), custom_call_target="tpu_custom_call", output_to_operand_aliasing={{0}: (6, {}), {1}: (7, {}), {2}: (8, {}), {3}: (9, {})} | custom-call | flops 1 | bytes 1 | tf_op jit(solution)/shard_map/pallas_call | solution.py:36
  138.1 1.5 collective-permute-start.32
  139.6 1.6 collective-permute-start.21
  141.1 1.1 collective-permute-done.30.refs_10_.refs_6_
  142.2 1.5 collective-permute-start.22
  143.8 1.4 shard_map.122.refs_11_.refs_1_
  145.2 3.6 %shard_map.123.refs_7_ = bf16[1024,256]{1,0:T(8,128)(2,1)} custom-call(bf16[384,1024]{1,0:T(8,128)(2,1)} %collective-permute-done.12.refs_0_, bf16[128,1024]{1,0:T(8,128)(2,1)S(1)} %collective-permute-done.14.refs_1_, bf16[384,1024]{1,0:T(8,128)(2,1)S(1)} %collective-permute-done.8.refs_5_.refs_2_, bf16[128,1024]{1,0:T(8,128)(2,1)} %collective-permute-done.9.refs_6_.refs_3_, ...), custom_call_target="tpu_custom_call" | custom-call | flops 1 | bytes 1 | tf_op jit(solution)/shard_map/pallas_call | solution.py:36
  148.8 1.4 shard_map.124.refs_0_.refs_1_
  150.2 2.8 %collective-permute-done.29.refs_1_.refs_2_ = bf16[1024,256]{1,0:T(8,128)(2,1)S(1)} collective-permute-done((bf16[1024,256]{1,0:T(8,128)(2,1)S(1)}, bf16[1024,256]{1,0:T(8,128)(2,1)S(1)}, u32[]{:S(2)}, u32[]{:S(2)}) %collective-permute-start.29) | collective-permute-done | bytes 524320 | tf_op jit(solution)/shard_map/ppermute | solution.py:335
  153.1 4.4 %collective-permute-done.32.refs_2_ = bf16[1024,256]{1,0:T(8,128)(2,1)S(1)} collective-permute-done((bf16[1024,256]{1,0:T(8,128)(2,1)S(1)}, bf16[1024,256]{1,0:T(8,128)(2,1)S(1)}, u32[]{:S(2)}, u32[]{:S(2)}) %collective-permute-start.32) | collective-permute-done | bytes 524320 | tf_op jit(solution)/shard_map/ppermute | solution.py:26
  157.5 0.8 copy-done.22
  158.3 2.9 %shard_map.127 = (f32[1024,1024]{1,0:T(8,128)}, f32[1024,1024]{1,0:T(8,128)}, f32[1024,1024]{1,0:T(8,128)}, bf16[2,1024,1024]{2,1,0:T(8,128)(2,1)}, bf16[1024,256]{1,0:T(8,128)(2,1)}) custom-call(s32[1]{0:T(128)} %bitcast.refs_0_, ...), custom_call_target="tpu_custom_call", output_to_operand_aliasing={{0}: (6, {}), {1}: (7, {}), {2}: (8, {}), {3}: (9, {})} | custom-call | flops 1 | bytes 1 | tf_op jit(solution)/shard_map/pallas_call | solution.py:36
  161.8 1.7 collective-permute-done.22.refs_2_
  163.5 1.6 copy-done.18
  165.1 1.4 shard_map.128.refs_1_
  166.6 1.3 collective-permute-start.33
  167.9 1.8 collective-permute-done.33
  169.7 4.2 %shard_map.129.refs_0_ = bf16[512,2048]{1,0:T(8,128)(2,1)} custom-call(s32[1]{0:T(128)} %bitcast.refs_0_, bf16[128,4096]{1,0:T(8,128)(2,1)S(1)} %shard_map.128.refs_1_, bf16[128,4096]{1,0:T(8,128)(2,1)S(1)} %copy-done.10, bf16[16,2048]{1,0:T(8,128)(2,1)S(1)} %pad.4.refs_3_), custom_call_target="tpu_custom_call" | custom-call | flops 1 | bytes 1 | tf_op jit(solution)/shard_map/pallas_call | solution.py:36
  173.8 3.4 %collective-permute-done.34.refs_1_.refs_2_ = bf16[1024,256]{1,0:T(8,128)(2,1)} collective-permute-done((bf16[1024,256]{1,0:T(8,128)(2,1)}, bf16[1024,256]{1,0:T(8,128)(2,1)}, u32[]{:S(2)}, u32[]{:S(2)}) %collective-permute-start.34) | collective-permute-done | bytes 524320 | tf_op jit(solution)/shard_map/ppermute | solution.py:335
  177.2 1.8 copy-done.19
  179.1 4.1 %shard_map.132 = (f32[1024,1024]{1,0:T(8,128)}, f32[1024,1024]{1,0:T(8,128)}, f32[1024,1024]{1,0:T(8,128)}, bf16[2,1024,1024]{2,1,0:T(8,128)(2,1)}, bf16[1024,256]{1,0:T(8,128)(2,1)S(1)}) custom-call(s32[1]{0:T(128)} %bitcast.refs_0_, ...), custom_call_target="tpu_custom_call", output_to_operand_aliasing={{0}: (6, {}), {1}: (7, {}), {2}: (8, {}), {3}: (9, {})} | custom-call | flops 1 | bytes 1 | tf_op jit(solution)/shard_map/pallas_call | solution.py:36
  183.8 12.9 %collective-permute-done.36.refs_4_ = bf16[1024,256]{1,0:T(8,128)(2,1)S(1)} collective-permute-done((bf16[1024,256]{1,0:T(8,128)(2,1)S(1)}, bf16[1024,256]{1,0:T(8,128)(2,1)S(1)}, u32[]{:S(2)}, u32[]{:S(2)}) %collective-permute-start.36) | collective-permute-done | bytes 524320 | tf_op jit(solution)/shard_map/ppermute | solution.py:26
  196.7 2.9 %shard_map.133 = bf16[2,1024,1024]{2,1,0:T(8,128)(2,1)} custom-call(s32[1]{0:T(128)} %bitcast.refs_0_, bf16[1024,256]{1,0:T(8,128)(2,1)S(1)} %copy-done.21, bf16[1024,256]{1,0:T(8,128)(2,1)S(1)} %copy-done.23, bf16[1024,256]{1,0:T(8,128)(2,1)} %collective-permute-done.35.refs_1_.refs_3_, ...), custom_call_target="tpu_custom_call", output_to_operand_aliasing={{}: (5, {})} | custom-call | flops 1 | bytes 1 | tf_op jit(solution)/shard_map/pallas_call | solution.py:36
  (113 shorter events, 8.5 us)
Async XLA Ops:
  0.6 27.1 %collective-permute-start.1 = (bf16[4096,1024]{1,0:T(8,128)(2,1)}, bf16[4096,1024]{1,0:T(8,128)(2,1)}, u32[]{:S(2)}, u32[]{:S(2)}) collective-permute-start(bf16[4096,1024]{1,0:T(8,128)(2,1)} %bitcast.40), channel_id=1, source_target_pairs={{0,1},{1,0},{2,3},{3,2},{4,5},{5,4},{6,7},{7,6},{8,9},{9,8},{10,11... | collective-permute-start | bytes 25165832 | tf_op jit(solution)/shard_map/ppermute | solution.py:26
  1.1 1.2 copy-start.24
  3.3 15.8 %copy-start.25 = (bf16[256,1024]{1,0:T(8,128)(2,1)}, bf16[256,1024]{1,0:T(8,128)(2,1)S(1)}, u32[]{:S(2)}) copy-start(bf16[256,1024]{1,0:T(8,128)(2,1)S(1)} %get-tuple-element.49.refs_0_) | copy-start | bytes 1572868
  3.3 18.8 %copy-start.11 = (bf16[512,256]{1,0:T(8,128)(2,1)}, bf16[512,256]{1,0:T(8,128)(2,1)S(1)}, u32[]{:S(2)}) copy-start(bf16[512,256]{1,0:T(8,128)(2,1)S(1)} %get-tuple-element.52.refs_2_.refs_0_.refs_8_.refs_4_) | copy-start | bytes 786436
  3.4 1.8 copy-start.7
  6.5 9.7 %collective-permute-start.4 = (bf16[128,1024]{1,0:T(8,128)(2,1)S(1)}, bf16[128,1024]{1,0:T(8,128)(2,1)S(1)}, u32[]{:S(2)}, u32[]{:S(2)}) collective-permute-start(bf16[128,1024]{1,0:T(8,128)(2,1)S(1)} %get-tuple-element.54), channel_id=1, source_target_pairs={{0,16},{16,0},{1,17},{17,1},{2,18},{18,2},{3,19},{19,3},{4,20},{20... | collective-permute-start | bytes 786440 | tf_op jit(solution)/shard_map/ppermute | solution.py:26
  9.0 8.4 %collective-permute-start.5 = (bf16[128,1024]{1,0:T(8,128)(2,1)S(1)}, bf16[128,1024]{1,0:T(8,128)(2,1)S(1)}, u32[]{:S(2)}, u32[]{:S(2)}) collective-permute-start(bf16[128,1024]{1,0:T(8,128)(2,1)S(1)} %get-tuple-element.55), channel_id=1, source_target_pairs={{0,4},{4,0},{8,12},{12,8},{1,5},{5,1},{9,13},{13,9},{2,6},{6,2},{1... | collective-permute-start | bytes 786440 | tf_op jit(solution)/shard_map/ppermute | solution.py:26
  10.6 11.5 %collective-permute-start.2 = (bf16[512,256]{1,0:T(8,128)(2,1)S(1)}, bf16[512,256]{1,0:T(8,128)(2,1)S(1)}, u32[]{:S(2)}, u32[]{:S(2)}) collective-permute-start(bf16[512,256]{1,0:T(8,128)(2,1)S(1)} %get-tuple-element.52.refs_2_.refs_0_.refs_8_.refs_4_), channel_id=1, source_target_pairs={{0,16},{16,0},{1,17},{17,1},{2,18},{18,2},{3,19},{19,3},{4,20},{20... | collective-permute-start | bytes 786440 | tf_op jit(solution)/shard_map/ppermute | solution.py:26
  17.5 19.0 %collective-permute-start.11 = (bf16[384,1024]{1,0:T(8,128)(2,1)S(1)}, bf16[384,1024]{1,0:T(8,128)(2,1)}, u32[]{:S(2)}, u32[]{:S(2)}) collective-permute-start(bf16[384,1024]{1,0:T(8,128)(2,1)S(1)} %shard_map.103.refs_2_.refs_6_), channel_id=1, source_target_pairs={{0,2},{1,3},{2,0},{3,1},{4,6},{5,7},{6,4},{7,5},{8,10},{9,11},{10,... | collective-permute-start | bytes 2359304 | tf_op jit(solution)/shard_map/ppermute | solution.py:26
  19.1 25.0 %collective-permute-start.3 = (bf16[512,768]{1,0:T(8,128)(2,1)S(1)}, bf16[512,768]{1,0:T(8,128)(2,1)S(1)}, u32[]{:S(2)}, u32[]{:S(2)}) collective-permute-start(bf16[512,768]{1,0:T(8,128)(2,1)S(1)} %get-tuple-element.51.refs_0_.refs_8_.refs_4_), channel_id=1, source_target_pairs={{0,16},{16,0},{1,17},{17,1},{2,18},{18,2},{3,19},{19,3},{4,20},{20... | collective-permute-start | bytes 2359304 | tf_op jit(solution)/shard_map/ppermute | solution.py:26
  19.8 8.0 %collective-permute-start.6 = (bf16[128,1024]{1,0:T(8,128)(2,1)S(1)}, bf16[128,1024]{1,0:T(8,128)(2,1)S(1)}, u32[]{:S(2)}, u32[]{:S(2)}) collective-permute-start(bf16[128,1024]{1,0:T(8,128)(2,1)S(1)} %get-tuple-element.56), channel_id=1, source_target_pairs={{0,20},{4,16},{8,28},{12,24},{16,4},{20,0},{24,12},{28,8},{1,21},{... | collective-permute-start | bytes 786440 | tf_op jit(solution)/shard_map/ppermute | solution.py:332
  22.2 7.4 %copy-start.14 = (bf16[512,256]{1,0:T(8,128)(2,1)}, bf16[512,256]{1,0:T(8,128)(2,1)S(1)}, u32[]{:S(2)}) copy-start(bf16[512,256]{1,0:T(8,128)(2,1)S(1)} %collective-permute-done.2.refs_1_.refs_9_.refs_5_) | copy-start | bytes 786436
  22.2 21.9 %collective-permute-start.8 = (bf16[384,1024]{1,0:T(8,128)(2,1)S(1)}, bf16[384,1024]{1,0:T(8,128)(2,1)S(1)}, u32[]{:S(2)}, u32[]{:S(2)}) collective-permute-start(bf16[384,1024]{1,0:T(8,128)(2,1)S(1)} %shard_map.103.refs_2_.refs_6_), channel_id=1, source_target_pairs={{0,1},{1,0},{2,3},{3,2},{4,5},{5,4},{6,7},{7,6},{8,9},{9,8},{10,11... | collective-permute-start | bytes 2359304 | tf_op jit(solution)/shard_map/ppermute | solution.py:26
  29.6 14.6 %collective-permute-start.7 = (bf16[1024,256]{1,0:T(8,128)(2,1)}, bf16[1024,256]{1,0:T(8,128)(2,1)}, u32[]{:S(2)}, u32[]{:S(2)}) collective-permute-start(bf16[1024,256]{1,0:T(8,128)(2,1)} %shard_map.104.refs_3_), channel_id=1, source_target_pairs={{0,4},{4,0},{8,12},{12,8},{1,5},{5,1},{9,13},{13,9},{2,6},{6,2},{1... | collective-permute-start | bytes 1572872 | tf_op jit(solution)/shard_map/ppermute | solution.py:26
  31.4 5.3 %collective-permute-start.9 = (bf16[128,1024]{1,0:T(8,128)(2,1)S(1)}, bf16[128,1024]{1,0:T(8,128)(2,1)}, u32[]{:S(2)}, u32[]{:S(2)}) collective-permute-start(bf16[128,1024]{1,0:T(8,128)(2,1)S(1)} %collective-permute-done.6.refs_4_.refs_7_), channel_id=1, source_target_pairs={{0,1},{1,0},{2,3},{3,2},{4,5},{5,4},{6,7},{7,6},{8,9},{9,8},{10,11... | collective-permute-start | bytes 786440 | tf_op jit(solution)/shard_map/ppermute | solution.py:26
  36.5 15.1 %collective-permute-start.12 = (bf16[384,1024]{1,0:T(8,128)(2,1)}, bf16[384,1024]{1,0:T(8,128)(2,1)}, u32[]{:S(2)}, u32[]{:S(2)}) collective-permute-start(bf16[384,1024]{1,0:T(8,128)(2,1)} %collective-permute-done.11.refs_4_), channel_id=1, source_target_pairs={{0,1},{1,0},{2,3},{3,2},{4,5},{5,4},{6,7},{7,6},{8,9},{9,8},{10,11... | collective-permute-start | bytes 2359304 | tf_op jit(solution)/shard_map/ppermute | solution.py:26
  36.6 10.6 %copy-start.8 = (bf16[1,512,2048]{2,1,0:T(8,128)(2,1)S(1)}, bf16[1,512,2048]{2,1,0:T(8,128)(2,1)}, u32[]{:S(2)}) copy-start(bf16[1,512,2048]{2,1,0:T(8,128)(2,1)} %param.6) | copy-start | bytes 6291460
  36.6 15.0 %copy-start.13 = (bf16[512,256]{1,0:T(8,128)(2,1)S(1)}, bf16[512,256]{1,0:T(8,128)(2,1)}, u32[]{:S(2)}) copy-start(bf16[512,256]{1,0:T(8,128)(2,1)} %copy-done.11) | copy-start | bytes 786436
  36.6 13.4 %collective-permute-start.13 = (bf16[128,1024]{1,0:T(8,128)(2,1)S(1)}, bf16[128,1024]{1,0:T(8,128)(2,1)S(1)}, u32[]{:S(2)}, u32[]{:S(2)}) collective-permute-start(bf16[128,1024]{1,0:T(8,128)(2,1)S(1)} %collective-permute-done.6.refs_4_.refs_7_), channel_id=1, source_target_pairs={{0,2},{1,3},{2,0},{3,1},{4,6},{5,7},{6,4},{7,5},{8,10},{9,11},{10,... | collective-permute-start | bytes 786440 | tf_op jit(solution)/shard_map/ppermute | solution.py:26
  45.1 6.5 %copy-start.16 = (bf16[512,256]{1,0:T(8,128)(2,1)S(1)}, bf16[512,256]{1,0:T(8,128)(2,1)}, u32[]{:S(2)}) copy-start(bf16[512,256]{1,0:T(8,128)(2,1)} %copy-done.14) | copy-start | bytes 786436
  45.3 11.9 %collective-permute-start.10 = (bf16[256,1024]{1,0:T(8,128)(2,1)S(1)}, bf16[256,1024]{1,0:T(8,128)(2,1)S(1)}, u32[]{:S(2)}, u32[]{:S(2)}) collective-permute-start(bf16[256,1024]{1,0:T(8,128)(2,1)S(1)} %get-tuple-element.58), channel_id=1, source_target_pairs={{0,1},{1,0},{2,3},{3,2},{4,5},{5,4},{6,7},{7,6},{8,9},{9,8},{10,11... | collective-permute-start | bytes 1572872 | tf_op jit(solution)/shard_map/ppermute | solution.py:26
  45.4 24.4 %collective-permute-start.18 = (bf16[1024,256]{1,0:T(8,128)(2,1)S(1)}, bf16[1024,256]{1,0:T(8,128)(2,1)S(1)}, u32[]{:S(2)}, u32[]{:S(2)}) collective-permute-start(bf16[1024,256]{1,0:T(8,128)(2,1)S(1)} %get-tuple-element.65), channel_id=1, source_target_pairs={{0,4},{4,0},{8,12},{12,8},{1,5},{5,1},{9,13},{13,9},{2,6},{6,2},{1... | collective-permute-start | bytes 1572872 | tf_op jit(solution)/shard_map/ppermute | solution.py:26
  48.5 24.2 %collective-permute-start.17 = (bf16[256,1024]{1,0:T(8,128)(2,1)S(1)}, bf16[256,1024]{1,0:T(8,128)(2,1)S(1)}, u32[]{:S(2)}, u32[]{:S(2)}) collective-permute-start(bf16[256,1024]{1,0:T(8,128)(2,1)S(1)} %get-tuple-element.64), channel_id=1, source_target_pairs={{0,16},{16,0},{1,17},{17,1},{2,18},{18,2},{3,19},{19,3},{4,20},{20... | collective-permute-start | bytes 1572872 | tf_op jit(solution)/shard_map/ppermute | solution.py:26
  50.1 1.5 collective-permute-start.14
  54.6 26.3 %collective-permute-start.20 = (bf16[1024,256]{1,0:T(8,128)(2,1)S(1)}, bf16[1024,256]{1,0:T(8,128)(2,1)S(1)}, u32[]{:S(2)}, u32[]{:S(2)}) collective-permute-start(bf16[1024,256]{1,0:T(8,128)(2,1)S(1)} %shard_map.107.refs_4_), channel_id=1, source_target_pairs={{0,8},{4,12},{8,0},{12,4},{1,9},{5,13},{9,1},{13,5},{2,10},{6,14},... | collective-permute-start | bytes 1572872 | tf_op jit(solution)/shard_map/ppermute | solution.py:335
  57.3 3.4 %copy-start.6 = (bf16[1,4096,1024]{2,1,0:T(8,128)(2,1)S(1)}, bf16[1,4096,1024]{2,1,0:T(8,128)(2,1)}, u32[]{:S(2)}) copy-start(bf16[1,4096,1024]{2,1,0:T(8,128)(2,1)} %param.8) | copy-start | bytes 25165828
  69.8 5.5 %copy-start.28 = (bf16[256,1024]{1,0:T(8,128)(2,1)S(1)}, bf16[256,1024]{1,0:T(8,128)(2,1)}, u32[]{:S(2)}) copy-start(bf16[256,1024]{1,0:T(8,128)(2,1)} %copy-done.27) | copy-start | bytes 1572868
  72.8 19.3 %collective-permute-start.19 = (bf16[256,1024]{1,0:T(8,128)(2,1)S(1)}, bf16[256,1024]{1,0:T(8,128)(2,1)S(1)}, u32[]{:S(2)}, u32[]{:S(2)}) collective-permute-start(bf16[256,1024]{1,0:T(8,128)(2,1)S(1)} %get-tuple-element.67), channel_id=1, source_target_pairs={{0,4},{4,0},{8,12},{12,8},{1,5},{5,1},{9,13},{13,9},{2,6},{6,2},{1... | collective-permute-start | bytes 1572872 | tf_op jit(solution)/shard_map/ppermute | solution.py:26
  73.3 19.4 %collective-permute-start.15 = (bf16[128,2048]{1,0:T(8,128)(2,1)S(1)}, bf16[128,2048]{1,0:T(8,128)(2,1)S(1)}, u32[]{:S(2)}, u32[]{:S(2)}) collective-permute-start(bf16[128,2048]{1,0:T(8,128)(2,1)S(1)} %get-tuple-element.61), channel_id=1, source_target_pairs={{0,2},{1,3},{2,0},{3,1},{4,6},{5,7},{6,4},{7,5},{8,10},{9,11},{10,... | collective-permute-start | bytes 1572872 | tf_op jit(solution)/shard_map/ppermute | solution.py:26
  74.9 24.6 %collective-permute-start.16 = (bf16[128,2048]{1,0:T(8,128)(2,1)S(1)}, bf16[128,2048]{1,0:T(8,128)(2,1)S(1)}, u32[]{:S(2)}, u32[]{:S(2)}) collective-permute-start(bf16[128,2048]{1,0:T(8,128)(2,1)S(1)} %get-tuple-element.62), channel_id=1, source_target_pairs={{0,2},{1,3},{2,0},{3,1},{4,6},{5,7},{6,4},{7,5},{8,10},{9,11},{10,... | collective-permute-start | bytes 1572872 | tf_op jit(solution)/shard_map/ppermute | solution.py:26
  75.4 24.8 %collective-permute-start = (bf16[256,1024]{1,0:T(8,128)(2,1)S(1)}, bf16[256,1024]{1,0:T(8,128)(2,1)S(1)}, u32[]{:S(2)}, u32[]{:S(2)}) collective-permute-start(bf16[256,1024]{1,0:T(8,128)(2,1)S(1)} %copy-done.28), channel_id=1, source_target_pairs={{0,1},{1,0},{2,3},{3,2},{4,5},{5,4},{6,7},{7,6},{8,9},{9,8},{10,11... | collective-permute-start | bytes 1572872 | tf_op jit(solution)/shard_map/ppermute | solution.py:26
  80.9 29.3 %collective-permute-start.25 = (bf16[1024,256]{1,0:T(8,128)(2,1)S(1)}, bf16[1024,256]{1,0:T(8,128)(2,1)S(1)}, u32[]{:S(2)}, u32[]{:S(2)}) collective-permute-start(bf16[1024,256]{1,0:T(8,128)(2,1)S(1)} %get-tuple-element.71), channel_id=1, source_target_pairs={{0,4},{4,0},{8,12},{12,8},{1,5},{5,1},{9,13},{13,9},{2,6},{6,2},{1... | collective-permute-start | bytes 1572872 | tf_op jit(solution)/shard_map/ppermute | solution.py:26
  92.1 25.9 %collective-permute-start.24 = (bf16[1024,256]{1,0:T(8,128)(2,1)S(1)}, bf16[1024,256]{1,0:T(8,128)(2,1)S(1)}, u32[]{:S(2)}, u32[]{:S(2)}) collective-permute-start(bf16[1024,256]{1,0:T(8,128)(2,1)S(1)} %shard_map.109.refs_3_), channel_id=1, source_target_pairs={{0,8},{4,12},{8,0},{12,4},{1,9},{5,13},{9,1},{13,5},{2,10},{6,14},... | collective-permute-start | bytes 1572872 | tf_op jit(solution)/shard_map/ppermute | solution.py:335
  92.7 7.5 %slice-start = ((s8[8388608]{0:T(1024)(128)(4,1)}), s8[4194304]{0:T(1024)(128)(4,1)S(1)}, s32[]{:S(2)}) async-start(s8[8388608]{0:T(1024)(128)(4,1)} %bitcast.42), calls=%async_computation | async-start | bytes 8388608
  92.7 7.5 %slice-start.1 = ((s8[8388608]{0:T(1024)(128)(4,1)}), s8[4194304]{0:T(1024)(128)(4,1)S(1)}, s32[]{:S(2)}) async-start(s8[8388608]{0:T(1024)(128)(4,1)} %bitcast.42), calls=%async_computation.1 | async-start | bytes 8388608
  92.7 7.5 %copy-start.26 = (bf16[256,1024]{1,0:T(8,128)(2,1)S(1)}, bf16[256,1024]{1,0:T(8,128)(2,1)}, u32[]{:S(2)}) copy-start(bf16[256,1024]{1,0:T(8,128)(2,1)} %copy-done.25) | copy-start | bytes 1572868
  92.8 27.7 %collective-permute-start.23 = (bf16[512,1024]{1,0:T(8,128)(2,1)S(1)}, bf16[512,1024]{1,0:T(8,128)(2,1)S(1)}, u32[]{:S(2)}, u32[]{:S(2)}) collective-permute-start(bf16[512,1024]{1,0:T(8,128)(2,1)S(1)} %shard_map.112.refs_3_), channel_id=1, source_target_pairs={{0,2},{1,3},{2,0},{3,1},{4,6},{5,7},{6,4},{7,5},{8,10},{9,11},{10,... | collective-permute-start | bytes 3145736 | tf_op jit(solution)/shard_map/ppermute | solution.py:26
  99.6 22.3 %collective-permute-start.26 = (bf16[128,4096]{1,0:T(8,128)(2,1)S(1)}, bf16[128,4096]{1,0:T(8,128)(2,1)S(1)}, u32[]{:S(2)}, u32[]{:S(2)}) collective-permute-start(bf16[128,4096]{1,0:T(8,128)(2,1)S(1)} %shard_map.113.refs_4_), channel_id=1, source_target_pairs={{0,16},{16,0},{1,17},{17,1},{2,18},{18,2},{3,19},{19,3},{4,20},{20... | collective-permute-start | bytes 3145736 | tf_op jit(solution)/shard_map/ppermute | solution.py:26
  100.2 21.7 %collective-permute-start.27 = (bf16[512,1024]{1,0:T(8,128)(2,1)S(1)}, bf16[512,1024]{1,0:T(8,128)(2,1)S(1)}, u32[]{:S(2)}, u32[]{:S(2)}) collective-permute-start(bf16[512,1024]{1,0:T(8,128)(2,1)S(1)} %shard_map.112.refs_3_), channel_id=1, source_target_pairs={{0,1},{1,0},{2,3},{3,2},{4,5},{5,4},{6,7},{7,6},{8,9},{9,8},{10,11... | collective-permute-start | bytes 3145736 | tf_op jit(solution)/shard_map/ppermute | solution.py:26
  110.1 7.9 %copy-start.17 = (f32[128,4096]{1,0:T(8,128)}, f32[128,4096]{1,0:T(8,128)S(1)}, u32[]{:S(2)}) copy-start(f32[128,4096]{1,0:T(8,128)S(1)} %get-tuple-element.68.refs_0_) | copy-start | bytes 6291460
  121.9 1.0 copy-start.9
  122.0 5.9 %collective-permute-start.28 = (bf16[512,1024]{1,0:T(8,128)(2,1)S(1)}, bf16[512,1024]{1,0:T(8,128)(2,1)S(1)}, u32[]{:S(2)}, u32[]{:S(2)}) collective-permute-start(bf16[512,1024]{1,0:T(8,128)(2,1)S(1)} %shard_map.116.refs_11_.refs_2_), channel_id=1, source_target_pairs={{0,1},{1,0},{2,3},{3,2},{4,5},{5,4},{6,7},{7,6},{8,9},{9,8},{10,11... | collective-permute-start | bytes 3145736 | tf_op jit(solution)/shard_map/ppermute | solution.py:26
  122.9 19.3 %collective-permute-start.30 = (bf16[1024,256]{1,0:T(8,128)(2,1)S(1)}, bf16[1024,256]{1,0:T(8,128)(2,1)S(1)}, u32[]{:S(2)}, u32[]{:S(2)}) collective-permute-start(bf16[1024,256]{1,0:T(8,128)(2,1)S(1)} %get-tuple-element.82), channel_id=1, source_target_pairs={{0,4},{4,0},{8,12},{12,8},{1,5},{5,1},{9,13},{13,9},{2,6},{6,2},{1... | collective-permute-start | bytes 1572872 | tf_op jit(solution)/shard_map/ppermute | solution.py:26
  124.5 6.0 %copy-start.2 = (f32[1,1024,1024]{2,1,0:T(8,128)S(1)}, f32[1,1024,1024]{2,1,0:T(8,128)}, u32[]{:S(2)}) copy-start(f32[1,1024,1024]{2,1,0:T(8,128)} %param.10) | copy-start | bytes 12582916
  124.5 6.0 %copy-start.4 = (f32[1,1024,1024]{2,1,0:T(8,128)S(1)}, f32[1,1024,1024]{2,1,0:T(8,128)}, u32[]{:S(2)}) copy-start(f32[1,1024,1024]{2,1,0:T(8,128)} %param.11) | copy-start | bytes 12582916
  127.5 3.0 %copy-start = (f32[1,1024,1024]{2,1,0:T(8,128)S(1)}, f32[1,1024,1024]{2,1,0:T(8,128)}, u32[]{:S(2)}) copy-start(f32[1,1024,1024]{2,1,0:T(8,128)} %param.9) | copy-start | bytes 12582916
  127.5 25.5 %collective-permute-start.29 = (bf16[1024,256]{1,0:T(8,128)(2,1)S(1)}, bf16[1024,256]{1,0:T(8,128)(2,1)S(1)}, u32[]{:S(2)}, u32[]{:S(2)}) collective-permute-start(bf16[1024,256]{1,0:T(8,128)(2,1)S(1)} %shard_map.117.refs_7_), channel_id=1, source_target_pairs={{0,8},{4,12},{8,0},{12,4},{1,9},{5,13},{9,1},{13,5},{2,10},{6,14},... | collective-permute-start | bytes 1572872 | tf_op jit(solution)/shard_map/ppermute | solution.py:335
  133.4 19.8 %collective-permute-start.31 = (bf16[1024,256]{1,0:T(8,128)(2,1)S(1)}, bf16[1024,256]{1,0:T(8,128)(2,1)S(1)}, u32[]{:S(2)}, u32[]{:S(2)}) collective-permute-start(bf16[1024,256]{1,0:T(8,128)(2,1)S(1)} %get-tuple-element.72.refs_7_), channel_id=1, source_target_pairs={{0,16},{16,0},{1,17},{17,1},{2,18},{18,2},{3,19},{19,3},{4,20},{20... | collective-permute-start | bytes 1572872 | tf_op jit(solution)/shard_map/ppermute | solution.py:26
  138.1 19.4 %collective-permute-start.32 = (bf16[1024,256]{1,0:T(8,128)(2,1)S(1)}, bf16[1024,256]{1,0:T(8,128)(2,1)S(1)}, u32[]{:S(2)}, u32[]{:S(2)}) collective-permute-start(bf16[1024,256]{1,0:T(8,128)(2,1)S(1)} %get-tuple-element.77.refs_7_), channel_id=1, source_target_pairs={{0,16},{16,0},{1,17},{17,1},{2,18},{18,2},{3,19},{19,3},{4,20},{20... | collective-permute-start | bytes 1572872 | tf_op jit(solution)/shard_map/ppermute | solution.py:26
  139.6 22.2 %collective-permute-start.21 = (bf16[128,2048]{1,0:T(8,128)(2,1)}, bf16[128,2048]{1,0:T(8,128)(2,1)}, u32[]{:S(2)}, u32[]{:S(2)}) collective-permute-start(bf16[128,2048]{1,0:T(8,128)(2,1)} %get-tuple-element.69), channel_id=1, source_target_pairs={{0,2},{1,3},{2,0},{3,1},{4,6},{5,7},{6,4},{7,5},{8,10},{9,11},{10,... | collective-permute-start | bytes 1572872 | tf_op jit(solution)/shard_map/ppermute | solution.py:26
  142.2 21.3 %collective-permute-start.22 = (bf16[128,2048]{1,0:T(8,128)(2,1)}, bf16[128,2048]{1,0:T(8,128)(2,1)}, u32[]{:S(2)}, u32[]{:S(2)}) collective-permute-start(bf16[128,2048]{1,0:T(8,128)(2,1)} %get-tuple-element.70), channel_id=1, source_target_pairs={{0,2},{1,3},{2,0},{3,1},{4,6},{5,7},{6,4},{7,5},{8,10},{9,11},{10,... | collective-permute-start | bytes 1572872 | tf_op jit(solution)/shard_map/ppermute | solution.py:26
  153.0 24.2 %collective-permute-start.34 = (bf16[1024,256]{1,0:T(8,128)(2,1)}, bf16[1024,256]{1,0:T(8,128)(2,1)}, u32[]{:S(2)}, u32[]{:S(2)}) collective-permute-start(bf16[1024,256]{1,0:T(8,128)(2,1)} %shard_map.123.refs_7_), channel_id=1, source_target_pairs={{0,8},{4,12},{8,0},{12,4},{1,9},{5,13},{9,1},{13,5},{2,10},{6,14},... | collective-permute-start | bytes 1572872 | tf_op jit(solution)/shard_map/ppermute | solution.py:335
  153.1 8.1 %copy-start.20 = (bf16[1024,256]{1,0:T(8,128)(2,1)}, bf16[1024,256]{1,0:T(8,128)(2,1)S(1)}, u32[]{:S(2)}) copy-start(bf16[1024,256]{1,0:T(8,128)(2,1)S(1)} %collective-permute-done.31.refs_1_) | copy-start | bytes 1572868
  158.3 3.4 %copy-start.10 = (bf16[128,4096]{1,0:T(8,128)(2,1)S(1)}, bf16[128,4096]{1,0:T(8,128)(2,1)}, u32[]{:S(2)}) copy-start(bf16[128,4096]{1,0:T(8,128)(2,1)} %copy-done.9) | copy-start | bytes 3145732
  161.2 17.9 %collective-permute-start.35 = (bf16[1024,256]{1,0:T(8,128)(2,1)}, bf16[1024,256]{1,0:T(8,128)(2,1)}, u32[]{:S(2)}, u32[]{:S(2)}) collective-permute-start(bf16[1024,256]{1,0:T(8,128)(2,1)} %get-tuple-element.83.refs_3_), channel_id=1, source_target_pairs={{0,16},{16,0},{1,17},{17,1},{2,18},{18,2},{3,19},{19,3},{4,20},{20... | collective-permute-start | bytes 1572872 | tf_op jit(solution)/shard_map/ppermute | solution.py:26
  163.5 1.6 copy-start.18
  166.6 3.1 %collective-permute-start.33 = (bf16[3,2048]{1,0:T(4,128)(2,1)S(1)}, bf16[3,2048]{1,0:T(4,128)(2,1)S(1)}, u32[]{:S(2)}, u32[]{:S(2)}) collective-permute-start(bf16[3,2048]{1,0:T(4,128)(2,1)S(1)} %reshape.78), channel_id=1, source_target_pairs={{1,0},{2,1},{3,2},{4,3},{5,4},{6,5},{7,6},{8,7},{9,8},{10,9},{11,1... | collective-permute-start | bytes 36872 | tf_op jit(solution)/shard_map/ppermute | solution.py:451
  173.8 5.2 %copy-start.1 = (f32[1,1024,1024]{2,1,0:T(8,128)S(1)}, f32[1,1024,1024]{2,1,0:T(8,128)}, u32[]{:S(2)}) copy-start(f32[1,1024,1024]{2,1,0:T(8,128)} %param.9) | copy-start | bytes 12582916
  173.8 5.3 %copy-start.3 = (f32[1,1024,1024]{2,1,0:T(8,128)S(1)}, f32[1,1024,1024]{2,1,0:T(8,128)}, u32[]{:S(2)}) copy-start(f32[1,1024,1024]{2,1,0:T(8,128)} %param.10) | copy-start | bytes 12582916
  173.8 5.3 %copy-start.5 = (f32[1,1024,1024]{2,1,0:T(8,128)S(1)}, f32[1,1024,1024]{2,1,0:T(8,128)}, u32[]{:S(2)}) copy-start(f32[1,1024,1024]{2,1,0:T(8,128)} %param.11) | copy-start | bytes 12582916
  177.2 1.8 copy-start.19
  179.1 17.6 %copy-start.21 = (bf16[1024,256]{1,0:T(8,128)(2,1)S(1)}, bf16[1024,256]{1,0:T(8,128)(2,1)}, u32[]{:S(2)}) copy-start(bf16[1024,256]{1,0:T(8,128)(2,1)} %copy-done.20) | copy-start | bytes 1572868
  179.1 17.6 %copy-start.23 = (bf16[1024,256]{1,0:T(8,128)(2,1)S(1)}, bf16[1024,256]{1,0:T(8,128)(2,1)}, u32[]{:S(2)}) copy-start(bf16[1024,256]{1,0:T(8,128)(2,1)} %copy-done.22) | copy-start | bytes 1572868
  183.3 13.4 %collective-permute-start.36 = (bf16[1024,256]{1,0:T(8,128)(2,1)S(1)}, bf16[1024,256]{1,0:T(8,128)(2,1)S(1)}, u32[]{:S(2)}, u32[]{:S(2)}) collective-permute-start(bf16[1024,256]{1,0:T(8,128)(2,1)S(1)} %get-tuple-element.91), channel_id=1, source_target_pairs={{0,16},{16,0},{1,17},{17,1},{2,18},{18,2},{3,19},{19,3},{4,20},{20... | collective-permute-start | bytes 1572872 | tf_op jit(solution)/shard_map/ppermute | solution.py:26
  (4 other events, 3.5 us)

commit v4 on v3

--- a/solution.py
+++ b/solution.py
@@ -148,6 +148,7 @@
             pl.BlockSpec((count, step), lambda i: (0, i)),
         ],
         after=after,
+        limit=46,
     )
 
 
@@ -398,16 +399,16 @@
 
     sums = {}
     sums[0], last = far_sums(0, [last])
-    *other_send, other_rest = act_products([other_rows, other_pair], [weights, pair_weights], [last])
+    near, to_seq = stack(
+        [[(0, 0, one), (2, 0, one)], [(1, 0, one), (2, one, one)]], own, to_seq, x_dp, after=[last]
+    )
+    *other_send, other_rest = act_products([other_rows, other_pair], [weights, pair_weights], [near])
     other_came = [swap(v, "mp", 2) for v in other_send]
     last = other_rest
 
     sums[1], last = far_sums(1, [last])
-    near, to_seq = stack(
-        [[(0, 0, one), (2, 0, one)], [(1, 0, one), (2, one, one)]], own, to_seq, x_dp, after=[last]
-    )
     x_seq = swap(to_seq, "seq", 1)
-    last = mark(SPANS[0], near, sums[0])
+    last = mark(SPANS[0], last, sums[0])
     (mine,) = stack([[(0, 0, 2 * one), (1, 0, 2 * one)]], near, x_seq, after=[last])
     across, beside = swap(mine, "mp", 2), swap(mine, "mp", 1)
     act_other = last_sum(other_rest, other_came, after=[mine])

time: 202 us -> 201 us (level)
  starting transfers between devices: 34.5 us -> 43 us
  waiting for transfers between devices: 86 us -> 78 us
  local copies, waits for them, and re-layouts: 14.5 us -> 11.5 us
  Pallas kernels: 63.5 us -> 66 us
    ppermute x4, waiting for transfers between devices: 19.6 us -> 5.13 us  [ahead(): lax.ppermute(v, 'seq', [(s, (s + 2 * k) % n_seq) for s in range(n_seq)])]
    ppermute x31, waiting for transfers between devices: 59.1 us -> 65.6 us  [swap(): return lax.ppermute(value, axis, [(i, i ^ step) for i in range(count)])]
    ppermute x4, starting transfers between devices: 3.71 us -> 8.21 us  [ahead(): lax.ppermute(v, 'seq', [(s, (s + 2 * k) % n_seq) for s in range(n_seq)])]
    ppermute x31, starting transfers between devices: 27.2 us -> 31.1 us  [swap(): return lax.ppermute(value, axis, [(i, i ^ step) for i in range(count)])]
    unnamed x62 -> x56, local copies, waits for them, and re-layouts: 14.2 us -> 11.3 us
    pallas_call x33, Pallas kernels: 63.5 us -> 66 us  [launch(): pl.pallas_call(body, grid_spec=pltpu.PrefetchScalarGridSpec(num_scalar_pr...]
  transfers between devices with their start and end apart: 37 -> 37, of which waited for: 20 -> 18; matrix products, arithmetic and copies ran while one was open for 0% -> 0% of each run, Pallas kernels for 28% -> 30%
where the time goes in v4:
time: 201 us; the launch traced here: 200 us
  waiting for transfers between devices  78 us (39%)
  Pallas kernels  66 us (33%)
  starting transfers between devices  43 us (21%)
  local copies, waits for them, and re-layouts  11.5 us (6%)
    pallas_call x33, Pallas kernels, launch(): pl.pallas_call(body, grid_spec=pltpu.PrefetchScalarGridSpec(num_scalar_pr...  66 us
    ppermute x31, waiting for transfers between devices, swap(): return lax.ppermute(value, axis, [(i, i ^ step) for i in range(count)])  65.6 us
    ppermute x31, starting transfers between devices, swap(): return lax.ppermute(value, axis, [(i, i ^ step) for i in range(count)])  31.1 us
    unnamed x56, local copies, waits for them, and re-layouts  11.3 us
    ppermute x4, starting transfers between devices, ahead(): lax.ppermute(v, 'seq', [(s, (s + 2 * k) % n_seq) for s in range(n_seq)])  8.21 us
    ppermute x1, waiting for transfers between devices, diagonal(): lax.ppermute(v, ('dp', 'seq'), [(i, i ^ n_seq ^ 1) for i in range(2 * n_s...  5.54 us
    ppermute x4, waiting for transfers between devices, ahead(): lax.ppermute(v, 'seq', [(s, (s + 2 * k) % n_seq) for s in range(n_seq)])  5.13 us
  transfers between devices with their start and end apart: 37, of which 18 were waited for; matrix products, arithmetic and copies ran while one was open for 0% of the time, Pallas kernels for 30%

profile of v4, /device:TPU:0, one launch (start us, length us, event | category | flops | bytes accessed | tf_op | source)
XLA Modules:
  0.0 199.6 jit_solution(13288197555115211612)
XLA Ops:
  1.2 1.2 copy-done.23
  3.4 1.8 copy-done.6
  5.2 1.3 shard_map.102
  6.5 2.6 %collective-permute-start.4 = (bf16[128,1024]{1,0:T(8,128)(2,1)S(1)}, bf16[128,1024]{1,0:T(8,128)(2,1)S(1)}, u32[]{:S(2)}, u32[]{:S(2)}) collective-permute-start(bf16[128,1024]{1,0:T(8,128)(2,1)S(1)} %get-tuple-element.54), channel_id=1, source_target_pairs={{0,16},{16,0},{1,17},{17,1},{2,18},{18,2},{3,19},{19,3},{4,20},{20... | collective-permute-start | bytes 786440 | tf_op jit(solution)/shard_map/ppermute | solution.py:26
  9.0 1.6 collective-permute-start.5
  11.2 5.0 %collective-permute-done.4.refs_1_ = bf16[128,1024]{1,0:T(8,128)(2,1)S(1)} collective-permute-done((bf16[128,1024]{1,0:T(8,128)(2,1)S(1)}, bf16[128,1024]{1,0:T(8,128)(2,1)S(1)}, u32[]{:S(2)}, u32[]{:S(2)}) %collective-permute-start.4) | collective-permute-done | bytes 262176 | tf_op jit(solution)/shard_map/ppermute | solution.py:26
  16.2 1.3 collective-permute-done.5.refs_2_
  17.5 1.6 collective-permute-start.12
  19.8 2.4 %collective-permute-start.6 = (bf16[128,1024]{1,0:T(8,128)(2,1)S(1)}, bf16[128,1024]{1,0:T(8,128)(2,1)S(1)}, u32[]{:S(2)}, u32[]{:S(2)}) collective-permute-start(bf16[128,1024]{1,0:T(8,128)(2,1)S(1)} %get-tuple-element.56), channel_id=1, source_target_pairs={{0,20},{4,16},{8,28},{12,24},{16,4},{20,0},{24,12},{28,8},{1,21},{... | collective-permute-start | bytes 786440 | tf_op jit(solution)/shard_map/ppermute | solution.py:333
  22.2 5.5 %collective-permute-done.6.refs_4_.refs_7_ = bf16[128,1024]{1,0:T(8,128)(2,1)S(1)} collective-permute-done((bf16[128,1024]{1,0:T(8,128)(2,1)S(1)}, bf16[128,1024]{1,0:T(8,128)(2,1)S(1)}, u32[]{:S(2)}, u32[]{:S(2)}) %collective-permute-start.6) | collective-permute-done | bytes 262176 | tf_op jit(solution)/shard_map/ppermute | solution.py:333
  27.8 0.9 copy-done.11
  29.6 1.8 collective-permute-start.7
  31.5 5.0 %collective-permute-done.12.refs_4_ = bf16[384,1024]{1,0:T(8,128)(2,1)} collective-permute-done((bf16[384,1024]{1,0:T(8,128)(2,1)S(1)}, bf16[384,1024]{1,0:T(8,128)(2,1)}, u32[]{:S(2)}, u32[]{:S(2)}) %collective-permute-start.12) | collective-permute-done | bytes 786464 | tf_op jit(solution)/shard_map/ppermute | solution.py:26
  36.6 1.6 collective-permute-start.14
  38.2 5.9 %collective-permute-done.3.refs_2_.refs_9_.refs_5_ = bf16[512,768]{1,0:T(8,128)(2,1)S(1)} collective-permute-done((bf16[512,768]{1,0:T(8,128)(2,1)S(1)}, bf16[512,768]{1,0:T(8,128)(2,1)S(1)}, u32[]{:S(2)}, u32[]{:S(2)}) %collective-permute-start.3) | collective-permute-done | bytes 786464 | tf_op jit(solution)/shard_map/ppermute | solution.py:26
  44.2 0.9 copy-done.14
  45.3 1.3 shard_map.106
  46.6 1.7 collective-permute-start.11
  48.9 1.6 collective-permute-start.19
  50.5 2.9 %shard_map.107.refs_3_ = bf16[1024,256]{1,0:T(8,128)(2,1)S(1)} custom-call(bf16[384,1024]{1,0:T(8,128)(2,1)} %collective-permute-done.13.refs_0_, bf16[128,1024]{1,0:T(8,128)(2,1)S(1)} %collective-permute-done.15.refs_1_, bf16[384,1024]{1,0:T(8,128)(2,1)S(1)} %collective-permute-done.8.refs_5_.refs_2_, ...), custom_call_target="tpu_custom_call" | custom-call | flops 1 | bytes 1 | tf_op jit(solution)/shard_map/pallas_call | solution.py:36
  53.4 2.7 %collective-permute-start.20 = (bf16[1024,256]{1,0:T(8,128)(2,1)S(1)}, bf16[1024,256]{1,0:T(8,128)(2,1)S(1)}, u32[]{:S(2)}, u32[]{:S(2)}) collective-permute-start(bf16[1024,256]{1,0:T(8,128)(2,1)S(1)} %shard_map.107.refs_3_), channel_id=1, source_target_pairs={{0,8},{4,12},{8,0},{12,4},{1,9},{5,13},{9,1},{13,5},{2,10},{6,14},... | collective-permute-start | bytes 1572872 | tf_op jit(solution)/shard_map/ppermute | solution.py:336
  56.1 4.2 %collective-permute-done.11.refs_2_ = bf16[256,1024]{1,0:T(8,128)(2,1)S(1)} collective-permute-done((bf16[256,1024]{1,0:T(8,128)(2,1)S(1)}, bf16[256,1024]{1,0:T(8,128)(2,1)S(1)}, u32[]{:S(2)}, u32[]{:S(2)}) %collective-permute-start.11) | collective-permute-done | bytes 524320 | tf_op jit(solution)/shard_map/ppermute | solution.py:26
  60.3 1.9 collective-permute-start.18
  62.2 10.7 %shard_map.109 = (bf16[128,2048]{1,0:T(8,128)(2,1)S(1)}, bf16[128,2048]{1,0:T(8,128)(2,1)S(1)}, f32[128,4096]{1,0:T(8,128)S(1)}) custom-call(bf16[256,1024]{1,0:T(8,128)(2,1)S(1)} %get-tuple-element.57.refs_2_.refs_0_, bf16[256,1024]{1,0:T(8,128)(2,1)S(1)} %collective-permute-done.10.refs_1_, bf16[4096,1024]{1,0:T(8,128)(2,1)} %bitcast.48, ...), custom_call_target="tpu_custom_call" | custom-call | flops 1 | bytes 1 | tf_op jit(solution)/shard_map/pallas_call | solution.py:36
  72.9 1.6 collective-permute-start.16
  75.0 2.8 %shard_map.110.refs_0_ = bf16[1024,256]{1,0:T(8,128)(2,1)S(1)} custom-call(bf16[384,1024]{1,0:T(8,128)(2,1)} %collective-permute-done.13.refs_0_, bf16[128,1024]{1,0:T(8,128)(2,1)S(1)} %collective-permute-done.15.refs_1_, bf16[384,1024]{1,0:T(8,128)(2,1)S(1)} %collective-permute-done.8.refs_5_.refs_2_, ...), custom_call_target="tpu_custom_call" | custom-call | flops 1 | bytes 1 | tf_op jit(solution)/shard_map/pallas_call | solution.py:36
  77.9 1.5 collective-permute-done.20.refs_1_.refs_2_
  79.9 6.2 %collective-permute-done.18.refs_1_ = bf16[256,1024]{1,0:T(8,128)(2,1)S(1)} collective-permute-done((bf16[256,1024]{1,0:T(8,128)(2,1)S(1)}, bf16[256,1024]{1,0:T(8,128)(2,1)S(1)}, u32[]{:S(2)}, u32[]{:S(2)}) %collective-permute-start.18) | collective-permute-done | bytes 524320 | tf_op jit(solution)/shard_map/ppermute | solution.py:26
  86.1 2.6 %collective-permute-start.24 = (bf16[1024,256]{1,0:T(8,128)(2,1)S(1)}, bf16[1024,256]{1,0:T(8,128)(2,1)S(1)}, u32[]{:S(2)}, u32[]{:S(2)}) collective-permute-start(bf16[1024,256]{1,0:T(8,128)(2,1)S(1)} %shard_map.110.refs_0_), channel_id=1, source_target_pairs={{0,8},{4,12},{8,0},{12,4},{1,9},{5,13},{9,1},{13,5},{2,10},{6,14},... | collective-permute-start | bytes 1572872 | tf_op jit(solution)/shard_map/ppermute | solution.py:336
  88.8 1.6 collective-permute-start.23
  90.4 8.7 %collective-permute-done.17.refs_2_ = bf16[128,2048]{1,0:T(8,128)(2,1)S(1)} collective-permute-done((bf16[128,2048]{1,0:T(8,128)(2,1)S(1)}, bf16[128,2048]{1,0:T(8,128)(2,1)S(1)}, u32[]{:S(2)}, u32[]{:S(2)}) %collective-permute-start.17) | collective-permute-done | bytes 524320 | tf_op jit(solution)/shard_map/ppermute | solution.py:26
  99.3 1.6 collective-permute-start.26
  100.9 11.4 %shard_map.114 = (bf16[128,2048]{1,0:T(8,128)(2,1)}, bf16[128,2048]{1,0:T(8,128)(2,1)}, f32[128,4096]{1,0:T(8,128)S(1)}) custom-call(bf16[256,1024]{1,0:T(8,128)(2,1)S(1)} %copy-done.25, bf16[256,1024]{1,0:T(8,128)(2,1)S(1)} %collective-permute-done.refs_1_, bf16[4096,1024]{1,0:T(8,128)(2,1)} %bitcast.49, bf16[4096,1024]{1,0:T(8,128)(2,1)} %collective-permute-done.1.refs_3_, ...), custom_call_target="tpu_custom_call" | custom-call | flops 1 | bytes 1 | tf_op jit(solution)/shard_map/pallas_call | solution.py:36
  112.3 1.3 copy-done.16
  113.5 5.6 %collective-permute-done.23.refs_0_ = bf16[512,1024]{1,0:T(8,128)(2,1)S(1)} collective-permute-done((bf16[512,1024]{1,0:T(8,128)(2,1)S(1)}, bf16[512,1024]{1,0:T(8,128)(2,1)S(1)}, u32[]{:S(2)}, u32[]{:S(2)}) %collective-permute-start.23) | collective-permute-done | bytes 1048608 | tf_op jit(solution)/shard_map/ppermute | solution.py:26
  119.8 1.0 copy-done.8
  121.3 2.9 %shard_map.117.refs_7_ = bf16[1024,256]{1,0:T(8,128)(2,1)S(1)} custom-call(bf16[384,1024]{1,0:T(8,128)(2,1)} %collective-permute-done.13.refs_0_, bf16[128,1024]{1,0:T(8,128)(2,1)S(1)} %collective-permute-done.15.refs_1_, bf16[384,1024]{1,0:T(8,128)(2,1)S(1)} %collective-permute-done.8.refs_5_.refs_2_, ...), custom_call_target="tpu_custom_call" | custom-call | flops 1 | bytes 1 | tf_op jit(solution)/shard_map/pallas_call | solution.py:36
  124.3 2.8 %collective-permute-start.29 = (bf16[1024,256]{1,0:T(8,128)(2,1)S(1)}, bf16[1024,256]{1,0:T(8,128)(2,1)S(1)}, u32[]{:S(2)}, u32[]{:S(2)}) collective-permute-start(bf16[1024,256]{1,0:T(8,128)(2,1)S(1)} %shard_map.117.refs_7_), channel_id=1, source_target_pairs={{0,8},{4,12},{8,0},{12,4},{1,9},{5,13},{9,1},{13,5},{2,10},{6,14},... | collective-permute-start | bytes 1572872 | tf_op jit(solution)/shard_map/ppermute | solution.py:336
  127.1 2.4 %shard_map.118.refs_1_ = f32[1024,256]{1,0:T(8,128)S(1)} custom-call(bf16[512,1024]{1,0:T(8,128)(2,1)S(1)} %collective-permute-done.28.refs_0_, bf16[512,1024]{1,0:T(8,128)(2,1)S(1)} %collective-permute-done.27.refs_3_.refs_1_, bf16[512,1024]{1,0:T(8,128)(2,1)S(1)} %shard_map.116.refs_11_.refs_2_, bf16[512,1024]{1,0:T(8,128)(2,1)S(1)} %shard_map.112.refs_3_, ...), custom_call_target="tpu_custom_call" | custom-call | flops 1 | bytes 1 | tf_op jit(solution)/shard_map/pallas_call | solution.py:36
  129.6 2.8 %shard_map.119 = (f32[1024,1024]{1,0:T(8,128)}, f32[1024,1024]{1,0:T(8,128)}, f32[1024,1024]{1,0:T(8,128)}, bf16[2,1024,1024]{2,1,0:T(8,128)(2,1)}, bf16[1024,256]{1,0:T(8,128)(2,1)S(1)}) custom-call(s32[1]{0:T(128)} %bitcast.refs_0_, f32[1024,256]{1,0:T(8,128)S(1)} %shard_map.118.refs_1_, bf16[1024,256]{1,0:T(8,128)(2,1)S(1)} %collective-permute-done.20.refs_1_.refs_2_, ...), custom_call_target="tpu_custom_call" | custom-call | flops 1 | bytes 1 | tf_op jit(solution)/shard_map/pallas_call | solution.py:36
  132.3 1.4 collective-permute-start.31
  133.8 1.4 shard_map.120.refs_1_
  135.1 2.8 %shard_map.121 = (f32[1024,1024]{1,0:T(8,128)}, f32[1024,1024]{1,0:T(8,128)}, f32[1024,1024]{1,0:T(8,128)}, bf16[2,1024,1024]{2,1,0:T(8,128)(2,1)}, bf16[1024,256]{1,0:T(8,128)(2,1)S(1)}) custom-call(s32[1]{0:T(128)} %bitcast.refs_0_, f32[1024,256]{1,0:T(8,128)S(1)} %shard_map.120.refs_1_, ...), custom_call_target="tpu_custom_call", output_to_operand_aliasing={{0}: (6, {}), {1}: (7, {}), {2}: (8, {}), {3}: (9, {})} | custom-call | flops 1 | bytes 1 | tf_op jit(solution)/shard_map/pallas_call | solution.py:36
  138.5 1.4 collective-permute-start.21
  139.9 4.3 %collective-permute-done.30.refs_10_.refs_6_ = bf16[1024,256]{1,0:T(8,128)(2,1)S(1)} collective-permute-done((bf16[1024,256]{1,0:T(8,128)(2,1)S(1)}, bf16[1024,256]{1,0:T(8,128)(2,1)S(1)}, u32[]{:S(2)}, u32[]{:S(2)}) %collective-permute-start.30) | collective-permute-done | bytes 524320 | tf_op jit(solution)/shard_map/ppermute | solution.py:26
  144.2 1.6 collective-permute-start.22
  145.7 1.4 shard_map.122.refs_11_.refs_1_
  147.1 3.6 %shard_map.123.refs_7_ = bf16[1024,256]{1,0:T(8,128)(2,1)} custom-call(bf16[384,1024]{1,0:T(8,128)(2,1)} %collective-permute-done.13.refs_0_, bf16[128,1024]{1,0:T(8,128)(2,1)S(1)} %collective-permute-done.15.refs_1_, bf16[384,1024]{1,0:T(8,128)(2,1)S(1)} %collective-permute-done.8.refs_5_.refs_2_, bf16[128,1024]{1,0:T(8,128)(2,1)} %collective-permute-done.9.refs_6_.refs_3_, ...), custom_call_target="tpu_custom_call" | custom-call | flops 1 | bytes 1 | tf_op jit(solution)/shard_map/pallas_call | solution.py:36
  150.7 1.4 shard_map.124.refs_0_.refs_1_
  152.2 5.1 %collective-permute-done.32.refs_2_ = bf16[1024,256]{1,0:T(8,128)(2,1)S(1)} collective-permute-done((bf16[1024,256]{1,0:T(8,128)(2,1)S(1)}, bf16[1024,256]{1,0:T(8,128)(2,1)S(1)}, u32[]{:S(2)}, u32[]{:S(2)}) %collective-permute-start.32) | collective-permute-done | bytes 524320 | tf_op jit(solution)/shard_map/ppermute | solution.py:26
  157.4 2.9 %shard_map.127 = (f32[1024,1024]{1,0:T(8,128)}, f32[1024,1024]{1,0:T(8,128)}, f32[1024,1024]{1,0:T(8,128)}, bf16[2,1024,1024]{2,1,0:T(8,128)(2,1)}, bf16[1024,256]{1,0:T(8,128)(2,1)}) custom-call(s32[1]{0:T(128)} %bitcast.refs_0_, ...), custom_call_target="tpu_custom_call", output_to_operand_aliasing={{0}: (6, {}), {1}: (7, {}), {2}: (8, {}), {3}: (9, {})} | custom-call | flops 1 | bytes 1 | tf_op jit(solution)/shard_map/pallas_call | solution.py:36
  160.2 1.5 collective-permute-start.35
  161.8 1.5 collective-permute-done.22.refs_2_
  163.3 1.6 copy-done.17
  164.9 1.4 shard_map.128.refs_1_
  166.4 1.3 collective-permute-start.33
  167.7 1.8 collective-permute-done.33
  169.5 4.2 %shard_map.129.refs_0_ = bf16[512,2048]{1,0:T(8,128)(2,1)} custom-call(s32[1]{0:T(128)} %bitcast.refs_0_, bf16[128,4096]{1,0:T(8,128)(2,1)S(1)} %shard_map.128.refs_1_, bf16[128,4096]{1,0:T(8,128)(2,1)S(1)} %copy-done.9, bf16[16,2048]{1,0:T(8,128)(2,1)S(1)} %pad.4.refs_3_), custom_call_target="tpu_custom_call" | custom-call | flops 1 | bytes 1 | tf_op jit(solution)/shard_map/pallas_call | solution.py:36
  173.7 3.7 %collective-permute-done.34.refs_1_.refs_2_ = bf16[1024,256]{1,0:T(8,128)(2,1)} collective-permute-done((bf16[1024,256]{1,0:T(8,128)(2,1)}, bf16[1024,256]{1,0:T(8,128)(2,1)}, u32[]{:S(2)}, u32[]{:S(2)}) %collective-permute-start.34) | collective-permute-done | bytes 524320 | tf_op jit(solution)/shard_map/ppermute | solution.py:336
  177.3 1.6 copy-done.18
  179.0 4.1 %shard_map.132 = (f32[1024,1024]{1,0:T(8,128)}, f32[1024,1024]{1,0:T(8,128)}, f32[1024,1024]{1,0:T(8,128)}, bf16[2,1024,1024]{2,1,0:T(8,128)(2,1)}, bf16[1024,256]{1,0:T(8,128)(2,1)S(1)}) custom-call(s32[1]{0:T(128)} %bitcast.refs_0_, ...), custom_call_target="tpu_custom_call", output_to_operand_aliasing={{0}: (6, {}), {1}: (7, {}), {2}: (8, {}), {3}: (9, {})} | custom-call | flops 1 | bytes 1 | tf_op jit(solution)/shard_map/pallas_call | solution.py:36
  183.1 1.4 collective-permute-start.36
  184.5 12.2 %collective-permute-done.36.refs_4_ = bf16[1024,256]{1,0:T(8,128)(2,1)S(1)} collective-permute-done((bf16[1024,256]{1,0:T(8,128)(2,1)S(1)}, bf16[1024,256]{1,0:T(8,128)(2,1)S(1)}, u32[]{:S(2)}, u32[]{:S(2)}) %collective-permute-start.36) | collective-permute-done | bytes 524320 | tf_op jit(solution)/shard_map/ppermute | solution.py:26
  196.7 2.9 %shard_map.133 = bf16[2,1024,1024]{2,1,0:T(8,128)(2,1)} custom-call(s32[1]{0:T(128)} %bitcast.refs_0_, bf16[1024,256]{1,0:T(8,128)(2,1)S(1)} %copy-done.20, bf16[1024,256]{1,0:T(8,128)(2,1)S(1)} %copy-done.22, bf16[1024,256]{1,0:T(8,128)(2,1)} %collective-permute-done.35.refs_1_.refs_3_, ...), custom_call_target="tpu_custom_call", output_to_operand_aliasing={{}: (5, {})} | custom-call | flops 1 | bytes 1 | tf_op jit(solution)/shard_map/pallas_call | solution.py:36
  (106 shorter events, 8.2 us)
Async XLA Ops:
  0.6 27.1 %collective-permute-start.1 = (bf16[4096,1024]{1,0:T(8,128)(2,1)}, bf16[4096,1024]{1,0:T(8,128)(2,1)}, u32[]{:S(2)}, u32[]{:S(2)}) collective-permute-start(bf16[4096,1024]{1,0:T(8,128)(2,1)} %bitcast.47), channel_id=1, source_target_pairs={{0,1},{1,0},{2,3},{3,2},{4,5},{5,4},{6,7},{7,6},{8,9},{9,8},{10,11... | collective-permute-start | bytes 25165832 | tf_op jit(solution)/shard_map/ppermute | solution.py:26
  1.1 1.2 copy-start.23
  3.3 15.8 %copy-start.24 = (bf16[256,1024]{1,0:T(8,128)(2,1)}, bf16[256,1024]{1,0:T(8,128)(2,1)S(1)}, u32[]{:S(2)}) copy-start(bf16[256,1024]{1,0:T(8,128)(2,1)S(1)} %get-tuple-element.49.refs_0_) | copy-start | bytes 1572868
  3.3 18.8 %copy-start.10 = (bf16[512,256]{1,0:T(8,128)(2,1)}, bf16[512,256]{1,0:T(8,128)(2,1)S(1)}, u32[]{:S(2)}) copy-start(bf16[512,256]{1,0:T(8,128)(2,1)S(1)} %get-tuple-element.52.refs_2_.refs_0_.refs_8_.refs_4_) | copy-start | bytes 786436
  3.4 1.8 copy-start.6
  6.5 9.7 %collective-permute-start.4 = (bf16[128,1024]{1,0:T(8,128)(2,1)S(1)}, bf16[128,1024]{1,0:T(8,128)(2,1)S(1)}, u32[]{:S(2)}, u32[]{:S(2)}) collective-permute-start(bf16[128,1024]{1,0:T(8,128)(2,1)S(1)} %get-tuple-element.54), channel_id=1, source_target_pairs={{0,16},{16,0},{1,17},{17,1},{2,18},{18,2},{3,19},{19,3},{4,20},{20... | collective-permute-start | bytes 786440 | tf_op jit(solution)/shard_map/ppermute | solution.py:26
  9.0 8.4 %collective-permute-start.5 = (bf16[128,1024]{1,0:T(8,128)(2,1)S(1)}, bf16[128,1024]{1,0:T(8,128)(2,1)S(1)}, u32[]{:S(2)}, u32[]{:S(2)}) collective-permute-start(bf16[128,1024]{1,0:T(8,128)(2,1)S(1)} %get-tuple-element.55), channel_id=1, source_target_pairs={{0,4},{4,0},{8,12},{12,8},{1,5},{5,1},{9,13},{13,9},{2,6},{6,2},{1... | collective-permute-start | bytes 786440 | tf_op jit(solution)/shard_map/ppermute | solution.py:26
  10.6 11.5 %collective-permute-start.2 = (bf16[512,256]{1,0:T(8,128)(2,1)S(1)}, bf16[512,256]{1,0:T(8,128)(2,1)S(1)}, u32[]{:S(2)}, u32[]{:S(2)}) collective-permute-start(bf16[512,256]{1,0:T(8,128)(2,1)S(1)} %get-tuple-element.52.refs_2_.refs_0_.refs_8_.refs_4_), channel_id=1, source_target_pairs={{0,16},{16,0},{1,17},{17,1},{2,18},{18,2},{3,19},{19,3},{4,20},{20... | collective-permute-start | bytes 786440 | tf_op jit(solution)/shard_map/ppermute | solution.py:26
  17.5 19.0 %collective-permute-start.12 = (bf16[384,1024]{1,0:T(8,128)(2,1)S(1)}, bf16[384,1024]{1,0:T(8,128)(2,1)}, u32[]{:S(2)}, u32[]{:S(2)}) collective-permute-start(bf16[384,1024]{1,0:T(8,128)(2,1)S(1)} %shard_map.103.refs_2_.refs_6_), channel_id=1, source_target_pairs={{0,2},{1,3},{2,0},{3,1},{4,6},{5,7},{6,4},{7,5},{8,10},{9,11},{10,... | collective-permute-start | bytes 2359304 | tf_op jit(solution)/shard_map/ppermute | solution.py:26
  19.1 25.0 %collective-permute-start.3 = (bf16[512,768]{1,0:T(8,128)(2,1)S(1)}, bf16[512,768]{1,0:T(8,128)(2,1)S(1)}, u32[]{:S(2)}, u32[]{:S(2)}) collective-permute-start(bf16[512,768]{1,0:T(8,128)(2,1)S(1)} %get-tuple-element.51.refs_0_.refs_8_.refs_4_), channel_id=1, source_target_pairs={{0,16},{16,0},{1,17},{17,1},{2,18},{18,2},{3,19},{19,3},{4,20},{20... | collective-permute-start | bytes 2359304 | tf_op jit(solution)/shard_map/ppermute | solution.py:26
  19.8 8.0 %collective-permute-start.6 = (bf16[128,1024]{1,0:T(8,128)(2,1)S(1)}, bf16[128,1024]{1,0:T(8,128)(2,1)S(1)}, u32[]{:S(2)}, u32[]{:S(2)}) collective-permute-start(bf16[128,1024]{1,0:T(8,128)(2,1)S(1)} %get-tuple-element.56), channel_id=1, source_target_pairs={{0,20},{4,16},{8,28},{12,24},{16,4},{20,0},{24,12},{28,8},{1,21},{... | collective-permute-start | bytes 786440 | tf_op jit(solution)/shard_map/ppermute | solution.py:333
  22.2 7.4 %copy-start.13 = (bf16[512,256]{1,0:T(8,128)(2,1)}, bf16[512,256]{1,0:T(8,128)(2,1)S(1)}, u32[]{:S(2)}) copy-start(bf16[512,256]{1,0:T(8,128)(2,1)S(1)} %collective-permute-done.2.refs_1_.refs_9_.refs_5_) | copy-start | bytes 786436
  22.2 21.9 %collective-permute-start.8 = (bf16[384,1024]{1,0:T(8,128)(2,1)S(1)}, bf16[384,1024]{1,0:T(8,128)(2,1)S(1)}, u32[]{:S(2)}, u32[]{:S(2)}) collective-permute-start(bf16[384,1024]{1,0:T(8,128)(2,1)S(1)} %shard_map.103.refs_2_.refs_6_), channel_id=1, source_target_pairs={{0,1},{1,0},{2,3},{3,2},{4,5},{5,4},{6,7},{7,6},{8,9},{9,8},{10,11... | collective-permute-start | bytes 2359304 | tf_op jit(solution)/shard_map/ppermute | solution.py:26
  27.8 1.0 copy-start.11
  29.6 14.6 %collective-permute-start.7 = (bf16[1024,256]{1,0:T(8,128)(2,1)}, bf16[1024,256]{1,0:T(8,128)(2,1)}, u32[]{:S(2)}, u32[]{:S(2)}) collective-permute-start(bf16[1024,256]{1,0:T(8,128)(2,1)} %shard_map.104.refs_3_), channel_id=1, source_target_pairs={{0,4},{4,0},{8,12},{12,8},{1,5},{5,1},{9,13},{13,9},{2,6},{6,2},{1... | collective-permute-start | bytes 1572872 | tf_op jit(solution)/shard_map/ppermute | solution.py:26
  31.4 5.3 %collective-permute-start.9 = (bf16[128,1024]{1,0:T(8,128)(2,1)S(1)}, bf16[128,1024]{1,0:T(8,128)(2,1)}, u32[]{:S(2)}, u32[]{:S(2)}) collective-permute-start(bf16[128,1024]{1,0:T(8,128)(2,1)S(1)} %collective-permute-done.6.refs_4_.refs_7_), channel_id=1, source_target_pairs={{0,1},{1,0},{2,3},{3,2},{4,5},{5,4},{6,7},{7,6},{8,9},{9,8},{10,11... | collective-permute-start | bytes 786440 | tf_op jit(solution)/shard_map/ppermute | solution.py:26
  36.5 13.9 %collective-permute-start.13 = (bf16[384,1024]{1,0:T(8,128)(2,1)}, bf16[384,1024]{1,0:T(8,128)(2,1)}, u32[]{:S(2)}, u32[]{:S(2)}) collective-permute-start(bf16[384,1024]{1,0:T(8,128)(2,1)} %collective-permute-done.12.refs_4_), channel_id=1, source_target_pairs={{0,1},{1,0},{2,3},{3,2},{4,5},{5,4},{6,7},{7,6},{8,9},{9,8},{10,11... | collective-permute-start | bytes 2359304 | tf_op jit(solution)/shard_map/ppermute | solution.py:26
  36.6 8.7 %copy-start.7 = (bf16[1,512,2048]{2,1,0:T(8,128)(2,1)S(1)}, bf16[1,512,2048]{2,1,0:T(8,128)(2,1)}, u32[]{:S(2)}) copy-start(bf16[1,512,2048]{2,1,0:T(8,128)(2,1)} %param.6) | copy-start | bytes 6291460
  36.6 13.8 %copy-start.12 = (bf16[512,256]{1,0:T(8,128)(2,1)S(1)}, bf16[512,256]{1,0:T(8,128)(2,1)}, u32[]{:S(2)}) copy-start(bf16[512,256]{1,0:T(8,128)(2,1)} %copy-done.10) | copy-start | bytes 786436
  36.6 11.7 %collective-permute-start.14 = (bf16[128,1024]{1,0:T(8,128)(2,1)S(1)}, bf16[128,1024]{1,0:T(8,128)(2,1)S(1)}, u32[]{:S(2)}, u32[]{:S(2)}) collective-permute-start(bf16[128,1024]{1,0:T(8,128)(2,1)S(1)} %collective-permute-done.6.refs_4_.refs_7_), channel_id=1, source_target_pairs={{0,2},{1,3},{2,0},{3,1},{4,6},{5,7},{6,4},{7,5},{8,10},{9,11},{10,... | collective-permute-start | bytes 786440 | tf_op jit(solution)/shard_map/ppermute | solution.py:26
  44.2 1.0 copy-start.14
  45.1 5.3 %copy-start.15 = (bf16[512,256]{1,0:T(8,128)(2,1)S(1)}, bf16[512,256]{1,0:T(8,128)(2,1)}, u32[]{:S(2)}) copy-start(bf16[512,256]{1,0:T(8,128)(2,1)} %copy-done.13) | copy-start | bytes 786436
  46.6 13.6 %collective-permute-start.11 = (bf16[256,1024]{1,0:T(8,128)(2,1)S(1)}, bf16[256,1024]{1,0:T(8,128)(2,1)S(1)}, u32[]{:S(2)}, u32[]{:S(2)}) collective-permute-start(bf16[256,1024]{1,0:T(8,128)(2,1)S(1)} %get-tuple-element.61), channel_id=1, source_target_pairs={{0,16},{16,0},{1,17},{17,1},{2,18},{18,2},{3,19},{19,3},{4,20},{20... | collective-permute-start | bytes 1572872 | tf_op jit(solution)/shard_map/ppermute | solution.py:26
  48.3 2.1 %collective-permute-start.15 = (bf16[128,1024]{1,0:T(8,128)(2,1)S(1)}, bf16[128,1024]{1,0:T(8,128)(2,1)S(1)}, u32[]{:S(2)}, u32[]{:S(2)}) collective-permute-start(bf16[128,1024]{1,0:T(8,128)(2,1)S(1)} %collective-permute-done.14.refs_5_), channel_id=1, source_target_pairs={{0,1},{1,0},{2,3},{3,2},{4,5},{5,4},{6,7},{7,6},{8,9},{9,8},{10,11... | collective-permute-start | bytes 786440 | tf_op jit(solution)/shard_map/ppermute | solution.py:26
  48.4 13.8 %collective-permute-start.10 = (bf16[256,1024]{1,0:T(8,128)(2,1)S(1)}, bf16[256,1024]{1,0:T(8,128)(2,1)S(1)}, u32[]{:S(2)}, u32[]{:S(2)}) collective-permute-start(bf16[256,1024]{1,0:T(8,128)(2,1)S(1)} %get-tuple-element.58), channel_id=1, source_target_pairs={{0,1},{1,0},{2,3},{3,2},{4,5},{5,4},{6,7},{7,6},{8,9},{9,8},{10,11... | collective-permute-start | bytes 1572872 | tf_op jit(solution)/shard_map/ppermute | solution.py:26
  48.9 26.2 %collective-permute-start.19 = (bf16[1024,256]{1,0:T(8,128)(2,1)S(1)}, bf16[1024,256]{1,0:T(8,128)(2,1)S(1)}, u32[]{:S(2)}, u32[]{:S(2)}) collective-permute-start(bf16[1024,256]{1,0:T(8,128)(2,1)S(1)} %get-tuple-element.67), channel_id=1, source_target_pairs={{0,4},{4,0},{8,12},{12,8},{1,5},{5,1},{9,13},{13,9},{2,6},{6,2},{1... | collective-permute-start | bytes 1572872 | tf_op jit(solution)/shard_map/ppermute | solution.py:26
  53.4 25.9 %collective-permute-start.20 = (bf16[1024,256]{1,0:T(8,128)(2,1)S(1)}, bf16[1024,256]{1,0:T(8,128)(2,1)S(1)}, u32[]{:S(2)}, u32[]{:S(2)}) collective-permute-start(bf16[1024,256]{1,0:T(8,128)(2,1)S(1)} %shard_map.107.refs_3_), channel_id=1, source_target_pairs={{0,8},{4,12},{8,0},{12,4},{1,9},{5,13},{9,1},{13,5},{2,10},{6,14},... | collective-permute-start | bytes 1572872 | tf_op jit(solution)/shard_map/ppermute | solution.py:336
  60.3 25.8 %collective-permute-start.18 = (bf16[256,1024]{1,0:T(8,128)(2,1)S(1)}, bf16[256,1024]{1,0:T(8,128)(2,1)S(1)}, u32[]{:S(2)}, u32[]{:S(2)}) collective-permute-start(bf16[256,1024]{1,0:T(8,128)(2,1)S(1)} %get-tuple-element.66), channel_id=1, source_target_pairs={{0,4},{4,0},{8,12},{12,8},{1,5},{5,1},{9,13},{13,9},{2,6},{6,2},{1... | collective-permute-start | bytes 1572872 | tf_op jit(solution)/shard_map/ppermute | solution.py:26
  62.2 12.8 %copy-start.27 = (bf16[256,1024]{1,0:T(8,128)(2,1)S(1)}, bf16[256,1024]{1,0:T(8,128)(2,1)}, u32[]{:S(2)}) copy-start(bf16[256,1024]{1,0:T(8,128)(2,1)} %copy-done.26) | copy-start | bytes 1572868
  72.9 15.9 %collective-permute-start.16 = (bf16[128,2048]{1,0:T(8,128)(2,1)S(1)}, bf16[128,2048]{1,0:T(8,128)(2,1)S(1)}, u32[]{:S(2)}, u32[]{:S(2)}) collective-permute-start(bf16[128,2048]{1,0:T(8,128)(2,1)S(1)} %get-tuple-element.64), channel_id=1, source_target_pairs={{0,2},{1,3},{2,0},{3,1},{4,6},{5,7},{6,4},{7,5},{8,10},{9,11},{10,... | collective-permute-start | bytes 1572872 | tf_op jit(solution)/shard_map/ppermute | solution.py:26
  74.5 24.6 %collective-permute-start.17 = (bf16[128,2048]{1,0:T(8,128)(2,1)S(1)}, bf16[128,2048]{1,0:T(8,128)(2,1)S(1)}, u32[]{:S(2)}, u32[]{:S(2)}) collective-permute-start(bf16[128,2048]{1,0:T(8,128)(2,1)S(1)} %get-tuple-element.65), channel_id=1, source_target_pairs={{0,2},{1,3},{2,0},{3,1},{4,6},{5,7},{6,4},{7,5},{8,10},{9,11},{10,... | collective-permute-start | bytes 1572872 | tf_op jit(solution)/shard_map/ppermute | solution.py:26
  75.0 25.8 %collective-permute-start = (bf16[256,1024]{1,0:T(8,128)(2,1)S(1)}, bf16[256,1024]{1,0:T(8,128)(2,1)S(1)}, u32[]{:S(2)}, u32[]{:S(2)}) collective-permute-start(bf16[256,1024]{1,0:T(8,128)(2,1)S(1)} %copy-done.27), channel_id=1, source_target_pairs={{0,1},{1,0},{2,3},{3,2},{4,5},{5,4},{6,7},{7,6},{8,9},{9,8},{10,11... | collective-permute-start | bytes 1572872 | tf_op jit(solution)/shard_map/ppermute | solution.py:26
  79.3 32.9 %collective-permute-start.25 = (bf16[1024,256]{1,0:T(8,128)(2,1)S(1)}, bf16[1024,256]{1,0:T(8,128)(2,1)S(1)}, u32[]{:S(2)}, u32[]{:S(2)}) collective-permute-start(bf16[1024,256]{1,0:T(8,128)(2,1)S(1)} %get-tuple-element.71), channel_id=1, source_target_pairs={{0,4},{4,0},{8,12},{12,8},{1,5},{5,1},{9,13},{13,9},{2,6},{6,2},{1... | collective-permute-start | bytes 1572872 | tf_op jit(solution)/shard_map/ppermute | solution.py:26
  86.1 26.1 %collective-permute-start.24 = (bf16[1024,256]{1,0:T(8,128)(2,1)S(1)}, bf16[1024,256]{1,0:T(8,128)(2,1)S(1)}, u32[]{:S(2)}, u32[]{:S(2)}) collective-permute-start(bf16[1024,256]{1,0:T(8,128)(2,1)S(1)} %shard_map.110.refs_0_), channel_id=1, source_target_pairs={{0,8},{4,12},{8,0},{12,4},{1,9},{5,13},{9,1},{13,5},{2,10},{6,14},... | collective-permute-start | bytes 1572872 | tf_op jit(solution)/shard_map/ppermute | solution.py:336
  88.8 12.1 %copy-start.25 = (bf16[256,1024]{1,0:T(8,128)(2,1)S(1)}, bf16[256,1024]{1,0:T(8,128)(2,1)}, u32[]{:S(2)}) copy-start(bf16[256,1024]{1,0:T(8,128)(2,1)} %copy-done.24) | copy-start | bytes 1572868
  88.8 30.3 %collective-permute-start.23 = (bf16[512,1024]{1,0:T(8,128)(2,1)S(1)}, bf16[512,1024]{1,0:T(8,128)(2,1)S(1)}, u32[]{:S(2)}, u32[]{:S(2)}) collective-permute-start(bf16[512,1024]{1,0:T(8,128)(2,1)S(1)} %shard_map.112.refs_3_), channel_id=1, source_target_pairs={{0,2},{1,3},{2,0},{3,1},{4,6},{5,7},{6,4},{7,5},{8,10},{9,11},{10,... | collective-permute-start | bytes 3145736 | tf_op jit(solution)/shard_map/ppermute | solution.py:26
  99.3 20.4 %collective-permute-start.26 = (bf16[128,4096]{1,0:T(8,128)(2,1)S(1)}, bf16[128,4096]{1,0:T(8,128)(2,1)S(1)}, u32[]{:S(2)}, u32[]{:S(2)}) collective-permute-start(bf16[128,4096]{1,0:T(8,128)(2,1)S(1)} %shard_map.113.refs_4_), channel_id=1, source_target_pairs={{0,16},{16,0},{1,17},{17,1},{2,18},{18,2},{3,19},{19,3},{4,20},{20... | collective-permute-start | bytes 3145736 | tf_op jit(solution)/shard_map/ppermute | solution.py:26
  100.9 18.8 %collective-permute-start.27 = (bf16[512,1024]{1,0:T(8,128)(2,1)S(1)}, bf16[512,1024]{1,0:T(8,128)(2,1)S(1)}, u32[]{:S(2)}, u32[]{:S(2)}) collective-permute-start(bf16[512,1024]{1,0:T(8,128)(2,1)S(1)} %shard_map.112.refs_3_), channel_id=1, source_target_pairs={{0,1},{1,0},{2,3},{3,2},{4,5},{5,4},{6,7},{7,6},{8,9},{9,8},{10,11... | collective-permute-start | bytes 3145736 | tf_op jit(solution)/shard_map/ppermute | solution.py:26
  112.2 1.3 copy-start.16
  119.7 1.0 copy-start.8
  120.8 6.4 %collective-permute-start.28 = (bf16[512,1024]{1,0:T(8,128)(2,1)S(1)}, bf16[512,1024]{1,0:T(8,128)(2,1)S(1)}, u32[]{:S(2)}, u32[]{:S(2)}) collective-permute-start(bf16[512,1024]{1,0:T(8,128)(2,1)S(1)} %shard_map.116.refs_11_.refs_2_), channel_id=1, source_target_pairs={{0,1},{1,0},{2,3},{3,2},{4,5},{5,4},{6,7},{7,6},{8,9},{9,8},{10,11... | collective-permute-start | bytes 3145736 | tf_op jit(solution)/shard_map/ppermute | solution.py:26
  120.8 23.4 %collective-permute-start.30 = (bf16[1024,256]{1,0:T(8,128)(2,1)S(1)}, bf16[1024,256]{1,0:T(8,128)(2,1)S(1)}, u32[]{:S(2)}, u32[]{:S(2)}) collective-permute-start(bf16[1024,256]{1,0:T(8,128)(2,1)S(1)} %get-tuple-element.82), channel_id=1, source_target_pairs={{0,4},{4,0},{8,12},{12,8},{1,5},{5,1},{9,13},{13,9},{2,6},{6,2},{1... | collective-permute-start | bytes 1572872 | tf_op jit(solution)/shard_map/ppermute | solution.py:26
  121.3 8.2 %copy-start.2 = (f32[1,1024,1024]{2,1,0:T(8,128)S(1)}, f32[1,1024,1024]{2,1,0:T(8,128)}, u32[]{:S(2)}) copy-start(f32[1,1024,1024]{2,1,0:T(8,128)} %param.10) | copy-start | bytes 12582916
  121.3 8.2 %copy-start.4 = (f32[1,1024,1024]{2,1,0:T(8,128)S(1)}, f32[1,1024,1024]{2,1,0:T(8,128)}, u32[]{:S(2)}) copy-start(f32[1,1024,1024]{2,1,0:T(8,128)} %param.11) | copy-start | bytes 12582916
  124.3 5.3 %copy-start = (f32[1,1024,1024]{2,1,0:T(8,128)S(1)}, f32[1,1024,1024]{2,1,0:T(8,128)}, u32[]{:S(2)}) copy-start(f32[1,1024,1024]{2,1,0:T(8,128)} %param.9) | copy-start | bytes 12582916
  124.3 27.8 %collective-permute-start.29 = (bf16[1024,256]{1,0:T(8,128)(2,1)S(1)}, bf16[1024,256]{1,0:T(8,128)(2,1)S(1)}, u32[]{:S(2)}, u32[]{:S(2)}) collective-permute-start(bf16[1024,256]{1,0:T(8,128)(2,1)S(1)} %shard_map.117.refs_7_), channel_id=1, source_target_pairs={{0,8},{4,12},{8,0},{12,4},{1,9},{5,13},{9,1},{13,5},{2,10},{6,14},... | collective-permute-start | bytes 1572872 | tf_op jit(solution)/shard_map/ppermute | solution.py:336
  132.3 19.8 %collective-permute-start.31 = (bf16[1024,256]{1,0:T(8,128)(2,1)S(1)}, bf16[1024,256]{1,0:T(8,128)(2,1)S(1)}, u32[]{:S(2)}, u32[]{:S(2)}) collective-permute-start(bf16[1024,256]{1,0:T(8,128)(2,1)S(1)} %get-tuple-element.72.refs_7_), channel_id=1, source_target_pairs={{0,16},{16,0},{1,17},{17,1},{2,18},{18,2},{3,19},{19,3},{4,20},{20... | collective-permute-start | bytes 1572872 | tf_op jit(solution)/shard_map/ppermute | solution.py:26
  137.9 19.4 %collective-permute-start.32 = (bf16[1024,256]{1,0:T(8,128)(2,1)S(1)}, bf16[1024,256]{1,0:T(8,128)(2,1)S(1)}, u32[]{:S(2)}, u32[]{:S(2)}) collective-permute-start(bf16[1024,256]{1,0:T(8,128)(2,1)S(1)} %get-tuple-element.77.refs_7_), channel_id=1, source_target_pairs={{0,16},{16,0},{1,17},{17,1},{2,18},{18,2},{3,19},{19,3},{4,20},{20... | collective-permute-start | bytes 1572872 | tf_op jit(solution)/shard_map/ppermute | solution.py:26
  138.5 23.2 %collective-permute-start.21 = (bf16[128,2048]{1,0:T(8,128)(2,1)}, bf16[128,2048]{1,0:T(8,128)(2,1)}, u32[]{:S(2)}, u32[]{:S(2)}) collective-permute-start(bf16[128,2048]{1,0:T(8,128)(2,1)} %get-tuple-element.69), channel_id=1, source_target_pairs={{0,2},{1,3},{2,0},{3,1},{4,6},{5,7},{6,4},{7,5},{8,10},{9,11},{10,... | collective-permute-start | bytes 1572872 | tf_op jit(solution)/shard_map/ppermute | solution.py:26
  144.2 19.1 %collective-permute-start.22 = (bf16[128,2048]{1,0:T(8,128)(2,1)}, bf16[128,2048]{1,0:T(8,128)(2,1)}, u32[]{:S(2)}, u32[]{:S(2)}) collective-permute-start(bf16[128,2048]{1,0:T(8,128)(2,1)} %get-tuple-element.70), channel_id=1, source_target_pairs={{0,2},{1,3},{2,0},{3,1},{4,6},{5,7},{6,4},{7,5},{8,10},{9,11},{10,... | collective-permute-start | bytes 1572872 | tf_op jit(solution)/shard_map/ppermute | solution.py:26
  152.1 25.2 %collective-permute-start.34 = (bf16[1024,256]{1,0:T(8,128)(2,1)}, bf16[1024,256]{1,0:T(8,128)(2,1)}, u32[]{:S(2)}, u32[]{:S(2)}) collective-permute-start(bf16[1024,256]{1,0:T(8,128)(2,1)} %shard_map.123.refs_7_), channel_id=1, source_target_pairs={{0,8},{4,12},{8,0},{12,4},{1,9},{5,13},{9,1},{13,5},{2,10},{6,14},... | collective-permute-start | bytes 1572872 | tf_op jit(solution)/shard_map/ppermute | solution.py:336
  152.2 8.0 %copy-start.19 = (bf16[1024,256]{1,0:T(8,128)(2,1)}, bf16[1024,256]{1,0:T(8,128)(2,1)S(1)}, u32[]{:S(2)}) copy-start(bf16[1024,256]{1,0:T(8,128)(2,1)S(1)} %collective-permute-done.31.refs_1_) | copy-start | bytes 1572868
  157.3 2.9 %copy-start.21 = (bf16[1024,256]{1,0:T(8,128)(2,1)}, bf16[1024,256]{1,0:T(8,128)(2,1)S(1)}, u32[]{:S(2)}) copy-start(bf16[1024,256]{1,0:T(8,128)(2,1)S(1)} %collective-permute-done.32.refs_2_) | copy-start | bytes 1572868
  157.4 4.4 %copy-start.9 = (bf16[128,4096]{1,0:T(8,128)(2,1)S(1)}, bf16[128,4096]{1,0:T(8,128)(2,1)}, u32[]{:S(2)}) copy-start(bf16[128,4096]{1,0:T(8,128)(2,1)} %copy-done.8) | copy-start | bytes 3145732
  160.2 18.7 %collective-permute-start.35 = (bf16[1024,256]{1,0:T(8,128)(2,1)}, bf16[1024,256]{1,0:T(8,128)(2,1)}, u32[]{:S(2)}, u32[]{:S(2)}) collective-permute-start(bf16[1024,256]{1,0:T(8,128)(2,1)} %get-tuple-element.83.refs_3_), channel_id=1, source_target_pairs={{0,16},{16,0},{1,17},{17,1},{2,18},{18,2},{3,19},{19,3},{4,20},{20... | collective-permute-start | bytes 1572872 | tf_op jit(solution)/shard_map/ppermute | solution.py:26
  163.3 1.6 copy-start.17
  166.4 3.1 %collective-permute-start.33 = (bf16[3,2048]{1,0:T(4,128)(2,1)S(1)}, bf16[3,2048]{1,0:T(4,128)(2,1)S(1)}, u32[]{:S(2)}, u32[]{:S(2)}) collective-permute-start(bf16[3,2048]{1,0:T(4,128)(2,1)S(1)} %reshape.78), channel_id=1, source_target_pairs={{1,0},{2,1},{3,2},{4,3},{5,4},{6,5},{7,6},{8,7},{9,8},{10,9},{11,1... | collective-permute-start | bytes 36872 | tf_op jit(solution)/shard_map/ppermute | solution.py:452
  173.6 5.3 %copy-start.1 = (f32[1,1024,1024]{2,1,0:T(8,128)S(1)}, f32[1,1024,1024]{2,1,0:T(8,128)}, u32[]{:S(2)}) copy-start(f32[1,1024,1024]{2,1,0:T(8,128)} %param.9) | copy-start | bytes 12582916
  173.6 5.3 %copy-start.3 = (f32[1,1024,1024]{2,1,0:T(8,128)S(1)}, f32[1,1024,1024]{2,1,0:T(8,128)}, u32[]{:S(2)}) copy-start(f32[1,1024,1024]{2,1,0:T(8,128)} %param.10) | copy-start | bytes 12582916
  173.7 5.3 %copy-start.5 = (f32[1,1024,1024]{2,1,0:T(8,128)S(1)}, f32[1,1024,1024]{2,1,0:T(8,128)}, u32[]{:S(2)}) copy-start(f32[1,1024,1024]{2,1,0:T(8,128)} %param.11) | copy-start | bytes 12582916
  177.3 1.6 copy-start.18
  178.9 17.8 %copy-start.20 = (bf16[1024,256]{1,0:T(8,128)(2,1)S(1)}, bf16[1024,256]{1,0:T(8,128)(2,1)}, u32[]{:S(2)}) copy-start(bf16[1024,256]{1,0:T(8,128)(2,1)} %copy-done.19) | copy-start | bytes 1572868
  179.0 17.8 %copy-start.22 = (bf16[1024,256]{1,0:T(8,128)(2,1)S(1)}, bf16[1024,256]{1,0:T(8,128)(2,1)}, u32[]{:S(2)}) copy-start(bf16[1024,256]{1,0:T(8,128)(2,1)} %copy-done.21) | copy-start | bytes 1572868
  183.1 13.6 %collective-permute-start.36 = (bf16[1024,256]{1,0:T(8,128)(2,1)S(1)}, bf16[1024,256]{1,0:T(8,128)(2,1)S(1)}, u32[]{:S(2)}, u32[]{:S(2)}) collective-permute-start(bf16[1024,256]{1,0:T(8,128)(2,1)S(1)} %get-tuple-element.91), channel_id=1, source_target_pairs={{0,16},{16,0},{1,17},{17,1},{2,18},{18,2},{3,19},{19,3},{4,20},{20... | collective-permute-start | bytes 1572872 | tf_op jit(solution)/shard_map/ppermute | solution.py:26
  (1 other events, 0.8 us)
